TPU v7x, 32 devices: a whole 2x2x4 slice. The times are simulated.
32 devices in a mesh: tm: 4 (over y, core), space: 8 (over z, x).
Axes of the slice: x: 2, y: 2, z: 4, core: 2. Of those that a mesh axis runs over, the one named last changes fastest.
Arguments:
- queries: bfloat16 [4, 8, 384, 1536], P('tm', 'space'), may hold values from -7 to 7
- keys: bfloat16 [4, 8, 384, 1536], P('tm', 'space'), may hold values from -7 to 7
- values: bfloat16 [4, 8, 384, 1536], P('tm', 'space'), may hold values from -2 to 2
- outputs: bfloat16 [4, 8, 384, 1536], P('tm', 'space'), may hold values from -2 to 2
- out_grads: bfloat16 [4, 8, 384, 1536], P('tm', 'space'), may hold values from -6 to 6
- log_sums: float32 [4, 8, 12, 384], P('tm', 'space'), may hold values from 8 to 9.5
- window_mask: int32 [4, 8, 9], P('tm', 'space'), may hold values 0 or 1
Outputs:
- query_grads: bfloat16 [4, 8, 384, 1536], P('tm', 'space')
- key_grads: bfloat16 [4, 8, 384, 1536], P('tm', 'space')
- value_grads: bfloat16 [4, 8, 384, 1536], P('tm', 'space')
All inputs are finite; a program needn't handle non-finite values. No bound on the sum of `window_mask` on one device may be relied on, other than what follows from the above.
Results may differ from a plain program's by a relative error of at most 0.0065.
Values may be sent and summed in bfloat16 or wider, within the bound.
No kernel may reach another device: no remote copies, remote signals or barrier semaphores. Data moves between devices by JAX's collectives and lax.ppermute only.
A program may use at most 192 MiB of HBM per device.

v0:
```python
import functools
import math

import jax
import jax.numpy as jnp
from jax import lax
from jax.experimental import pallas as pl
from jax.experimental.pallas import tpu as pltpu
from jax.sharding import PartitionSpec as P

F32 = jnp.float32
BF16 = jnp.bfloat16
FAR_AWAY = 1e30

OUTER, OWN, PARTNER = (0, 1, 2)
HERE, NEAR, FAR = (0, 1, 2)
CHUNKS = (4, 5, 3)
STAGES = (
    ((HERE, (OWN,)), (NEAR, (OWN,))),
    ((HERE, (PARTNER,)), (NEAR, (PARTNER,))),
    ((HERE, (OUTER,)), (NEAR, (OUTER,)), (FAR, (OWN, PARTNER, OUTER))),
)
LATER_STAGES = (
    STAGES[0],
    STAGES[1] + ((FAR, (PARTNER,)),),
    ((HERE, (OUTER,)), (NEAR, (OUTER,)), (FAR, (OWN, OUTER))),
)
ORDER = (('stage', 0, 0), ('stage', 1, 0), ('hand', 0), ('stage', 0, 1), ('stage', 2, 0), ('hand', 1), ('stage', 0, 2), ('hand', 2), ('stage', 1, 1), ('back', 0), ('stage', 1, 2), ('stage', 2, 1), ('back', 1), ('stage', 2, 2, (0, 'q2'), (0, 'kv1')), ('finish', 0), ('finish', 1), ('finish', 2))
JOINED = ('kv2',)
WEIGHTS = ((60, 60, 60), (60, 30, 60), (240, 120, 60))
EXTRA = 32
VMEM_LIMIT = 20 * 1024 * 1024
GROUP = 1
BLOCK = 256


def dot(a, b, dims):
    return lax.dot_general(a, b, (dims, ((), ())), preferred_element_type=F32)


def three_terms(row):
    terms = []
    for _ in range(3):
        term = row.astype(BF16).astype(F32)
        terms.append(term)
        row = row - term
    return terms


def fold(row):
    lanes = 128
    return [row[:, i : i + lanes] for i in range(0, row.shape[1], lanes)]


def flag_row(frames, rows, frame, row, mask_ref, lanes):
    toward = 1 - 2 * lax.rem(row, 2)
    near = 1 - 2 * lax.rem(frame, 2)
    lane = lax.broadcasted_iota(jnp.int32, (1, lanes), 1)
    flags = jnp.zeros((1, lanes), F32)
    for role in (OUTER, OWN, PARTNER):
        for slot in (HERE, NEAR, FAR):
            row_off = (role - 1) * toward
            frame_off = (0, near, -near)[slot]
            inside = (
                (row + row_off >= 0)
                & (row + row_off < rows)
                & (frame + frame_off >= 0)
                & (frame + frame_off < frames)
            )
            index = 3 * (frame_off + 1) + row_off + 1
            on = inside & ((mask_ref[index] > 0) | (index == 4))
            flags = jnp.where(lane == 3 * role + slot, on.astype(F32), flags)
    return flags


def prep_kernel(
    counts, frames, rows, frame_ref, row_ref, mask_ref, q_ref, g_ref, o_ref, lse_ref, *outs
):
    tile = q_ref.shape[0]
    width = q_ref.shape[1] // sum(counts)
    flags = flag_row(frames, rows, frame_ref[0], row_ref[0], mask_ref, width)
    ones = jnp.ones((8, width), BF16)
    head = 0
    for out, count in zip(outs, counts):
        for h in range(count):
            source = slice(head * width, (head + 1) * width)
            cols = slice(h * width, (h + 1) * width)
            grad = g_ref[:, source]
            out[0:tile, cols] = q_ref[:, source]
            out[tile : 2 * tile, cols] = grad
            prod = grad.astype(F32) * o_ref[:, source].astype(F32)
            high = prod.astype(BF16)
            low = (prod - high.astype(F32)).astype(BF16)
            delta = dot(ones, high, ((1,), (1,))) + dot(ones, low, ((1,), (1,)))
            lines = []
            for line in (lse_ref[head], delta[0:1, :]):
                for term in three_terms(line):
                    lines += fold(term)
            lines.append(flags)
            lines.append(jnp.zeros((EXTRA - len(lines), width), F32))
            extra = jnp.concatenate(lines, axis=0).astype(BF16)
            out[2 * tile : 2 * tile + EXTRA, cols] = extra
            head += 1


def prep(first, counts, head_width, sizes, place, mask, q, g, o, lse):
    tile, full = q.shape
    count = sum(counts)
    offset = first * head_width
    cols = pl.BlockSpec(
        (pl.Element(tile), pl.Element(count * head_width)), lambda i, *_: (0, offset)
    )
    shapes = [(2 * tile + EXTRA, n * head_width) for n in counts]
    return pl.pallas_call(
        functools.partial(prep_kernel, counts, *sizes),
        grid_spec=pltpu.PrefetchScalarGridSpec(
            num_scalar_prefetch=3,
            grid=(1,),
            in_specs=[
                cols,
                cols,
                cols,
                pl.BlockSpec(
                    (pl.Element(count), pl.Element(1), pl.Element(tile)),
                    lambda i, *_: (first, 0, 0),
                ),
            ],
            out_specs=[pl.BlockSpec(shape, lambda i, *_: (0, 0)) for shape in shapes],
        ),
        out_shape=[jax.ShapeDtypeStruct(shape, BF16) for shape in shapes],
        compiler_params=pltpu.CompilerParams(vmem_limit_bytes=VMEM_LIMIT),
        cost_estimate=pl.CostEstimate(
            flops=2 * tile * count * head_width,
            bytes_accessed=10 * tile * count * head_width,
            transcendentals=0,
        ),
        name="prep",
    )(*place, mask, *(pltpu.with_memory_space_constraint(a, pltpu.HBM) for a in (q, g, o)), lse)


def pack_kernel(k_ref, v_ref, out):
    out[0] = k_ref[...]
    out[1] = v_ref[...]


def pack(k, v, steps=2):
    tile, full = k.shape
    cols = pl.BlockSpec((tile, full // steps), lambda i: (0, i))
    return pl.pallas_call(
        pack_kernel,
        grid=(steps,),
        in_specs=[cols, cols],
        out_specs=pl.BlockSpec((2, tile, full // steps), lambda i: (0, 0, i)),
        out_shape=jax.ShapeDtypeStruct((2, tile, full), k.dtype),
        compiler_params=pltpu.CompilerParams(vmem_limit_bytes=VMEM_LIMIT),
        cost_estimate=pl.CostEstimate(flops=0, bytes_accessed=8 * k.size, transcendentals=0),
        name="pack",
    )(*(pltpu.with_memory_space_constraint(a, pltpu.HBM) for a in (k, v)))


def row_stats(message, tile):
    extra = message[2 * tile : 2 * tile + EXTRA, :].astype(F32)
    parts = tile // 128
    rows = []
    for base in (0, 3 * parts):
        pieces = []
        for p in range(parts):
            a, b, c = (extra[base + i * parts + p : base + i * parts + p + 1] for i in range(3))
            pieces.append(a + b + c)
        rows.append(jnp.concatenate(pieces, axis=1))
    return (rows[0], rows[1], extra[6 * parts : 6 * parts + 1])


def stage_kernel(work, names, carried, last, factor, group, far_ref, *refs):
    env = dict(zip(names, refs))
    tile, wide = env["message%d" % work[0][1][0]].shape
    tile = (tile - EXTRA) // 2
    width = wide // group
    heads = [slice(i * width, (i + 1) * width) for i in range(group)]
    used = sorted({j for _, js in work for j in js})
    stats = {
        (j, i): row_stats(env["message%d" % j].at[:, cols], tile)
        for j in used
        for i, cols in enumerate(heads)
    }
    started = set()

    def add_q(j, i, rows, term):
        name, cols = ("q%d" % j, heads[i])
        if (j, i, rows.start) in started:
            env["sum_" + name][rows, cols] += term
        elif "acc_" + name in env:
            env["sum_" + name][rows, cols] = env["acc_" + name][rows, cols] + term
        else:
            env["sum_" + name][rows, cols] = term
        started.add((j, i, rows.start))

    def pair_terms(slot, j, i):
        cols = heads[i]
        message, keys = (env["message%d" % j], env["keys%d" % slot])
        key, value = (keys[0, :, cols], keys[1, :, cols])
        shift, delta, flags = stats[j, i]
        lane = 3 * j + slot
        shift = jnp.where(flags[:, lane : lane + 1] > 0, shift, FAR_AWAY)
        term_k, term_v = (None, None)
        for low in range(0, tile, BLOCK):
            rows = slice(low, min(low + BLOCK, tile))
            queries = message[rows, cols]
            grads = message[tile + rows.start : tile + rows.stop, cols]
            scores = dot(key, queries, ((1,), (1,)))
            weights = jnp.exp(scores * factor - shift[:, rows])
            grad_prob = dot(value, grads, ((1,), (1,)))
            grad_score = (weights * (grad_prob - delta[:, rows])).astype(BF16)
            more_v = dot(weights.astype(BF16), grads, ((1,), (0,)))
            more_k = dot(grad_score, queries, ((1,), (0,)))
            add_q(j, i, rows, dot(grad_score, key, ((0,), (0,))))
            term_k = more_k if term_k is None else term_k + more_k
            term_v = more_v if term_v is None else term_v + more_v
        return (term_k, term_v)

    def key_frames(slots_js):
        for slot, js in slots_js:
            name = "kv%d" % slot
            out = env["out_" + name]
            for i, cols in enumerate(heads):
                dk, dv = pair_terms(slot, js[0], i)
                for j in js[1:]:
                    more_k, more_v = pair_terms(slot, j, i)
                    dk, dv = (dk + more_k, dv + more_v)
                if "acc_" + name in env:
                    acc = env["acc_" + name]
                    dk, dv = (dk + acc[0, :, cols], dv + acc[1, :, cols])
                out[0, :, cols] = (dk * factor if name in last else dk).astype(out.dtype)
                out[1, :, cols] = dv.astype(out.dtype)

    key_frames([(slot, js) for slot, js in work if slot != FAR])
    for slot, js in work:
        if slot == FAR:
            fresh = [j for j in js if (j, 0, 0) not in started]
            pl.when(far_ref[0] > 0)(functools.partial(key_frames, [(slot, js)]))

            @pl.when(far_ref[0] == 0)
            def _():
                out = env["out_kv%d" % FAR]
                out[...] = jnp.zeros_like(out)
                for j in fresh:
                    name = "q%d" % j
                    env["sum_" + name][...] = env["acc_" + name][...]

    for j in used:
        out = env["out_q%d" % j]
        out[...] = (env["sum_q%d" % j][...]).astype(out.dtype)


def run_stage(work, weight, last, joined, first, count, head_width, far, keys, messages, sums):
    rows, wide = next(iter(messages.values())).shape
    tile = (rows - EXTRA) // 2
    group = math.gcd(count, GROUP) if first % math.gcd(count, GROUP) == 0 else 1
    step, begin = (group * head_width, first // group)
    one = pl.BlockSpec((tile, step), lambda h, *_: (0, h))
    two = pl.BlockSpec((2, tile, step), lambda h, *_: (0, 0, h))
    cols = pl.BlockSpec((2, tile, step), lambda h, *_: (0, 0, h + begin))
    whole = pl.BlockSpec((rows, step), lambda h, *_: (0, h))
    used = sorted({j for _, js in work for j in js})
    slots = [slot for slot, _ in work]
    names, args, specs = ([], [], [])

    def give(name, arg, spec):
        names.append(name)
        args.append(arg)
        specs.append(spec)

    for j in used:
        give("message%d" % j, messages[j], whole)
    for slot in slots:
        give("keys%d" % slot, keys[slot], cols)
    touched = [("q%d" % j, one) for j in used] + [("kv%d" % s, two) for s in slots]
    carried = [name for name, _ in touched if name in sums]
    for name, spec in touched:
        if name in sums:
            give("acc_" + name, sums[name], spec)
    out_specs, out_shapes, aliases = ([], [], {})
    for name, spec in touched:
        shape = (tile, wide) if name.startswith("q") else (2, tile, wide)
        if name in last and name in joined:
            total, begun = joined[name]
            spec = cols
            shape = (2, tile, total)
            if begun is not None:
                aliases[1 + len(args)] = len(out_specs)
                give("begun_" + name, begun, pl.BlockSpec(memory_space=pl.ANY))
        out_specs.append(spec)
        out_shapes.append(jax.ShapeDtypeStruct(shape, BF16 if name in last else F32))
    names += ["out_" + name for name, _ in touched]
    names += ["sum_q%d" % j for j in used]
    pairs = count * sum(len(js) for _, js in work)
    results = pl.pallas_call(
        functools.partial(stage_kernel, work, names, carried, last, head_width**-0.5, group),
        grid_spec=pltpu.PrefetchScalarGridSpec(
            num_scalar_prefetch=1,
            grid=(count // group,),
            in_specs=specs,
            out_specs=out_specs,
            scratch_shapes=[pltpu.VMEM((tile, step), F32)] * len(used),
        ),
        out_shape=out_shapes,
        input_output_aliases=aliases,
        compiler_params=pltpu.CompilerParams(vmem_limit_bytes=VMEM_LIMIT),
        cost_estimate=pl.CostEstimate(
            flops=weight * pairs * tile * tile * head_width,
            bytes_accessed=20 * tile * wide,
            transcendentals=0,
        ),
        name="pairs",
    )(far, *args)
    return {**sums, **{name: value for (name, _), value in zip(touched, results)}}


def finish_kernel(factor, backs, own_kv, near, far, own_q, *rest):
    out_q, out_k, out_v = rest[-3:]
    total = own_q[...]
    for back in rest[:backs]:
        total = total + back[...].astype(F32)
    out_q[...] = (total * factor).astype(BF16)
    for i, (out, scale) in enumerate(((out_k, factor), (out_v, 1.0))):
        others = near[i].astype(F32) + far[i].astype(F32)
        out[...] = (own_kv[i] * scale + others).astype(BF16)


def finish(first, count, head_width, full, parts, so_far):
    tile = parts[0].shape[1]
    wide = count * head_width
    one = pl.BlockSpec((tile, wide), lambda i: (0, 0))
    two = pl.BlockSpec((2, tile, wide), lambda i: (0, 0, 0))

    def part(array):
        offset = first * head_width if array.shape[2] > wide else 0
        return pl.BlockSpec(
            (pl.Element(2), pl.Element(tile), pl.Element(wide)), lambda i: (0, 0, offset)
        )

    cols = pl.BlockSpec(
        (pl.Element(tile), pl.Element(wide)), lambda i: (0, first * head_width)
    )
    kept = [] if so_far is None else list(so_far)
    return pl.pallas_call(
        functools.partial(finish_kernel, head_width**-0.5, len(parts) - 4),
        grid=(1,),
        in_specs=[two, part(parts[1]), part(parts[2])] + [one] * (len(parts) - 3) + [pl.BlockSpec(memory_space=pl.ANY)] * len(kept),
        out_specs=[cols] * 3,
        out_shape=[jax.ShapeDtypeStruct((tile, full), BF16)] * 3,
        input_output_aliases={len(parts) + i: i for i in range(len(kept))},
        compiler_params=pltpu.CompilerParams(vmem_limit_bytes=VMEM_LIMIT),
        cost_estimate=pl.CostEstimate(
            flops=8 * tile * count * head_width,
            bytes_accessed=30 * tile * count * head_width,
            transcendentals=0,
        ),
        name="finish",
    )(*parts, *kept)


def after(value, *earlier):
    return lax.optimization_barrier((value, *earlier))[0]


def per_device(queries, keys, values, outputs, out_grads, log_sums, window_mask):
    tile, full = queries.shape[2:]
    heads = log_sums.shape[2]
    width = full // heads
    frames, rows = (lax.axis_size("tm"), lax.axis_size("space"))
    q, k, v, o, g = (a.reshape(tile, full) for a in (queries, keys, values, outputs, out_grads))
    partner = [(i, i ^ 1) for i in range(rows)]
    onward = [(i, (i + 2) % rows) for i in range(0, rows, 2)]
    onward += [(i, (i - 2) % rows) for i in range(1, rows, 2)]
    homeward = [(i + 2, i) for i in range(0, rows - 2, 2)]
    homeward += [(i, i + 2) for i in range(1, rows - 2, 2)]
    homeward += [(0, 1), (rows - 1, rows - 2)]
    owners = [(0, 0), (rows - 1, rows - 1)]
    for i in range(1, rows - 1, 2):
        owners += [(i, i + 1), (i + 1, i)]
    near_pairs = [(i, i ^ 1) for i in range(frames)]
    far_pairs = [(0, 0), (frames - 1, frames - 1)]
    for i in range(1, frames - 1, 2):
        far_pairs += [(i, i + 1), (i + 1, i)]

    frame, row = (lax.axis_index("tm"), lax.axis_index("space"))
    far_frame = frame - 1 + 2 * lax.rem(frame, 2)
    has_far = ((far_frame >= 0) & (far_frame < frames)).astype(jnp.int32).reshape(1)
    place = (frame.reshape(1), row.reshape(1))

    firsts = [sum(CHUNKS[:c]) for c in range(len(CHUNKS))]
    lse = log_sums.reshape(heads, 1, tile)
    mask = window_mask.reshape(9)
    own_kv = pack(k, v)
    near_kv = lax.ppermute(own_kv, "tm", near_pairs)
    far_kv = lax.ppermute(own_kv, "tm", far_pairs)
    make = lambda first, counts, source: prep(
        first, counts, width, (frames, rows), place, mask, source, g, o, lse
    )
    mine = make(0, CHUNKS[:1], q)
    theirs = {0: lax.ppermute(mine[0], "space", partner)}
    mine += make(firsts[1], CHUNKS[1:], after(q, mine[0]))
    frames_kv = {HERE: own_kv, NEAR: near_kv, FAR: far_kv}
    last = len(CHUNKS) - 1
    outers = {}
    sums = [{} for _ in CHUNKS]
    backs = [{} for _ in CHUNKS]
    done = []
    out = None

    def stage(c, step, *awaited):
        messages = {OUTER: outers.get(c), OWN: mine[c], PARTNER: theirs.get(c)}
        stages = LATER_STAGES if c == last else STAGES
        work = stages[step]
        needed = {j: messages[j] for _, js in work for j in js}
        first_used = min(needed)
        arrived = [backs[i][name] for i, name in awaited]
        needed[first_used] = after(needed[first_used], *done[-1:], *arrived)
        later = {j for other in stages[step + 1 :] for _, js in other for j in js}
        slots = {slot for other in stages[step + 1 :] for slot, _ in other}
        straight = (OUTER, PARTNER) if c == last else (OUTER,)
        final = {"q%d" % j for j in straight if j not in later}
        final |= {"kv%d" % slot for slot in (NEAR, FAR) if slot not in slots}
        joined = {}
        if c < last and step + 1 == len(stages):
            for name in JOINED:
                joined[name] = (firsts[last] * width, sums[c - 1][name] if c else None)
        sums[c] = run_stage(
            work, WEIGHTS[c][step], final, joined, firsts[c], CHUNKS[c], width, has_far, frames_kv, needed, sums[c]
        )
        done.append(sums[c]["kv0"])
        for name, axis, pairs in (
            ("q0", "space", owners if c == last else homeward),
            ("q2", "space", partner),
            ("kv1", "tm", near_pairs),
            ("kv2", "tm", far_pairs),
        ):
            if name not in final or name not in sums[c] or name in backs[c]:
                continue
            if name in joined and c + 1 < last:
                continue
            backs[c][name] = lax.ppermute(sums[c][name], axis, pairs)
            if name in joined:
                for earlier in range(c):
                    backs[earlier][name] = backs[c][name]

    def hand_on(c):
        outers[c] = lax.ppermute(after(theirs[c], *done[-1:]), "space", onward)

    def send_back(c):
        total = sums[c]["q2"] + after(backs[c]["q0"], *done[-1:]).astype(F32)
        backs[c]["q2"] = lax.ppermute(total.astype(BF16), "space", partner)

    def complete(c, so_far):
        back = backs[c]
        own = after(sums[c]["q1"], *done[-1:])
        from_others = [back["q2"]] + ([back["q0"]] if c == last else [])
        so_far = finish(
            firsts[c], CHUNKS[c], width, full,
            (sums[c]["kv0"], back["kv1"], back["kv2"], own, *from_others), so_far,
        )
        done.append(so_far[0])
        return so_far

    for c in range(1, len(CHUNKS)):
        theirs[c] = lax.ppermute(mine[c], "space", partner)
    for kind, c, *rest in ORDER:
        if kind == "stage":
            stage(c, *rest)
        elif kind == "hand":
            hand_on(c)
        elif kind == "back":
            send_back(c)
        else:
            out = complete(c, out)
    return tuple(a.reshape(queries.shape) for a in out)


def solution(mesh):
    tile = P("tm", "space", None, None)
    return jax.shard_map(
        per_device,
        mesh=mesh,
        in_specs=(tile,) * 6 + (P("tm", "space", None),),
        out_specs=(tile,) * 3,
        check_vma=False,
    )
```

profile of v0, /device:TPU:9, one launch (start us, length us, event | category | flops | bytes accessed | tf_op | source)
XLA Modules:
  0.0 147.6 jit_solution(7718402292017204489)
XLA Ops:
  0.7 1.8 %pack.1.refs_1_.refs_3_.refs_2_ = bf16[2,384,1536]{2,1,0:T(8,128)(2,1)S(1)} custom-call(bf16[384,1536]{1,0:T(8,128)(2,1)} %bitcast.26, bf16[384,1536]{1,0:T(8,128)(2,1)} %bitcast.27), custom_call_target="tpu_custom_call" | custom-call | bytes 4718592 | tf_op jit(solution)/shard_map/pack/pallas_call | solution.py:149
  2.4 0.7 collective-permute-start.2
  3.2 3.0 %collective-permute-start.4 = (bf16[2,384,1536]{2,1,0:T(8,128)(2,1)S(1)}, bf16[2,384,1536]{2,1,0:T(8,128)(2,1)}, u32[]{:S(2)}, u32[]{:S(2)}) collective-permute-start(bf16[2,384,1536]{2,1,0:T(8,128)(2,1)S(1)} %pack.1.refs_1_.refs_3_.refs_2_), channel_id=1, source_target_pairs={{0,0},{24,24},{8,16},{16,8},{1,1},{25,25},{9,17},{17,9},{2,2},{26,... | collective-permute-start | bytes 7077896 | tf_op jit(solution)/shard_map/ppermute | solution.py:397
  6.3 2.2 %prep.2.refs_0_.refs_1_ = bf16[800,512]{1,0:T(8,128)(2,1)S(1)} custom-call(s32[1]{0:T(128)} %bitcast.1.frame_ref, s32[1]{0:T(128)} %bitcast.2.row_ref, s32[9]{0:T(128)S(1)} %bitcast.15, bf16[384,1536]{1,0:T(8,128)(2,1)} %bitcast.20, bf16[384,1536]{1,0:T(8,128)(2,1)} %bitcast.22, bf16[384,1536]{1,0:T(8,128)(2,1)} %bitcast.24, f32[12,1,384]{2,1,0:T(1,128)S(1)} %bitcast.13), custom_call_target="tpu_custom_call" | custom-call | flops 393216 | bytes 1966080 | tf_op jit(solution)/shard_map/prep/pallas_call | solution.py:114
  8.5 1.3 collective-permute-start.1
  9.8 4.0 %prep.3 = (bf16[800,640]{1,0:T(8,128)(2,1)}, bf16[800,384]{1,0:T(8,128)(2,1)}) custom-call(s32[1]{0:T(128)} %bitcast.1.frame_ref, s32[1]{0:T(128)} %bitcast.2.row_ref, s32[9]{0:T(128)S(1)} %bitcast.16, bf16[384,1536]{1,0:T(8,128)(2,1)} %bitcast.21, bf16[384,1536]{1,0:T(8,128)(2,1)} %bitcast.23, bf16[384,1536]{1,0:T(8,128)(2,1)} %bitcast.25, ...), custom_call_target="tpu_custom_call" | custom-call | flops 786432 | bytes 3932160 | tf_op jit(solution)/shard_map/prep/pallas_call | solution.py:114
  13.8 0.3 collective-permute-start.6
  14.0 1.2 collective-permute-start
  15.3 7.4 %pairs.9 = (f32[384,512]{1,0:T(8,128)S(1)}, f32[2,384,512]{2,1,0:T(8,128)S(1)}, f32[2,384,512]{2,1,0:T(8,128)S(1)}) custom-call(s32[1]{0:T(128)} %bitcast.far_ref, bf16[800,512]{1,0:T(8,128)(2,1)S(1)} %prep.2.refs_0_.refs_1_, bf16[2,384,1536]{2,1,0:T(8,128)(2,1)S(1)} %pack.1.refs_1_.refs_3_.refs_2_, ...), custom_call_target="tpu_custom_call" | custom-call | flops 9059696640 | bytes 3932160 | tf_op jit(solution)/shard_map/pairs/pallas_call | solution.py:297
  22.7 8.7 %pairs.10 = (f32[384,640]{1,0:T(8,128)S(1)}, f32[2,384,640]{2,1,0:T(8,128)S(1)}, f32[2,384,640]{2,1,0:T(8,128)S(1)}) custom-call(s32[1]{0:T(128)} %bitcast.far_ref, bf16[800,640]{1,0:T(8,128)(2,1)} %get-tuple-element.70.refs_0_.refs_1_, bf16[2,384,1536]{2,1,0:T(8,128)(2,1)S(1)} %pack.1.refs_1_.refs_3_.refs_2_, ...), custom_call_target="tpu_custom_call" | custom-call | flops 11324620800 | bytes 4915200 | tf_op jit(solution)/shard_map/pairs/pallas_call | solution.py:297
  31.4 0.0 collective-permute-done.1.refs_0_.refs_2_
  31.4 1.4 collective-permute-start.3
  32.8 7.6 %pairs.11 = (f32[384,512]{1,0:T(8,128)S(1)}, f32[2,384,512]{2,1,0:T(8,128)S(1)}, f32[2,384,512]{2,1,0:T(8,128)S(1)}) custom-call(s32[1]{0:T(128)} %bitcast.far_ref, bf16[800,512]{1,0:T(8,128)(2,1)} %collective-permute-done.1.refs_0_.refs_2_, bf16[2,384,1536]{2,1,0:T(8,128)(2,1)S(1)} %pack.1.refs_1_.refs_3_.refs_2_, ...), custom_call_target="tpu_custom_call" | custom-call | flops 9059696640 | bytes 3932160 | tf_op jit(solution)/shard_map/pairs/pallas_call | solution.py:297
  40.4 5.6 %pairs.12 = (f32[384,384]{1,0:T(8,128)S(1)}, f32[2,384,384]{2,1,0:T(8,128)S(1)}, f32[2,384,384]{2,1,0:T(8,128)S(1)}) custom-call(s32[1]{0:T(128)} %bitcast.far_ref, bf16[800,384]{1,0:T(8,128)(2,1)} %get-tuple-element.75.refs_0_.refs_1_, bf16[2,384,1536]{2,1,0:T(8,128)(2,1)S(1)} %pack.1.refs_1_.refs_3_.refs_2_, ...), custom_call_target="tpu_custom_call" | custom-call | flops 27179089920 | bytes 2949120 | tf_op jit(solution)/shard_map/pairs/pallas_call | solution.py:297
  46.0 4.8 %collective-permute-done.6.refs_0_.refs_2_ = bf16[800,640]{1,0:T(8,128)(2,1)} collective-permute-done((bf16[800,640]{1,0:T(8,128)(2,1)}, bf16[800,640]{1,0:T(8,128)(2,1)}, u32[]{:S(2)}, u32[]{:S(2)}) %collective-permute-start.6) | collective-permute-done | bytes 1024032 | tf_op jit(solution)/shard_map/ppermute | solution.py:467
  50.8 1.3 collective-permute-start.7
  52.1 0.0 collective-permute-done.3.refs_0_
  52.1 17.7 %pairs.13 = (bf16[384,512]{1,0:T(8,128)(2,1)S(1)}, f32[384,512]{1,0:T(8,128)S(1)}, f32[384,512]{1,0:T(8,128)S(1)}, f32[2,384,512]{2,1,0:T(8,128)S(1)}, bf16[2,38...) custom-call(s32[1]{0:T(128)} %bitcast.far_ref, bf16[800,512]{1,0:T(8,128)(2,1)S(1)} %collective-permute-done.3.refs_0_, ...), custom_call_target="tpu_custom_call" | custom-call | flops 22649241600 | bytes 3932160 | tf_op jit(solution)/shard_map/pairs/pallas_call | solution.py:297
  69.8 1.6 %collective-permute-start.8 = (bf16[384,512]{1,0:T(8,128)(2,1)S(1)}, bf16[384,512]{1,0:T(8,128)(2,1)S(1)}, u32[]{:S(2)}, u32[]{:S(2)}) collective-permute-start(bf16[384,512]{1,0:T(8,128)(2,1)S(1)} %get-tuple-element.97), channel_id=1, source_target_pairs={{2,0},{4,2},{6,4},{1,3},{3,5},{5,7},{0,1},{7,6},{10,8},{12,10},{14... | collective-permute-start | bytes 1179656 | tf_op jit(solution)/shard_map/ppermute | solution.py:443
  71.5 0.0 collective-permute-start.10
  71.5 0.1 collective-permute-start.5
  71.5 8.9 %pairs.14 = (f32[384,640]{1,0:T(8,128)S(1)}, f32[2,384,640]{2,1,0:T(8,128)S(1)}, f32[2,384,640]{2,1,0:T(8,128)S(1)}) custom-call(s32[1]{0:T(128)} %bitcast.far_ref, bf16[800,640]{1,0:T(8,128)(2,1)} %collective-permute-done.6.refs_0_.refs_2_, bf16[2,384,1536]{2,1,0:T(8,128)(2,1)S(1)} %pack.1.refs_1_.refs_3_.refs_2_, ...), custom_call_target="tpu_custom_call" | custom-call | flops 5662310400 | bytes 4915200 | tf_op jit(solution)/shard_map/pairs/pallas_call | solution.py:297
  80.5 0.0 collective-permute-done.7.refs_0_
  80.5 21.5 %pairs.15 = (bf16[384,640]{1,0:T(8,128)(2,1)S(1)}, f32[384,640]{1,0:T(8,128)S(1)}, f32[384,640]{1,0:T(8,128)S(1)}, f32[2,384,640]{2,1,0:T(8,128)S(1)}, bf16[2,38...) custom-call(s32[1]{0:T(128)} %bitcast.far_ref, ...), custom_call_target="tpu_custom_call", output_to_operand_aliasing={{5}: (11, {})} | custom-call | flops 28311552000 | bytes 4915200 | tf_op jit(solution)/shard_map/pairs/pallas_call | solution.py:297
  102.0 1.8 %collective-permute-start.15 = (bf16[384,640]{1,0:T(8,128)(2,1)S(1)}, bf16[384,640]{1,0:T(8,128)(2,1)S(1)}, u32[]{:S(2)}, u32[]{:S(2)}) collective-permute-start(bf16[384,640]{1,0:T(8,128)(2,1)S(1)} %get-tuple-element.116), channel_id=1, source_target_pairs={{2,0},{4,2},{6,4},{1,3},{3,5},{5,7},{0,1},{7,6},{10,8},{12,10},{14... | collective-permute-start | bytes 1474568 | tf_op jit(solution)/shard_map/ppermute | solution.py:443
  103.9 4.2 %collective-permute-start.14 = (bf16[2,384,1152]{2,1,0:T(8,128)(2,1)S(1)}, bf16[2,384,1152]{2,1,0:T(8,128)(2,1)S(1)}, u32[]{:S(2)}, u32[]{:S(2)}) collective-permute-start(bf16[2,384,1152]{2,1,0:T(8,128)(2,1)S(1)} %get-tuple-element.109), channel_id=1, source_target_pairs={{0,0},{24,24},{8,16},{16,8},{1,1},{25,25},{9,17},{17,9},{2,2},{26,... | collective-permute-start | bytes 5308424 | tf_op jit(solution)/shard_map/ppermute | solution.py:443
  108.1 0.1 add_convert_fusion.1
  108.3 0.1 collective-permute-start.9
  108.4 8.6 %pairs.16 = (bf16[384,384]{1,0:T(8,128)(2,1)S(1)}, f32[2,384,384]{2,1,0:T(8,128)S(1)}, f32[2,384,384]{2,1,0:T(8,128)S(1)}, f32[2,384,384]{2,1,0:T(8,128)S(1)}) custom-call(s32[1]{0:T(128)} %bitcast.far_ref, bf16[800,384]{1,0:T(8,128)(2,1)} %collective-permute-done.refs_0_, bf16[2,384,1536]{2,1,0:T(8,128)(2,1)S(1)} %pack.1.refs_1_.refs_3_.refs_2_, ...), custom_call_target="tpu_custom_call" | custom-call | flops 20384317440 | bytes 2949120 | tf_op jit(solution)/shard_map/pairs/pallas_call | solution.py:297
  117.0 0.0 collective-permute-done.15
  117.0 0.1 collective-permute-start.13
  117.1 0.1 add_convert_fusion
  117.2 0.0 collective-permute-done.5.refs_0_
  117.2 1.5 %collective-permute-start.16 = (bf16[384,640]{1,0:T(8,128)(2,1)S(1)}, bf16[384,640]{1,0:T(8,128)(2,1)S(1)}, u32[]{:S(2)}, u32[]{:S(2)}) collective-permute-start(bf16[384,640]{1,0:T(8,128)(2,1)S(1)} %add_convert_fusion), channel_id=1, source_target_pairs={{0,1},{1,0},{2,3},{3,2},{4,5},{5,4},{6,7},{7,6},{8,9},{9,8},{10,11... | collective-permute-start | bytes 1474568 | tf_op jit(solution)/shard_map/ppermute | solution.py:453
  118.7 10.9 %pairs.17 = (bf16[384,384]{1,0:T(8,128)(2,1)S(1)}, f32[384,384]{1,0:T(8,128)S(1)}, f32[2,384,384]{2,1,0:T(8,128)S(1)}, bf16[2,384,384]{2,1,0:T(8,128)(2,1)S(1)}, bf16[2,384,384]{2,1,0:T(8,128)(2,1)S(1)}) custom-call(s32[1]{0:T(128)} %bitcast.far_ref, bf16[800,384]{1,0:T(8,128)(2,1)S(1)} %collective-permute-done.5.refs_0_, ...), custom_call_target="tpu_custom_call" | custom-call | flops 13589544960 | bytes 2949120 | tf_op jit(solution)/shard_map/pairs/pallas_call | solution.py:297
  129.6 0.1 collective-permute-start.11
  129.7 2.5 %collective-permute-start.12 = (bf16[2,384,384]{2,1,0:T(8,128)(2,1)S(1)}, bf16[2,384,384]{2,1,0:T(8,128)(2,1)S(1)}, u32[]{:S(2)}, u32[]{:S(2)}) collective-permute-start(bf16[2,384,384]{2,1,0:T(8,128)(2,1)S(1)} %get-tuple-element.106), channel_id=1, source_target_pairs={{0,0},{24,24},{8,16},{16,8},{1,1},{25,25},{9,17},{17,9},{2,2},{26,... | collective-permute-start | bytes 1769480 | tf_op jit(solution)/shard_map/ppermute | solution.py:443
  132.2 0.0 collective-permute-done.16.rest_0_
  132.2 0.2 collective-permute-start.17
  132.4 4.3 %collective-permute-start.18 = (bf16[384,384]{1,0:T(8,128)(2,1)S(1)}, bf16[384,384]{1,0:T(8,128)(2,1)S(1)}, u32[]{:S(2)}, u32[]{:S(2)}) collective-permute-start(bf16[384,384]{1,0:T(8,128)(2,1)S(1)} %get-tuple-element.123), channel_id=1, source_target_pairs={{0,0},{7,7},{1,2},{2,1},{3,4},{4,3},{5,6},{6,5},{8,8},{15,15},{9,1... | collective-permute-start | bytes 884744 | tf_op jit(solution)/shard_map/ppermute | solution.py:443
  136.7 1.2 finish.3
  137.8 0.0 collective-permute-done.13.near
  137.8 1.8 %finish.4 = (bf16[384,1536]{1,0:T(8,128)(2,1)}, bf16[384,1536]{1,0:T(8,128)(2,1)}, bf16[384,1536]{1,0:T(8,128)(2,1)}) custom-call(f32[2,384,640]{2,1,0:T(8,128)S(1)} %get-tuple-element.92.own_kv, bf16[2,384,640]{2,1,0:T(8,128)(2,1)S(1)} %collective-permute-done.13.near, ...), custom_call_target="tpu_custom_call", output_to_operand_aliasing={{0}: (5, {}), {1}: (6, {}), {2}: (7, {})} | custom-call | flops 1966080 | bytes 7372800 | tf_op jit(solution)/shard_map/finish/pallas_call | solution.py:346
  139.6 6.8 %collective-permute-done.17.rest_0_ = bf16[384,384]{1,0:T(8,128)(2,1)S(1)} collective-permute-done((bf16[384,384]{1,0:T(8,128)(2,1)S(1)}, bf16[384,384]{1,0:T(8,128)(2,1)S(1)}, u32[]{:S(2)}, u32[]{:S(2)}) %collective-permute-start.17) | collective-permute-done | bytes 294944 | tf_op jit(solution)/shard_map/ppermute | solution.py:443
  146.5 0.0 collective-permute-done.18.rest_1_
  146.5 0.0 collective-permute-done.11.near
  146.5 0.0 collective-permute-done.12.far
  146.5 1.1 finish.5
  (11 shorter events, 0.0 us)
Async XLA Ops:
  0.6 5.6 %copy-start = (f32[1,1,12,384]{3,1,2,0:T(1,128)S(1)}, f32[1,1,12,384]{3,1,2,0:T(1,128)}, u32[]{:S(2)}) copy-start(f32[1,1,12,384]{3,1,2,0:T(1,128)} %param.12) | copy-start | bytes 55300
  0.6 5.6 %copy-start.1 = (s32[1,1,9]{2,1,0:T(1,128)S(1)}, s32[1,1,9]{2,1,0:T(1,128)}, u32[]{:S(2)}) copy-start(s32[1,1,9]{2,1,0:T(1,128)} %param.13) | copy-start | bytes 112
  2.4 12.8 %collective-permute-start.2 = (bf16[2,384,1536]{2,1,0:T(8,128)(2,1)S(1)}, bf16[2,384,1536]{2,1,0:T(8,128)(2,1)}, u32[]{:S(2)}, u32[]{:S(2)}) collective-permute-start(bf16[2,384,1536]{2,1,0:T(8,128)(2,1)S(1)} %pack.1.refs_1_.refs_3_.refs_2_), channel_id=1, source_target_pairs={{0,8},{8,0},{16,24},{24,16},{1,9},{9,1},{17,25},{25,17},{2,10},{10... | collective-permute-start | bytes 7077896 | tf_op jit(solution)/shard_map/ppermute | solution.py:396
  3.2 48.9 %collective-permute-start.4 = (bf16[2,384,1536]{2,1,0:T(8,128)(2,1)S(1)}, bf16[2,384,1536]{2,1,0:T(8,128)(2,1)}, u32[]{:S(2)}, u32[]{:S(2)}) collective-permute-start(bf16[2,384,1536]{2,1,0:T(8,128)(2,1)S(1)} %pack.1.refs_1_.refs_3_.refs_2_), channel_id=1, source_target_pairs={{0,0},{24,24},{8,16},{16,8},{1,1},{25,25},{9,17},{17,9},{2,2},{26,... | collective-permute-start | bytes 7077896 | tf_op jit(solution)/shard_map/ppermute | solution.py:397
  8.5 22.9 %collective-permute-start.1 = (bf16[800,512]{1,0:T(8,128)(2,1)S(1)}, bf16[800,512]{1,0:T(8,128)(2,1)}, u32[]{:S(2)}, u32[]{:S(2)}) collective-permute-start(bf16[800,512]{1,0:T(8,128)(2,1)S(1)} %prep.2.refs_0_.refs_1_), channel_id=1, source_target_pairs={{0,1},{1,0},{2,3},{3,2},{4,5},{5,4},{6,7},{7,6},{8,9},{9,8},{10,11... | collective-permute-start | bytes 2457608 | tf_op jit(solution)/shard_map/ppermute | solution.py:402
  13.8 37.0 %collective-permute-start.6 = (bf16[800,640]{1,0:T(8,128)(2,1)}, bf16[800,640]{1,0:T(8,128)(2,1)}, u32[]{:S(2)}, u32[]{:S(2)}) collective-permute-start(bf16[800,640]{1,0:T(8,128)(2,1)} %get-tuple-element.70.refs_0_.refs_1_), channel_id=1, source_target_pairs={{0,1},{1,0},{2,3},{3,2},{4,5},{5,4},{6,7},{7,6},{8,9},{9,8},{10,11... | collective-permute-start | bytes 3072008 | tf_op jit(solution)/shard_map/ppermute | solution.py:467
  14.0 57.4 %collective-permute-start = (bf16[800,384]{1,0:T(8,128)(2,1)}, bf16[800,384]{1,0:T(8,128)(2,1)}, u32[]{:S(2)}, u32[]{:S(2)}) collective-permute-start(bf16[800,384]{1,0:T(8,128)(2,1)} %get-tuple-element.75.refs_0_.refs_1_), channel_id=1, source_target_pairs={{0,1},{1,0},{2,3},{3,2},{4,5},{5,4},{6,7},{7,6},{8,9},{9,8},{10,11... | collective-permute-start | bytes 1843208 | tf_op jit(solution)/shard_map/ppermute | solution.py:467
  31.4 20.7 %collective-permute-start.3 = (bf16[800,512]{1,0:T(8,128)(2,1)}, bf16[800,512]{1,0:T(8,128)(2,1)S(1)}, u32[]{:S(2)}, u32[]{:S(2)}) collective-permute-start(bf16[800,512]{1,0:T(8,128)(2,1)} %collective-permute-done.1.refs_0_.refs_2_), channel_id=1, source_target_pairs={{0,2},{2,4},{4,6},{6,0},{1,7},{3,1},{5,3},{7,5},{8,10},{10,12},{12... | collective-permute-start | bytes 2457608 | tf_op jit(solution)/shard_map/ppermute | solution.py:449
  50.8 29.7 %collective-permute-start.7 = (bf16[800,640]{1,0:T(8,128)(2,1)}, bf16[800,640]{1,0:T(8,128)(2,1)S(1)}, u32[]{:S(2)}, u32[]{:S(2)}) collective-permute-start(bf16[800,640]{1,0:T(8,128)(2,1)} %collective-permute-done.6.refs_0_.refs_2_), channel_id=1, source_target_pairs={{0,2},{2,4},{4,6},{6,0},{1,7},{3,1},{5,3},{7,5},{8,10},{10,12},{12... | collective-permute-start | bytes 3072008 | tf_op jit(solution)/shard_map/ppermute | solution.py:449
  69.8 38.3 %collective-permute-start.8 = (bf16[384,512]{1,0:T(8,128)(2,1)S(1)}, bf16[384,512]{1,0:T(8,128)(2,1)S(1)}, u32[]{:S(2)}, u32[]{:S(2)}) collective-permute-start(bf16[384,512]{1,0:T(8,128)(2,1)S(1)} %get-tuple-element.97), channel_id=1, source_target_pairs={{2,0},{4,2},{6,4},{1,3},{3,5},{5,7},{0,1},{7,6},{10,8},{12,10},{14... | collective-permute-start | bytes 1179656 | tf_op jit(solution)/shard_map/ppermute | solution.py:443
  71.5 47.3 %collective-permute-start.10 = (bf16[2,384,512]{2,1,0:T(8,128)(2,1)S(1)}, bf16[2,384,512]{2,1,0:T(8,128)(2,1)S(1)}, u32[]{:S(2)}, u32[]{:S(2)}) collective-permute-start(bf16[2,384,512]{2,1,0:T(8,128)(2,1)S(1)} %get-tuple-element.99), channel_id=1, source_target_pairs={{0,8},{8,0},{16,24},{24,16},{1,9},{9,1},{17,25},{25,17},{2,10},{10... | collective-permute-start | bytes 2359304 | tf_op jit(solution)/shard_map/ppermute | solution.py:443
  71.5 45.8 %collective-permute-start.5 = (bf16[800,384]{1,0:T(8,128)(2,1)}, bf16[800,384]{1,0:T(8,128)(2,1)S(1)}, u32[]{:S(2)}, u32[]{:S(2)}) collective-permute-start(bf16[800,384]{1,0:T(8,128)(2,1)} %collective-permute-done.refs_0_), channel_id=1, source_target_pairs={{0,2},{2,4},{4,6},{6,0},{1,7},{3,1},{5,3},{7,5},{8,10},{10,12},{12... | collective-permute-start | bytes 1843208 | tf_op jit(solution)/shard_map/ppermute | solution.py:449
  102.0 15.0 %collective-permute-start.15 = (bf16[384,640]{1,0:T(8,128)(2,1)S(1)}, bf16[384,640]{1,0:T(8,128)(2,1)S(1)}, u32[]{:S(2)}, u32[]{:S(2)}) collective-permute-start(bf16[384,640]{1,0:T(8,128)(2,1)S(1)} %get-tuple-element.116), channel_id=1, source_target_pairs={{2,0},{4,2},{6,4},{1,3},{3,5},{5,7},{0,1},{7,6},{10,8},{12,10},{14... | collective-permute-start | bytes 1474568 | tf_op jit(solution)/shard_map/ppermute | solution.py:443
  103.9 28.5 %collective-permute-start.14 = (bf16[2,384,1152]{2,1,0:T(8,128)(2,1)S(1)}, bf16[2,384,1152]{2,1,0:T(8,128)(2,1)S(1)}, u32[]{:S(2)}, u32[]{:S(2)}) collective-permute-start(bf16[2,384,1152]{2,1,0:T(8,128)(2,1)S(1)} %get-tuple-element.109), channel_id=1, source_target_pairs={{0,0},{24,24},{8,16},{16,8},{1,1},{25,25},{9,17},{17,9},{2,2},{26,... | collective-permute-start | bytes 5308424 | tf_op jit(solution)/shard_map/ppermute | solution.py:443
  108.3 10.5 %collective-permute-start.9 = (bf16[384,512]{1,0:T(8,128)(2,1)S(1)}, bf16[384,512]{1,0:T(8,128)(2,1)S(1)}, u32[]{:S(2)}, u32[]{:S(2)}) collective-permute-start(bf16[384,512]{1,0:T(8,128)(2,1)S(1)} %add_convert_fusion.1), channel_id=1, source_target_pairs={{0,1},{1,0},{2,3},{3,2},{4,5},{5,4},{6,7},{7,6},{8,9},{9,8},{10,11... | collective-permute-start | bytes 1179656 | tf_op jit(solution)/shard_map/ppermute | solution.py:453
  117.0 20.8 %collective-permute-start.13 = (bf16[2,384,640]{2,1,0:T(8,128)(2,1)S(1)}, bf16[2,384,640]{2,1,0:T(8,128)(2,1)S(1)}, u32[]{:S(2)}, u32[]{:S(2)}) collective-permute-start(bf16[2,384,640]{2,1,0:T(8,128)(2,1)S(1)} %get-tuple-element.108), channel_id=1, source_target_pairs={{0,8},{8,0},{16,24},{24,16},{1,9},{9,1},{17,25},{25,17},{2,10},{10... | collective-permute-start | bytes 2949128 | tf_op jit(solution)/shard_map/ppermute | solution.py:443
  117.2 14.9 %collective-permute-start.16 = (bf16[384,640]{1,0:T(8,128)(2,1)S(1)}, bf16[384,640]{1,0:T(8,128)(2,1)S(1)}, u32[]{:S(2)}, u32[]{:S(2)}) collective-permute-start(bf16[384,640]{1,0:T(8,128)(2,1)S(1)} %add_convert_fusion), channel_id=1, source_target_pairs={{0,1},{1,0},{2,3},{3,2},{4,5},{5,4},{6,7},{7,6},{8,9},{9,8},{10,11... | collective-permute-start | bytes 1474568 | tf_op jit(solution)/shard_map/ppermute | solution.py:453
  129.6 16.9 %collective-permute-start.11 = (bf16[2,384,384]{2,1,0:T(8,128)(2,1)S(1)}, bf16[2,384,384]{2,1,0:T(8,128)(2,1)S(1)}, u32[]{:S(2)}, u32[]{:S(2)}) collective-permute-start(bf16[2,384,384]{2,1,0:T(8,128)(2,1)S(1)} %get-tuple-element.105), channel_id=1, source_target_pairs={{0,8},{8,0},{16,24},{24,16},{1,9},{9,1},{17,25},{25,17},{2,10},{10... | collective-permute-start | bytes 1769480 | tf_op jit(solution)/shard_map/ppermute | solution.py:443
  129.7 16.8 %collective-permute-start.12 = (bf16[2,384,384]{2,1,0:T(8,128)(2,1)S(1)}, bf16[2,384,384]{2,1,0:T(8,128)(2,1)S(1)}, u32[]{:S(2)}, u32[]{:S(2)}) collective-permute-start(bf16[2,384,384]{2,1,0:T(8,128)(2,1)S(1)} %get-tuple-element.106), channel_id=1, source_target_pairs={{0,0},{24,24},{8,16},{16,8},{1,1},{25,25},{9,17},{17,9},{2,2},{26,... | collective-permute-start | bytes 1769480 | tf_op jit(solution)/shard_map/ppermute | solution.py:443
  132.2 14.3 %collective-permute-start.17 = (bf16[384,384]{1,0:T(8,128)(2,1)S(1)}, bf16[384,384]{1,0:T(8,128)(2,1)S(1)}, u32[]{:S(2)}, u32[]{:S(2)}) collective-permute-start(bf16[384,384]{1,0:T(8,128)(2,1)S(1)} %get-tuple-element.122), channel_id=1, source_target_pairs={{0,1},{1,0},{2,3},{3,2},{4,5},{5,4},{6,7},{7,6},{8,9},{9,8},{10,11... | collective-permute-start | bytes 884744 | tf_op jit(solution)/shard_map/ppermute | solution.py:443
  132.4 14.1 %collective-permute-start.18 = (bf16[384,384]{1,0:T(8,128)(2,1)S(1)}, bf16[384,384]{1,0:T(8,128)(2,1)S(1)}, u32[]{:S(2)}, u32[]{:S(2)}) collective-permute-start(bf16[384,384]{1,0:T(8,128)(2,1)S(1)} %get-tuple-element.123), channel_id=1, source_target_pairs={{0,0},{7,7},{1,2},{2,1},{3,4},{4,3},{5,6},{6,5},{8,8},{15,15},{9,1... | collective-permute-start | bytes 884744 | tf_op jit(solution)/shard_map/ppermute | solution.py:443
where the time goes:
time: 149 us; the launch traced here: 148 us
  Pallas kernels  109 us (73%)
  starting transfers between devices  25.6 us (17%)
  waiting for transfers between devices  11.7 us (8%)
    pallas_call x9, Pallas kernels, run_stage(): pl.pallas_call(functools.partial(stage_kernel, work, names, carried, last...  97 us
    ppermute x9, starting transfers between devices, stage(): backs[c][name] = lax.ppermute(sums[c][name], axis, pairs)  14.8 us
    ppermute x9, waiting for transfers between devices, stage(): backs[c][name] = lax.ppermute(sums[c][name], axis, pairs)  6.84 us
    pallas_call x2, Pallas kernels, prep(): pl.pallas_call(functools.partial(prep_kernel, counts, *sizes), grid_spec=...  6.24 us
    ppermute x2, waiting for transfers between devices, per_device(): theirs[c] = lax.ppermute(mine[c], 'space', partner)  4.79 us
    pallas_call x3, Pallas kernels, finish(): pl.pallas_call(functools.partial(finish_kernel, head_width ** (-0.5), len...  4.08 us
    ppermute x1, starting transfers between devices, per_device(): far_kv = lax.ppermute(own_kv, 'tm', far_pairs)  3.05 us
  transfers between devices with their start and end apart: 19, of which 2 were waited for; matrix products, arithmetic and copies ran while one was open for 0% of the time, Pallas kernels for 72%

commit v1 on v0

--- a/solution.py
+++ b/solution.py
@@ -10,6 +10,7 @@
 
 F32 = jnp.float32
 BF16 = jnp.bfloat16
+LOG2E = math.log2(math.e)
 FAR_AWAY = 1e30
 
 OUTER, OWN, PARTNER = (0, 1, 2)
@@ -31,7 +32,6 @@
 EXTRA = 32
 VMEM_LIMIT = 20 * 1024 * 1024
 GROUP = 1
-BLOCK = 256
 
 
 def dot(a, b, dims):
@@ -93,7 +93,7 @@
             low = (prod - high.astype(F32)).astype(BF16)
             delta = dot(ones, high, ((1,), (1,))) + dot(ones, low, ((1,), (1,)))
             lines = []
-            for line in (lse_ref[head], delta[0:1, :]):
+            for line in (lse_ref[head] * LOG2E, delta[0:1, :]):
                 for term in three_terms(line):
                     lines += fold(term)
             lines.append(flags)
@@ -185,37 +185,31 @@
     }
     started = set()
 
-    def add_q(j, i, rows, term):
+    def add_q(j, i, term):
         name, cols = ("q%d" % j, heads[i])
-        if (j, i, rows.start) in started:
-            env["sum_" + name][rows, cols] += term
+        if (j, i) in started:
+            env["sum_" + name][:, cols] += term
         elif "acc_" + name in env:
-            env["sum_" + name][rows, cols] = env["acc_" + name][rows, cols] + term
+            env["sum_" + name][:, cols] = env["acc_" + name][:, cols] + term
         else:
-            env["sum_" + name][rows, cols] = term
-        started.add((j, i, rows.start))
+            env["sum_" + name][:, cols] = term
+        started.add((j, i))
 
     def pair_terms(slot, j, i):
         cols = heads[i]
         message, keys = (env["message%d" % j], env["keys%d" % slot])
+        queries, grads = (message[0:tile, cols], message[tile : 2 * tile, cols])
         key, value = (keys[0, :, cols], keys[1, :, cols])
         shift, delta, flags = stats[j, i]
         lane = 3 * j + slot
         shift = jnp.where(flags[:, lane : lane + 1] > 0, shift, FAR_AWAY)
-        term_k, term_v = (None, None)
-        for low in range(0, tile, BLOCK):
-            rows = slice(low, min(low + BLOCK, tile))
-            queries = message[rows, cols]
-            grads = message[tile + rows.start : tile + rows.stop, cols]
-            scores = dot(key, queries, ((1,), (1,)))
-            weights = jnp.exp(scores * factor - shift[:, rows])
-            grad_prob = dot(value, grads, ((1,), (1,)))
-            grad_score = (weights * (grad_prob - delta[:, rows])).astype(BF16)
-            more_v = dot(weights.astype(BF16), grads, ((1,), (0,)))
-            more_k = dot(grad_score, queries, ((1,), (0,)))
-            add_q(j, i, rows, dot(grad_score, key, ((0,), (0,))))
-            term_k = more_k if term_k is None else term_k + more_k
-            term_v = more_v if term_v is None else term_v + more_v
+        scores = dot(key, queries, ((1,), (1,)))
+        weights = jnp.exp2(scores * (factor * LOG2E) - shift)
+        grad_prob = dot(value, grads, ((1,), (1,)))
+        grad_score = (weights * (grad_prob - delta)).astype(BF16)
+        term_v = dot(weights.astype(BF16), grads, ((1,), (0,)))
+        term_k = dot(grad_score, queries, ((1,), (0,)))
+        add_q(j, i, dot(grad_score, key, ((0,), (0,))))
         return (term_k, term_v)
 
     def key_frames(slots_js):
@@ -236,7 +230,7 @@
     key_frames([(slot, js) for slot, js in work if slot != FAR])
     for slot, js in work:
         if slot == FAR:
-            fresh = [j for j in js if (j, 0, 0) not in started]
+            fresh = [j for j in js if (j, 0) not in started]
             pl.when(far_ref[0] > 0)(functools.partial(key_frames, [(slot, js)]))
 
             @pl.when(far_ref[0] == 0)

time: 149 us -> 140 us (0.940)
  Pallas kernels: 109 us -> 90 us
  waiting for transfers between devices: 11.7 us -> 20.9 us
    pallas_call x9, Pallas kernels: 97 us -> 77.9 us  [run_stage(): pl.pallas_call(functools.partial(stage_kernel, work, names, carried, last...]
    ppermute x2, waiting for transfers between devices: 4.79 us -> 9.5 us  [per_device(): theirs[c] = lax.ppermute(mine[c], 'space', partner)]
    ppermute x9, starting transfers between devices: 14.8 us -> 12.1 us  [stage(): backs[c][name] = lax.ppermute(sums[c][name], axis, pairs)]
    ppermute x9, waiting for transfers between devices: 6.84 us -> 9.41 us  [stage(): backs[c][name] = lax.ppermute(sums[c][name], axis, pairs)]
    ppermute x2, starting transfers between devices: 1.59 us -> 3.7 us  [send_back(): backs[c]['q2'] = lax.ppermute(total.astype(BF16), 'space', partner)]
  transfers between devices with their start and end apart: 19 -> 19, of which waited for: 2 -> 5; matrix products, arithmetic and copies ran while one was open for 0% -> 0% of each run, Pallas kernels for 72% -> 63%
where the time goes in v1:
time: 140 us; the launch traced here: 139 us
  Pallas kernels  90 us (64%)
  starting transfers between devices  26.5 us (19%)
  waiting for transfers between devices  20.9 us (15%)
    pallas_call x9, Pallas kernels, run_stage(): pl.pallas_call(functools.partial(stage_kernel, work, names, carried, last...  77.9 us
    ppermute x9, starting transfers between devices, stage(): backs[c][name] = lax.ppermute(sums[c][name], axis, pairs)  12.1 us
    ppermute x2, waiting for transfers between devices, per_device(): theirs[c] = lax.ppermute(mine[c], 'space', partner)  9.5 us
    ppermute x9, waiting for transfers between devices, stage(): backs[c][name] = lax.ppermute(sums[c][name], axis, pairs)  9.41 us
    pallas_call x2, Pallas kernels, prep(): pl.pallas_call(functools.partial(prep_kernel, counts, *sizes), grid_spec=...  6.23 us
    ppermute x3, starting transfers between devices, hand_on(): outers[c] = lax.ppermute(after(theirs[c], *done[-1:]), 'space', onward)  4.08 us
    pallas_call x3, Pallas kernels, finish(): pl.pallas_call(functools.partial(finish_kernel, head_width ** (-0.5), len...  4.08 us
    ppermute x2, starting transfers between devices, send_back(): backs[c]['q2'] = lax.ppermute(total.astype(BF16), 'space', partner)  3.7 us
  transfers between devices with their start and end apart: 19, of which 5 were waited for; matrix products, arithmetic and copies ran while one was open for 0% of the time, Pallas kernels for 63%

profile of v1, /device:TPU:9, one launch (start us, length us, event | category | flops | bytes accessed | tf_op | source)
XLA Modules:
  0.0 138.5 jit_solution(1829151278564237819)
XLA Ops:
  0.7 1.8 %pack.1.refs_1_.refs_3_.refs_2_ = bf16[2,384,1536]{2,1,0:T(8,128)(2,1)S(1)} custom-call(bf16[384,1536]{1,0:T(8,128)(2,1)} %bitcast.26, bf16[384,1536]{1,0:T(8,128)(2,1)} %bitcast.27), custom_call_target="tpu_custom_call" | custom-call | bytes 4718592 | tf_op jit(solution)/shard_map/pack/pallas_call | solution.py:149
  2.4 0.7 collective-permute-start.2
  3.2 3.0 %collective-permute-start.4 = (bf16[2,384,1536]{2,1,0:T(8,128)(2,1)S(1)}, bf16[2,384,1536]{2,1,0:T(8,128)(2,1)}, u32[]{:S(2)}, u32[]{:S(2)}) collective-permute-start(bf16[2,384,1536]{2,1,0:T(8,128)(2,1)S(1)} %pack.1.refs_1_.refs_3_.refs_2_), channel_id=1, source_target_pairs={{0,0},{24,24},{8,16},{16,8},{1,1},{25,25},{9,17},{17,9},{2,2},{26,... | collective-permute-start | bytes 7077896 | tf_op jit(solution)/shard_map/ppermute | solution.py:391
  6.3 2.2 %prep.2.refs_0_.refs_1_ = bf16[800,512]{1,0:T(8,128)(2,1)S(1)} custom-call(s32[1]{0:T(128)} %bitcast.1.frame_ref, s32[1]{0:T(128)} %bitcast.2.row_ref, s32[9]{0:T(128)S(1)} %bitcast.15, bf16[384,1536]{1,0:T(8,128)(2,1)} %bitcast.20, bf16[384,1536]{1,0:T(8,128)(2,1)} %bitcast.22, bf16[384,1536]{1,0:T(8,128)(2,1)} %bitcast.24, f32[12,1,384]{2,1,0:T(1,128)S(1)} %bitcast.13), custom_call_target="tpu_custom_call" | custom-call | flops 393216 | bytes 1966080 | tf_op jit(solution)/shard_map/prep/pallas_call | solution.py:114
  8.5 1.3 collective-permute-start.1
  9.8 4.0 %prep.3 = (bf16[800,640]{1,0:T(8,128)(2,1)}, bf16[800,384]{1,0:T(8,128)(2,1)}) custom-call(s32[1]{0:T(128)} %bitcast.1.frame_ref, s32[1]{0:T(128)} %bitcast.2.row_ref, s32[9]{0:T(128)S(1)} %bitcast.16, bf16[384,1536]{1,0:T(8,128)(2,1)} %bitcast.21, bf16[384,1536]{1,0:T(8,128)(2,1)} %bitcast.23, bf16[384,1536]{1,0:T(8,128)(2,1)} %bitcast.25, ...), custom_call_target="tpu_custom_call" | custom-call | flops 786432 | bytes 3932160 | tf_op jit(solution)/shard_map/prep/pallas_call | solution.py:114
  13.8 0.3 collective-permute-start.6
  14.0 1.2 collective-permute-start
  15.3 0.0 collective-permute-done.2.refs_2_.refs_4_.refs_3_
  15.3 5.6 %pairs.9 = (f32[384,512]{1,0:T(8,128)S(1)}, f32[2,384,512]{2,1,0:T(8,128)S(1)}, f32[2,384,512]{2,1,0:T(8,128)S(1)}) custom-call(s32[1]{0:T(128)} %bitcast.far_ref, bf16[800,512]{1,0:T(8,128)(2,1)S(1)} %prep.2.refs_0_.refs_1_, bf16[2,384,1536]{2,1,0:T(8,128)(2,1)S(1)} %pack.1.refs_1_.refs_3_.refs_2_, ...), custom_call_target="tpu_custom_call" | custom-call | flops 9059696640 | bytes 3932160 | tf_op jit(solution)/shard_map/pairs/pallas_call | solution.py:291
  20.9 6.5 %pairs.10 = (f32[384,640]{1,0:T(8,128)S(1)}, f32[2,384,640]{2,1,0:T(8,128)S(1)}, f32[2,384,640]{2,1,0:T(8,128)S(1)}) custom-call(s32[1]{0:T(128)} %bitcast.far_ref, bf16[800,640]{1,0:T(8,128)(2,1)} %get-tuple-element.70.refs_0_.refs_1_, bf16[2,384,1536]{2,1,0:T(8,128)(2,1)S(1)} %pack.1.refs_1_.refs_3_.refs_2_, ...), custom_call_target="tpu_custom_call" | custom-call | flops 11324620800 | bytes 4915200 | tf_op jit(solution)/shard_map/pairs/pallas_call | solution.py:291
  27.4 1.5 %collective-permute-done.1.refs_0_.refs_2_ = bf16[800,512]{1,0:T(8,128)(2,1)} collective-permute-done((bf16[800,512]{1,0:T(8,128)(2,1)S(1)}, bf16[800,512]{1,0:T(8,128)(2,1)}, u32[]{:S(2)}, u32[]{:S(2)}) %collective-permute-start.1) | collective-permute-done | bytes 819232 | tf_op jit(solution)/shard_map/ppermute | solution.py:396
  28.9 1.3 collective-permute-start.3
  30.2 6.8 %pairs.11 = (f32[384,512]{1,0:T(8,128)S(1)}, f32[2,384,512]{2,1,0:T(8,128)S(1)}, f32[2,384,512]{2,1,0:T(8,128)S(1)}) custom-call(s32[1]{0:T(128)} %bitcast.far_ref, bf16[800,512]{1,0:T(8,128)(2,1)} %collective-permute-done.1.refs_0_.refs_2_, bf16[2,384,1536]{2,1,0:T(8,128)(2,1)S(1)} %pack.1.refs_1_.refs_3_.refs_2_, ...), custom_call_target="tpu_custom_call" | custom-call | flops 9059696640 | bytes 3932160 | tf_op jit(solution)/shard_map/pairs/pallas_call | solution.py:291
  37.0 4.3 %pairs.12 = (f32[384,384]{1,0:T(8,128)S(1)}, f32[2,384,384]{2,1,0:T(8,128)S(1)}, f32[2,384,384]{2,1,0:T(8,128)S(1)}) custom-call(s32[1]{0:T(128)} %bitcast.far_ref, bf16[800,384]{1,0:T(8,128)(2,1)} %get-tuple-element.75.refs_0_.refs_1_, bf16[2,384,1536]{2,1,0:T(8,128)(2,1)S(1)} %pack.1.refs_1_.refs_3_.refs_2_, ...), custom_call_target="tpu_custom_call" | custom-call | flops 27179089920 | bytes 2949120 | tf_op jit(solution)/shard_map/pairs/pallas_call | solution.py:291
  41.3 9.5 %collective-permute-done.6.refs_0_.refs_2_ = bf16[800,640]{1,0:T(8,128)(2,1)} collective-permute-done((bf16[800,640]{1,0:T(8,128)(2,1)}, bf16[800,640]{1,0:T(8,128)(2,1)}, u32[]{:S(2)}, u32[]{:S(2)}) %collective-permute-start.6) | collective-permute-done | bytes 1024032 | tf_op jit(solution)/shard_map/ppermute | solution.py:461
  50.8 1.3 collective-permute-start.7
  52.1 0.0 collective-permute-done.3.refs_0_
  52.1 0.0 collective-permute-done.4.refs_5_.refs_3_.refs_4_
  52.1 13.8 %pairs.13 = (bf16[384,512]{1,0:T(8,128)(2,1)S(1)}, f32[384,512]{1,0:T(8,128)S(1)}, f32[384,512]{1,0:T(8,128)S(1)}, f32[2,384,512]{2,1,0:T(8,128)S(1)}, bf16[2,38...) custom-call(s32[1]{0:T(128)} %bitcast.far_ref, bf16[800,512]{1,0:T(8,128)(2,1)S(1)} %collective-permute-done.3.refs_0_, ...), custom_call_target="tpu_custom_call" | custom-call | flops 22649241600 | bytes 3932160 | tf_op jit(solution)/shard_map/pairs/pallas_call | solution.py:291
  66.0 0.2 collective-permute-start.8
  66.2 0.0 collective-permute-start.10
  66.2 1.5 %collective-permute-start.5 = (bf16[800,384]{1,0:T(8,128)(2,1)}, bf16[800,384]{1,0:T(8,128)(2,1)S(1)}, u32[]{:S(2)}, u32[]{:S(2)}) collective-permute-start(bf16[800,384]{1,0:T(8,128)(2,1)} %collective-permute-done.refs_0_), channel_id=1, source_target_pairs={{0,2},{2,4},{4,6},{6,0},{1,7},{3,1},{5,3},{7,5},{8,10},{10,12},{12... | collective-permute-start | bytes 1843208 | tf_op jit(solution)/shard_map/ppermute | solution.py:443
  67.7 8.0 %pairs.14 = (f32[384,640]{1,0:T(8,128)S(1)}, f32[2,384,640]{2,1,0:T(8,128)S(1)}, f32[2,384,640]{2,1,0:T(8,128)S(1)}) custom-call(s32[1]{0:T(128)} %bitcast.far_ref, bf16[800,640]{1,0:T(8,128)(2,1)} %collective-permute-done.6.refs_0_.refs_2_, bf16[2,384,1536]{2,1,0:T(8,128)(2,1)S(1)} %pack.1.refs_1_.refs_3_.refs_2_, ...), custom_call_target="tpu_custom_call" | custom-call | flops 5662310400 | bytes 4915200 | tf_op jit(solution)/shard_map/pairs/pallas_call | solution.py:291
  75.6 0.0 collective-permute-done.7.refs_0_
  75.7 16.7 %pairs.15 = (bf16[384,640]{1,0:T(8,128)(2,1)S(1)}, f32[384,640]{1,0:T(8,128)S(1)}, f32[384,640]{1,0:T(8,128)S(1)}, f32[2,384,640]{2,1,0:T(8,128)S(1)}, bf16[2,38...) custom-call(s32[1]{0:T(128)} %bitcast.far_ref, ...), custom_call_target="tpu_custom_call", output_to_operand_aliasing={{5}: (11, {})} | custom-call | flops 28311552000 | bytes 4915200 | tf_op jit(solution)/shard_map/pairs/pallas_call | solution.py:291
  92.3 1.9 %collective-permute-start.15 = (bf16[384,640]{1,0:T(8,128)(2,1)S(1)}, bf16[384,640]{1,0:T(8,128)(2,1)S(1)}, u32[]{:S(2)}, u32[]{:S(2)}) collective-permute-start(bf16[384,640]{1,0:T(8,128)(2,1)S(1)} %get-tuple-element.116), channel_id=1, source_target_pairs={{2,0},{4,2},{6,4},{1,3},{3,5},{5,7},{0,1},{7,6},{10,8},{12,10},{14... | collective-permute-start | bytes 1474568 | tf_op jit(solution)/shard_map/ppermute | solution.py:437
  94.2 4.6 %collective-permute-start.14 = (bf16[2,384,1152]{2,1,0:T(8,128)(2,1)S(1)}, bf16[2,384,1152]{2,1,0:T(8,128)(2,1)S(1)}, u32[]{:S(2)}, u32[]{:S(2)}) collective-permute-start(bf16[2,384,1152]{2,1,0:T(8,128)(2,1)S(1)} %get-tuple-element.109), channel_id=1, source_target_pairs={{0,0},{24,24},{8,16},{16,8},{1,1},{25,25},{9,17},{17,9},{2,2},{26,... | collective-permute-start | bytes 5308424 | tf_op jit(solution)/shard_map/ppermute | solution.py:437
  98.8 0.1 add_convert_fusion.1
  98.9 0.8 collective-permute-start.9
  99.7 7.2 %pairs.16 = (bf16[384,384]{1,0:T(8,128)(2,1)S(1)}, f32[2,384,384]{2,1,0:T(8,128)S(1)}, f32[2,384,384]{2,1,0:T(8,128)S(1)}, f32[2,384,384]{2,1,0:T(8,128)S(1)}) custom-call(s32[1]{0:T(128)} %bitcast.far_ref, bf16[800,384]{1,0:T(8,128)(2,1)} %collective-permute-done.refs_0_, bf16[2,384,1536]{2,1,0:T(8,128)(2,1)S(1)} %pack.1.refs_1_.refs_3_.refs_2_, ...), custom_call_target="tpu_custom_call" | custom-call | flops 20384317440 | bytes 2949120 | tf_op jit(solution)/shard_map/pairs/pallas_call | solution.py:291
  107.0 1.3 collective-permute-done.15
  108.3 0.4 collective-permute-start.13
  108.7 0.1 add_convert_fusion
  108.8 2.9 %collective-permute-start.16 = (bf16[384,640]{1,0:T(8,128)(2,1)S(1)}, bf16[384,640]{1,0:T(8,128)(2,1)S(1)}, u32[]{:S(2)}, u32[]{:S(2)}) collective-permute-start(bf16[384,640]{1,0:T(8,128)(2,1)S(1)} %add_convert_fusion), channel_id=1, source_target_pairs={{0,1},{1,0},{2,3},{3,2},{4,5},{5,4},{6,7},{7,6},{8,9},{9,8},{10,11... | collective-permute-start | bytes 1474568 | tf_op jit(solution)/shard_map/ppermute | solution.py:447
  111.7 0.0 collective-permute-done.9.rest_0_
  111.7 9.0 %pairs.17 = (bf16[384,384]{1,0:T(8,128)(2,1)S(1)}, f32[384,384]{1,0:T(8,128)S(1)}, f32[2,384,384]{2,1,0:T(8,128)S(1)}, bf16[2,384,384]{2,1,0:T(8,128)(2,1)S(1)}, bf16[2,384,384]{2,1,0:T(8,128)(2,1)S(1)}) custom-call(s32[1]{0:T(128)} %bitcast.far_ref, bf16[800,384]{1,0:T(8,128)(2,1)S(1)} %collective-permute-done.5.refs_0_, ...), custom_call_target="tpu_custom_call" | custom-call | flops 13589544960 | bytes 2949120 | tf_op jit(solution)/shard_map/pairs/pallas_call | solution.py:291
  120.7 0.1 collective-permute-start.11
  120.8 1.9 %collective-permute-start.12 = (bf16[2,384,384]{2,1,0:T(8,128)(2,1)S(1)}, bf16[2,384,384]{2,1,0:T(8,128)(2,1)S(1)}, u32[]{:S(2)}, u32[]{:S(2)}) collective-permute-start(bf16[2,384,384]{2,1,0:T(8,128)(2,1)S(1)} %get-tuple-element.106), channel_id=1, source_target_pairs={{0,0},{24,24},{8,16},{16,8},{1,1},{25,25},{9,17},{17,9},{2,2},{26,... | collective-permute-start | bytes 1769480 | tf_op jit(solution)/shard_map/ppermute | solution.py:437
  122.7 0.5 collective-permute-done.16.rest_0_
  123.2 1.2 collective-permute-start.17
  124.4 0.0 collective-permute-done.14.far
  124.4 1.9 %collective-permute-start.18 = (bf16[384,384]{1,0:T(8,128)(2,1)S(1)}, bf16[384,384]{1,0:T(8,128)(2,1)S(1)}, u32[]{:S(2)}, u32[]{:S(2)}) collective-permute-start(bf16[384,384]{1,0:T(8,128)(2,1)S(1)} %get-tuple-element.123), channel_id=1, source_target_pairs={{0,0},{7,7},{1,2},{2,1},{3,4},{4,3},{5,6},{6,5},{8,8},{15,15},{9,1... | collective-permute-start | bytes 884744 | tf_op jit(solution)/shard_map/ppermute | solution.py:437
  126.3 1.2 finish.3
  127.5 0.0 collective-permute-done.13.near
  127.5 1.8 %finish.4 = (bf16[384,1536]{1,0:T(8,128)(2,1)}, bf16[384,1536]{1,0:T(8,128)(2,1)}, bf16[384,1536]{1,0:T(8,128)(2,1)}) custom-call(f32[2,384,640]{2,1,0:T(8,128)S(1)} %get-tuple-element.92.own_kv, bf16[2,384,640]{2,1,0:T(8,128)(2,1)S(1)} %collective-permute-done.13.near, ...), custom_call_target="tpu_custom_call", output_to_operand_aliasing={{0}: (5, {}), {1}: (6, {}), {2}: (7, {})} | custom-call | flops 1966080 | bytes 7372800 | tf_op jit(solution)/shard_map/finish/pallas_call | solution.py:340
  129.3 8.1 %collective-permute-done.17.rest_0_ = bf16[384,384]{1,0:T(8,128)(2,1)S(1)} collective-permute-done((bf16[384,384]{1,0:T(8,128)(2,1)S(1)}, bf16[384,384]{1,0:T(8,128)(2,1)S(1)}, u32[]{:S(2)}, u32[]{:S(2)}) %collective-permute-start.17) | collective-permute-done | bytes 294944 | tf_op jit(solution)/shard_map/ppermute | solution.py:437
  137.4 1.1 finish.5
  (11 shorter events, 0.0 us)
Async XLA Ops:
  0.6 5.6 %copy-start = (f32[1,1,12,384]{3,1,2,0:T(1,128)S(1)}, f32[1,1,12,384]{3,1,2,0:T(1,128)}, u32[]{:S(2)}) copy-start(f32[1,1,12,384]{3,1,2,0:T(1,128)} %param.12) | copy-start | bytes 55300
  0.6 5.6 %copy-start.1 = (s32[1,1,9]{2,1,0:T(1,128)S(1)}, s32[1,1,9]{2,1,0:T(1,128)}, u32[]{:S(2)}) copy-start(s32[1,1,9]{2,1,0:T(1,128)} %param.13) | copy-start | bytes 112
  2.4 12.8 %collective-permute-start.2 = (bf16[2,384,1536]{2,1,0:T(8,128)(2,1)S(1)}, bf16[2,384,1536]{2,1,0:T(8,128)(2,1)}, u32[]{:S(2)}, u32[]{:S(2)}) collective-permute-start(bf16[2,384,1536]{2,1,0:T(8,128)(2,1)S(1)} %pack.1.refs_1_.refs_3_.refs_2_), channel_id=1, source_target_pairs={{0,8},{8,0},{16,24},{24,16},{1,9},{9,1},{17,25},{25,17},{2,10},{10... | collective-permute-start | bytes 7077896 | tf_op jit(solution)/shard_map/ppermute | solution.py:390
  3.2 48.9 %collective-permute-start.4 = (bf16[2,384,1536]{2,1,0:T(8,128)(2,1)S(1)}, bf16[2,384,1536]{2,1,0:T(8,128)(2,1)}, u32[]{:S(2)}, u32[]{:S(2)}) collective-permute-start(bf16[2,384,1536]{2,1,0:T(8,128)(2,1)S(1)} %pack.1.refs_1_.refs_3_.refs_2_), channel_id=1, source_target_pairs={{0,0},{24,24},{8,16},{16,8},{1,1},{25,25},{9,17},{17,9},{2,2},{26,... | collective-permute-start | bytes 7077896 | tf_op jit(solution)/shard_map/ppermute | solution.py:391
  8.5 20.4 %collective-permute-start.1 = (bf16[800,512]{1,0:T(8,128)(2,1)S(1)}, bf16[800,512]{1,0:T(8,128)(2,1)}, u32[]{:S(2)}, u32[]{:S(2)}) collective-permute-start(bf16[800,512]{1,0:T(8,128)(2,1)S(1)} %prep.2.refs_0_.refs_1_), channel_id=1, source_target_pairs={{0,1},{1,0},{2,3},{3,2},{4,5},{5,4},{6,7},{7,6},{8,9},{9,8},{10,11... | collective-permute-start | bytes 2457608 | tf_op jit(solution)/shard_map/ppermute | solution.py:396
  13.8 37.0 %collective-permute-start.6 = (bf16[800,640]{1,0:T(8,128)(2,1)}, bf16[800,640]{1,0:T(8,128)(2,1)}, u32[]{:S(2)}, u32[]{:S(2)}) collective-permute-start(bf16[800,640]{1,0:T(8,128)(2,1)} %get-tuple-element.70.refs_0_.refs_1_), channel_id=1, source_target_pairs={{0,1},{1,0},{2,3},{3,2},{4,5},{5,4},{6,7},{7,6},{8,9},{9,8},{10,11... | collective-permute-start | bytes 3072008 | tf_op jit(solution)/shard_map/ppermute | solution.py:461
  14.0 52.1 %collective-permute-start = (bf16[800,384]{1,0:T(8,128)(2,1)}, bf16[800,384]{1,0:T(8,128)(2,1)}, u32[]{:S(2)}, u32[]{:S(2)}) collective-permute-start(bf16[800,384]{1,0:T(8,128)(2,1)} %get-tuple-element.75.refs_0_.refs_1_), channel_id=1, source_target_pairs={{0,1},{1,0},{2,3},{3,2},{4,5},{5,4},{6,7},{7,6},{8,9},{9,8},{10,11... | collective-permute-start | bytes 1843208 | tf_op jit(solution)/shard_map/ppermute | solution.py:461
  28.9 23.2 %collective-permute-start.3 = (bf16[800,512]{1,0:T(8,128)(2,1)}, bf16[800,512]{1,0:T(8,128)(2,1)S(1)}, u32[]{:S(2)}, u32[]{:S(2)}) collective-permute-start(bf16[800,512]{1,0:T(8,128)(2,1)} %collective-permute-done.1.refs_0_.refs_2_), channel_id=1, source_target_pairs={{0,2},{2,4},{4,6},{6,0},{1,7},{3,1},{5,3},{7,5},{8,10},{10,12},{12... | collective-permute-start | bytes 2457608 | tf_op jit(solution)/shard_map/ppermute | solution.py:443
  50.8 24.9 %collective-permute-start.7 = (bf16[800,640]{1,0:T(8,128)(2,1)}, bf16[800,640]{1,0:T(8,128)(2,1)S(1)}, u32[]{:S(2)}, u32[]{:S(2)}) collective-permute-start(bf16[800,640]{1,0:T(8,128)(2,1)} %collective-permute-done.6.refs_0_.refs_2_), channel_id=1, source_target_pairs={{0,2},{2,4},{4,6},{6,0},{1,7},{3,1},{5,3},{7,5},{8,10},{10,12},{12... | collective-permute-start | bytes 3072008 | tf_op jit(solution)/shard_map/ppermute | solution.py:443
  66.0 32.8 %collective-permute-start.8 = (bf16[384,512]{1,0:T(8,128)(2,1)S(1)}, bf16[384,512]{1,0:T(8,128)(2,1)S(1)}, u32[]{:S(2)}, u32[]{:S(2)}) collective-permute-start(bf16[384,512]{1,0:T(8,128)(2,1)S(1)} %get-tuple-element.97), channel_id=1, source_target_pairs={{2,0},{4,2},{6,4},{1,3},{3,5},{5,7},{0,1},{7,6},{10,8},{12,10},{14... | collective-permute-start | bytes 1179656 | tf_op jit(solution)/shard_map/ppermute | solution.py:437
  66.2 45.6 %collective-permute-start.10 = (bf16[2,384,512]{2,1,0:T(8,128)(2,1)S(1)}, bf16[2,384,512]{2,1,0:T(8,128)(2,1)S(1)}, u32[]{:S(2)}, u32[]{:S(2)}) collective-permute-start(bf16[2,384,512]{2,1,0:T(8,128)(2,1)S(1)} %get-tuple-element.99), channel_id=1, source_target_pairs={{0,8},{8,0},{16,24},{24,16},{1,9},{9,1},{17,25},{25,17},{2,10},{10... | collective-permute-start | bytes 2359304 | tf_op jit(solution)/shard_map/ppermute | solution.py:437
  66.2 42.6 %collective-permute-start.5 = (bf16[800,384]{1,0:T(8,128)(2,1)}, bf16[800,384]{1,0:T(8,128)(2,1)S(1)}, u32[]{:S(2)}, u32[]{:S(2)}) collective-permute-start(bf16[800,384]{1,0:T(8,128)(2,1)} %collective-permute-done.refs_0_), channel_id=1, source_target_pairs={{0,2},{2,4},{4,6},{6,0},{1,7},{3,1},{5,3},{7,5},{8,10},{10,12},{12... | collective-permute-start | bytes 1843208 | tf_op jit(solution)/shard_map/ppermute | solution.py:443
  92.3 15.9 %collective-permute-start.15 = (bf16[384,640]{1,0:T(8,128)(2,1)S(1)}, bf16[384,640]{1,0:T(8,128)(2,1)S(1)}, u32[]{:S(2)}, u32[]{:S(2)}) collective-permute-start(bf16[384,640]{1,0:T(8,128)(2,1)S(1)} %get-tuple-element.116), channel_id=1, source_target_pairs={{2,0},{4,2},{6,4},{1,3},{3,5},{5,7},{0,1},{7,6},{10,8},{12,10},{14... | collective-permute-start | bytes 1474568 | tf_op jit(solution)/shard_map/ppermute | solution.py:437
  94.2 30.2 %collective-permute-start.14 = (bf16[2,384,1152]{2,1,0:T(8,128)(2,1)S(1)}, bf16[2,384,1152]{2,1,0:T(8,128)(2,1)S(1)}, u32[]{:S(2)}, u32[]{:S(2)}) collective-permute-start(bf16[2,384,1152]{2,1,0:T(8,128)(2,1)S(1)} %get-tuple-element.109), channel_id=1, source_target_pairs={{0,0},{24,24},{8,16},{16,8},{1,1},{25,25},{9,17},{17,9},{2,2},{26,... | collective-permute-start | bytes 5308424 | tf_op jit(solution)/shard_map/ppermute | solution.py:437
  98.9 12.8 %collective-permute-start.9 = (bf16[384,512]{1,0:T(8,128)(2,1)S(1)}, bf16[384,512]{1,0:T(8,128)(2,1)S(1)}, u32[]{:S(2)}, u32[]{:S(2)}) collective-permute-start(bf16[384,512]{1,0:T(8,128)(2,1)S(1)} %add_convert_fusion.1), channel_id=1, source_target_pairs={{0,1},{1,0},{2,3},{3,2},{4,5},{5,4},{6,7},{7,6},{8,9},{9,8},{10,11... | collective-permute-start | bytes 1179656 | tf_op jit(solution)/shard_map/ppermute | solution.py:447
  108.3 19.2 %collective-permute-start.13 = (bf16[2,384,640]{2,1,0:T(8,128)(2,1)S(1)}, bf16[2,384,640]{2,1,0:T(8,128)(2,1)S(1)}, u32[]{:S(2)}, u32[]{:S(2)}) collective-permute-start(bf16[2,384,640]{2,1,0:T(8,128)(2,1)S(1)} %get-tuple-element.108), channel_id=1, source_target_pairs={{0,8},{8,0},{16,24},{24,16},{1,9},{9,1},{17,25},{25,17},{2,10},{10... | collective-permute-start | bytes 2949128 | tf_op jit(solution)/shard_map/ppermute | solution.py:437
  108.8 14.4 %collective-permute-start.16 = (bf16[384,640]{1,0:T(8,128)(2,1)S(1)}, bf16[384,640]{1,0:T(8,128)(2,1)S(1)}, u32[]{:S(2)}, u32[]{:S(2)}) collective-permute-start(bf16[384,640]{1,0:T(8,128)(2,1)S(1)} %add_convert_fusion), channel_id=1, source_target_pairs={{0,1},{1,0},{2,3},{3,2},{4,5},{5,4},{6,7},{7,6},{8,9},{9,8},{10,11... | collective-permute-start | bytes 1474568 | tf_op jit(solution)/shard_map/ppermute | solution.py:447
  120.7 16.7 %collective-permute-start.11 = (bf16[2,384,384]{2,1,0:T(8,128)(2,1)S(1)}, bf16[2,384,384]{2,1,0:T(8,128)(2,1)S(1)}, u32[]{:S(2)}, u32[]{:S(2)}) collective-permute-start(bf16[2,384,384]{2,1,0:T(8,128)(2,1)S(1)} %get-tuple-element.105), channel_id=1, source_target_pairs={{0,8},{8,0},{16,24},{24,16},{1,9},{9,1},{17,25},{25,17},{2,10},{10... | collective-permute-start | bytes 1769480 | tf_op jit(solution)/shard_map/ppermute | solution.py:437
  120.8 16.6 %collective-permute-start.12 = (bf16[2,384,384]{2,1,0:T(8,128)(2,1)S(1)}, bf16[2,384,384]{2,1,0:T(8,128)(2,1)S(1)}, u32[]{:S(2)}, u32[]{:S(2)}) collective-permute-start(bf16[2,384,384]{2,1,0:T(8,128)(2,1)S(1)} %get-tuple-element.106), channel_id=1, source_target_pairs={{0,0},{24,24},{8,16},{16,8},{1,1},{25,25},{9,17},{17,9},{2,2},{26,... | collective-permute-start | bytes 1769480 | tf_op jit(solution)/shard_map/ppermute | solution.py:437
  123.2 14.2 %collective-permute-start.17 = (bf16[384,384]{1,0:T(8,128)(2,1)S(1)}, bf16[384,384]{1,0:T(8,128)(2,1)S(1)}, u32[]{:S(2)}, u32[]{:S(2)}) collective-permute-start(bf16[384,384]{1,0:T(8,128)(2,1)S(1)} %get-tuple-element.122), channel_id=1, source_target_pairs={{0,1},{1,0},{2,3},{3,2},{4,5},{5,4},{6,7},{7,6},{8,9},{9,8},{10,11... | collective-permute-start | bytes 884744 | tf_op jit(solution)/shard_map/ppermute | solution.py:437
  124.4 13.0 %collective-permute-start.18 = (bf16[384,384]{1,0:T(8,128)(2,1)S(1)}, bf16[384,384]{1,0:T(8,128)(2,1)S(1)}, u32[]{:S(2)}, u32[]{:S(2)}) collective-permute-start(bf16[384,384]{1,0:T(8,128)(2,1)S(1)} %get-tuple-element.123), channel_id=1, source_target_pairs={{0,0},{7,7},{1,2},{2,1},{3,4},{4,3},{5,6},{6,5},{8,8},{15,15},{9,1... | collective-permute-start | bytes 884744 | tf_op jit(solution)/shard_map/ppermute | solution.py:437

commit v2 on v1

--- a/solution.py
+++ b/solution.py
@@ -171,7 +171,7 @@
     return (rows[0], rows[1], extra[6 * parts : 6 * parts + 1])
 
 
-def stage_kernel(work, names, carried, last, factor, group, far_ref, *refs):
+def stage_kernel(work, names, factor, group, far_ref, *refs):
     env = dict(zip(names, refs))
     tile, wide = env["message%d" % work[0][1][0]].shape
     tile = (tile - EXTRA) // 2
@@ -208,7 +208,7 @@
         grad_prob = dot(value, grads, ((1,), (1,)))
         grad_score = (weights * (grad_prob - delta)).astype(BF16)
         term_v = dot(weights.astype(BF16), grads, ((1,), (0,)))
-        term_k = dot(grad_score, queries, ((1,), (0,)))
+        term_k = dot(grad_score, queries, ((1,), (0,))) * factor
         add_q(j, i, dot(grad_score, key, ((0,), (0,))))
         return (term_k, term_v)
 
@@ -217,14 +217,15 @@
             name = "kv%d" % slot
             out = env["out_" + name]
             for i, cols in enumerate(heads):
-                dk, dv = pair_terms(slot, js[0], i)
-                for j in js[1:]:
-                    more_k, more_v = pair_terms(slot, j, i)
-                    dk, dv = (dk + more_k, dv + more_v)
+                dk, dv = (None, None)
                 if "acc_" + name in env:
                     acc = env["acc_" + name]
-                    dk, dv = (dk + acc[0, :, cols], dv + acc[1, :, cols])
-                out[0, :, cols] = (dk * factor if name in last else dk).astype(out.dtype)
+                    dk, dv = (acc[0, :, cols], acc[1, :, cols])
+                for j in js:
+                    term_k, term_v = pair_terms(slot, j, i)
+                    dk = term_k if dk is None else dk + term_k
+                    dv = term_v if dv is None else dv + term_v
+                out[0, :, cols] = dk.astype(out.dtype)
                 out[1, :, cols] = dv.astype(out.dtype)
 
     key_frames([(slot, js) for slot, js in work if slot != FAR])
@@ -269,7 +270,6 @@
     for slot in slots:
         give("keys%d" % slot, keys[slot], cols)
     touched = [("q%d" % j, one) for j in used] + [("kv%d" % s, two) for s in slots]
-    carried = [name for name, _ in touched if name in sums]
     for name, spec in touched:
         if name in sums:
             give("acc_" + name, sums[name], spec)
@@ -289,7 +289,7 @@
     names += ["sum_q%d" % j for j in used]
     pairs = count * sum(len(js) for _, js in work)
     results = pl.pallas_call(
-        functools.partial(stage_kernel, work, names, carried, last, head_width**-0.5, group),
+        functools.partial(stage_kernel, work, names, head_width**-0.5, group),
         grid_spec=pltpu.PrefetchScalarGridSpec(
             num_scalar_prefetch=1,
             grid=(count // group,),
@@ -316,9 +316,9 @@
     for back in rest[:backs]:
         total = total + back[...].astype(F32)
     out_q[...] = (total * factor).astype(BF16)
-    for i, (out, scale) in enumerate(((out_k, factor), (out_v, 1.0))):
-        others = near[i].astype(F32) + far[i].astype(F32)
-        out[...] = (own_kv[i] * scale + others).astype(BF16)
+    sums = own_kv[...] + near[...].astype(F32) + far[...].astype(F32)
+    out_k[...] = sums[0].astype(BF16)
+    out_v[...] = sums[1].astype(BF16)
 
 
 def finish(first, count, head_width, full, parts, so_far):
@@ -388,12 +388,12 @@
     mask = window_mask.reshape(9)
     own_kv = pack(k, v)
     near_kv = lax.ppermute(own_kv, "tm", near_pairs)
-    far_kv = lax.ppermute(own_kv, "tm", far_pairs)
     make = lambda first, counts, source: prep(
         first, counts, width, (frames, rows), place, mask, source, g, o, lse
     )
     mine = make(0, CHUNKS[:1], q)
     theirs = {0: lax.ppermute(mine[0], "space", partner)}
+    far_kv = lax.ppermute(after(own_kv, mine[0]), "tm", far_pairs)
     mine += make(firsts[1], CHUNKS[1:], after(q, mine[0]))
     frames_kv = {HERE: own_kv, NEAR: near_kv, FAR: far_kv}
     last = len(CHUNKS) - 1

time: 140 us -> 137 us (0.979)
  Pallas kernels: 90 us -> 82.7 us
  starting transfers between devices: 26.5 us -> 30.6 us
    pallas_call x9, Pallas kernels: 77.9 us -> 70.6 us  [run_stage(): pl.pallas_call(functools.partial(stage_kernel, work, names, head_width **...]
    ppermute x9, starting transfers between devices: 12.1 us -> 17.8 us  [stage(): backs[c][name] = lax.ppermute(sums[c][name], axis, pairs)]
    ppermute x9, waiting for transfers between devices: 9.41 us -> 11.3 us  [stage(): backs[c][name] = lax.ppermute(sums[c][name], axis, pairs)]
    ppermute x1, waiting for transfers between devices: 1.49 us -> 0.01 us  [per_device(): theirs = {0: lax.ppermute(mine[0], 'space', partner)}]
  transfers between devices with their start and end apart: 19 -> 19, of which waited for: 5 -> 5; matrix products, arithmetic and copies ran while one was open for 0% -> 0% of each run, Pallas kernels for 63% -> 59%
where the time goes in v2:
time: 137 us; the launch traced here: 135 us
  Pallas kernels  82.7 us (60%)
  starting transfers between devices  30.6 us (22%)
  waiting for transfers between devices  20.9 us (15%)
    pallas_call x9, Pallas kernels, run_stage(): pl.pallas_call(functools.partial(stage_kernel, work, names, head_width **...  70.6 us
    ppermute x9, starting transfers between devices, stage(): backs[c][name] = lax.ppermute(sums[c][name], axis, pairs)  17.8 us
    ppermute x9, waiting for transfers between devices, stage(): backs[c][name] = lax.ppermute(sums[c][name], axis, pairs)  11.3 us
    ppermute x2, waiting for transfers between devices, per_device(): theirs[c] = lax.ppermute(mine[c], 'space', partner)  8.28 us
    pallas_call x2, Pallas kernels, prep(): pl.pallas_call(functools.partial(prep_kernel, counts, *sizes), grid_spec=...  6.23 us
    pallas_call x3, Pallas kernels, finish(): pl.pallas_call(functools.partial(finish_kernel, head_width ** (-0.5), len...  4.09 us
    ppermute x1, starting transfers between devices, per_device(): far_kv = lax.ppermute(after(own_kv, mine[0]), 'tm', far_pairs)  3.34 us
    ppermute x2, starting transfers between devices, send_back(): backs[c]['q2'] = lax.ppermute(total.astype(BF16), 'space', partner)  3.21 us
  transfers between devices with their start and end apart: 19, of which 5 were waited for; matrix products, arithmetic and copies ran while one was open for 0% of the time, Pallas kernels for 59%

profile of v2, /device:TPU:9, one launch (start us, length us, event | category | flops | bytes accessed | tf_op | source)
XLA Modules:
  0.0 135.3 jit_solution(11345246704212553027)
XLA Ops:
  0.7 1.8 %pack.1.refs_1_.refs_3_.refs_2_ = bf16[2,384,1536]{2,1,0:T(8,128)(2,1)S(1)} custom-call(bf16[384,1536]{1,0:T(8,128)(2,1)} %bitcast.26, bf16[384,1536]{1,0:T(8,128)(2,1)} %bitcast.27), custom_call_target="tpu_custom_call" | custom-call | bytes 4718592 | tf_op jit(solution)/shard_map/pack/pallas_call | solution.py:149
  2.4 0.7 collective-permute-start.2
  3.2 2.2 %prep.2.refs_0_.refs_1_ = bf16[800,512]{1,0:T(8,128)(2,1)S(1)} custom-call(s32[1]{0:T(128)} %bitcast.1.frame_ref, s32[1]{0:T(128)} %bitcast.2.row_ref, s32[9]{0:T(128)S(1)} %bitcast.15, bf16[384,1536]{1,0:T(8,128)(2,1)} %bitcast.20, bf16[384,1536]{1,0:T(8,128)(2,1)} %bitcast.22, bf16[384,1536]{1,0:T(8,128)(2,1)} %bitcast.24, f32[12,1,384]{2,1,0:T(1,128)S(1)} %bitcast.13), custom_call_target="tpu_custom_call" | custom-call | flops 393216 | bytes 1966080 | tf_op jit(solution)/shard_map/prep/pallas_call | solution.py:114
  5.4 1.3 collective-permute-start.1
  6.7 3.3 %collective-permute-start.4 = (bf16[2,384,1536]{2,1,0:T(8,128)(2,1)S(1)}, bf16[2,384,1536]{2,1,0:T(8,128)(2,1)}, u32[]{:S(2)}, u32[]{:S(2)}) collective-permute-start(bf16[2,384,1536]{2,1,0:T(8,128)(2,1)S(1)} %pack.1.refs_1_.refs_3_.refs_2_), channel_id=1, source_target_pairs={{0,0},{24,24},{8,16},{16,8},{1,1},{25,25},{9,17},{17,9},{2,2},{26,... | collective-permute-start | bytes 7077896 | tf_op jit(solution)/shard_map/ppermute | solution.py:396
  10.0 4.0 %prep.3 = (bf16[800,640]{1,0:T(8,128)(2,1)}, bf16[800,384]{1,0:T(8,128)(2,1)}) custom-call(s32[1]{0:T(128)} %bitcast.1.frame_ref, s32[1]{0:T(128)} %bitcast.2.row_ref, s32[9]{0:T(128)S(1)} %bitcast.16, bf16[384,1536]{1,0:T(8,128)(2,1)} %bitcast.21, bf16[384,1536]{1,0:T(8,128)(2,1)} %bitcast.23, bf16[384,1536]{1,0:T(8,128)(2,1)} %bitcast.25, ...), custom_call_target="tpu_custom_call" | custom-call | flops 786432 | bytes 3932160 | tf_op jit(solution)/shard_map/prep/pallas_call | solution.py:114
  14.1 0.3 collective-permute-start.6
  14.3 1.2 collective-permute-start
  15.5 0.0 collective-permute-done.2.refs_2_.refs_4_.refs_3_
  15.5 5.6 %pairs.9 = (f32[384,512]{1,0:T(8,128)S(1)}, f32[2,384,512]{2,1,0:T(8,128)S(1)}, f32[2,384,512]{2,1,0:T(8,128)S(1)}) custom-call(s32[1]{0:T(128)} %bitcast.far_ref, bf16[800,512]{1,0:T(8,128)(2,1)S(1)} %prep.2.refs_0_.refs_1_, bf16[2,384,1536]{2,1,0:T(8,128)(2,1)S(1)} %pack.1.refs_1_.refs_3_.refs_2_, ...), custom_call_target="tpu_custom_call" | custom-call | flops 9059696640 | bytes 3932160 | tf_op jit(solution)/shard_map/pairs/pallas_call | solution.py:291
  21.2 6.5 %pairs.10 = (f32[384,640]{1,0:T(8,128)S(1)}, f32[2,384,640]{2,1,0:T(8,128)S(1)}, f32[2,384,640]{2,1,0:T(8,128)S(1)}) custom-call(s32[1]{0:T(128)} %bitcast.far_ref, bf16[800,640]{1,0:T(8,128)(2,1)} %get-tuple-element.71.refs_0_.refs_1_, bf16[2,384,1536]{2,1,0:T(8,128)(2,1)S(1)} %pack.1.refs_1_.refs_3_.refs_2_, ...), custom_call_target="tpu_custom_call" | custom-call | flops 11324620800 | bytes 4915200 | tf_op jit(solution)/shard_map/pairs/pallas_call | solution.py:291
  27.7 0.0 collective-permute-done.1.refs_0_.refs_2_
  27.7 1.3 collective-permute-start.3
  29.0 5.8 %pairs.11 = (f32[384,512]{1,0:T(8,128)S(1)}, f32[2,384,512]{2,1,0:T(8,128)S(1)}, f32[2,384,512]{2,1,0:T(8,128)S(1)}) custom-call(s32[1]{0:T(128)} %bitcast.far_ref, bf16[800,512]{1,0:T(8,128)(2,1)} %collective-permute-done.1.refs_0_.refs_2_, bf16[2,384,1536]{2,1,0:T(8,128)(2,1)S(1)} %pack.1.refs_1_.refs_3_.refs_2_, ...), custom_call_target="tpu_custom_call" | custom-call | flops 9059696640 | bytes 3932160 | tf_op jit(solution)/shard_map/pairs/pallas_call | solution.py:291
  34.8 4.3 %pairs.12 = (f32[384,384]{1,0:T(8,128)S(1)}, f32[2,384,384]{2,1,0:T(8,128)S(1)}, f32[2,384,384]{2,1,0:T(8,128)S(1)}) custom-call(s32[1]{0:T(128)} %bitcast.far_ref, bf16[800,384]{1,0:T(8,128)(2,1)} %get-tuple-element.76.refs_0_.refs_1_, bf16[2,384,1536]{2,1,0:T(8,128)(2,1)S(1)} %pack.1.refs_1_.refs_3_.refs_2_, ...), custom_call_target="tpu_custom_call" | custom-call | flops 27179089920 | bytes 2949120 | tf_op jit(solution)/shard_map/pairs/pallas_call | solution.py:291
  39.1 8.3 %collective-permute-done.6.refs_0_.refs_2_ = bf16[800,640]{1,0:T(8,128)(2,1)} collective-permute-done((bf16[800,640]{1,0:T(8,128)(2,1)}, bf16[800,640]{1,0:T(8,128)(2,1)}, u32[]{:S(2)}, u32[]{:S(2)}) %collective-permute-start.6) | collective-permute-done | bytes 1024032 | tf_op jit(solution)/shard_map/ppermute | solution.py:461
  47.4 1.3 collective-permute-start.7
  48.7 0.0 collective-permute-done.3.refs_0_
  48.7 12.5 %pairs.13 = (bf16[384,512]{1,0:T(8,128)(2,1)S(1)}, f32[384,512]{1,0:T(8,128)S(1)}, f32[384,512]{1,0:T(8,128)S(1)}, f32[2,384,512]{2,1,0:T(8,128)S(1)}, bf16[2,38...) custom-call(s32[1]{0:T(128)} %bitcast.far_ref, bf16[800,512]{1,0:T(8,128)(2,1)S(1)} %collective-permute-done.3.refs_0_, ...), custom_call_target="tpu_custom_call" | custom-call | flops 22649241600 | bytes 3932160 | tf_op jit(solution)/shard_map/pairs/pallas_call | solution.py:291
  61.2 1.6 %collective-permute-start.8 = (bf16[384,512]{1,0:T(8,128)(2,1)S(1)}, bf16[384,512]{1,0:T(8,128)(2,1)S(1)}, u32[]{:S(2)}, u32[]{:S(2)}) collective-permute-start(bf16[384,512]{1,0:T(8,128)(2,1)S(1)} %get-tuple-element.99), channel_id=1, source_target_pairs={{2,0},{4,2},{6,4},{1,3},{3,5},{5,7},{0,1},{7,6},{10,8},{12,10},{14... | collective-permute-start | bytes 1179656 | tf_op jit(solution)/shard_map/ppermute | solution.py:437
  62.7 0.0 collective-permute-start.10
  62.7 0.0 collective-permute-done.refs_0_
  62.7 0.1 collective-permute-start.5
  62.9 6.7 %pairs.14 = (f32[384,640]{1,0:T(8,128)S(1)}, f32[2,384,640]{2,1,0:T(8,128)S(1)}, f32[2,384,640]{2,1,0:T(8,128)S(1)}) custom-call(s32[1]{0:T(128)} %bitcast.far_ref, bf16[800,640]{1,0:T(8,128)(2,1)} %collective-permute-done.6.refs_0_.refs_2_, bf16[2,384,1536]{2,1,0:T(8,128)(2,1)S(1)} %pack.1.refs_1_.refs_3_.refs_2_, ...), custom_call_target="tpu_custom_call" | custom-call | flops 5662310400 | bytes 4915200 | tf_op jit(solution)/shard_map/pairs/pallas_call | solution.py:291
  69.6 0.9 collective-permute-done.7.refs_0_
  70.5 15.0 %pairs.15 = (bf16[384,640]{1,0:T(8,128)(2,1)S(1)}, f32[384,640]{1,0:T(8,128)S(1)}, f32[384,640]{1,0:T(8,128)S(1)}, f32[2,384,640]{2,1,0:T(8,128)S(1)}, bf16[2,38...) custom-call(s32[1]{0:T(128)} %bitcast.far_ref, ...), custom_call_target="tpu_custom_call", output_to_operand_aliasing={{5}: (11, {})} | custom-call | flops 28311552000 | bytes 4915200 | tf_op jit(solution)/shard_map/pairs/pallas_call | solution.py:291
  85.5 2.4 %collective-permute-start.15 = (bf16[384,640]{1,0:T(8,128)(2,1)S(1)}, bf16[384,640]{1,0:T(8,128)(2,1)S(1)}, u32[]{:S(2)}, u32[]{:S(2)}) collective-permute-start(bf16[384,640]{1,0:T(8,128)(2,1)S(1)} %get-tuple-element.118), channel_id=1, source_target_pairs={{2,0},{4,2},{6,4},{1,3},{3,5},{5,7},{0,1},{7,6},{10,8},{12,10},{14... | collective-permute-start | bytes 1474568 | tf_op jit(solution)/shard_map/ppermute | solution.py:437
  87.9 6.9 %collective-permute-start.14 = (bf16[2,384,1152]{2,1,0:T(8,128)(2,1)S(1)}, bf16[2,384,1152]{2,1,0:T(8,128)(2,1)S(1)}, u32[]{:S(2)}, u32[]{:S(2)}) collective-permute-start(bf16[2,384,1152]{2,1,0:T(8,128)(2,1)S(1)} %get-tuple-element.111), channel_id=1, source_target_pairs={{0,0},{24,24},{8,16},{16,8},{1,1},{25,25},{9,17},{17,9},{2,2},{26,... | collective-permute-start | bytes 5308424 | tf_op jit(solution)/shard_map/ppermute | solution.py:437
  94.8 0.0 collective-permute-done.8
  94.8 0.1 add_convert_fusion.1
  94.9 0.6 collective-permute-start.9
  95.5 6.4 %pairs.16 = (bf16[384,384]{1,0:T(8,128)(2,1)S(1)}, f32[2,384,384]{2,1,0:T(8,128)S(1)}, f32[2,384,384]{2,1,0:T(8,128)S(1)}, f32[2,384,384]{2,1,0:T(8,128)S(1)}) custom-call(s32[1]{0:T(128)} %bitcast.far_ref, bf16[800,384]{1,0:T(8,128)(2,1)} %collective-permute-done.refs_0_, bf16[2,384,1536]{2,1,0:T(8,128)(2,1)S(1)} %pack.1.refs_1_.refs_3_.refs_2_, ...), custom_call_target="tpu_custom_call" | custom-call | flops 20384317440 | bytes 2949120 | tf_op jit(solution)/shard_map/pairs/pallas_call | solution.py:291
  102.0 3.2 %collective-permute-done.15 = bf16[384,640]{1,0:T(8,128)(2,1)S(1)} collective-permute-done((bf16[384,640]{1,0:T(8,128)(2,1)S(1)}, bf16[384,640]{1,0:T(8,128)(2,1)S(1)}, u32[]{:S(2)}, u32[]{:S(2)}) %collective-permute-start.15) | collective-permute-done | bytes 491552 | tf_op jit(solution)/shard_map/ppermute | solution.py:437
  105.1 0.4 collective-permute-start.13
  105.5 0.1 add_convert_fusion
  105.7 0.0 collective-permute-done.5.refs_0_
  105.7 2.6 %collective-permute-start.16 = (bf16[384,640]{1,0:T(8,128)(2,1)S(1)}, bf16[384,640]{1,0:T(8,128)(2,1)S(1)}, u32[]{:S(2)}, u32[]{:S(2)}) collective-permute-start(bf16[384,640]{1,0:T(8,128)(2,1)S(1)} %add_convert_fusion), channel_id=1, source_target_pairs={{0,1},{1,0},{2,3},{3,2},{4,5},{5,4},{6,7},{7,6},{8,9},{9,8},{10,11... | collective-permute-start | bytes 1474568 | tf_op jit(solution)/shard_map/ppermute | solution.py:447
  108.3 7.8 %pairs.17 = (bf16[384,384]{1,0:T(8,128)(2,1)S(1)}, f32[384,384]{1,0:T(8,128)S(1)}, f32[2,384,384]{2,1,0:T(8,128)S(1)}, bf16[2,384,384]{2,1,0:T(8,128)(2,1)S(1)}, bf16[2,384,384]{2,1,0:T(8,128)(2,1)S(1)}) custom-call(s32[1]{0:T(128)} %bitcast.far_ref, bf16[800,384]{1,0:T(8,128)(2,1)S(1)} %collective-permute-done.5.refs_0_, ...), custom_call_target="tpu_custom_call" | custom-call | flops 13589544960 | bytes 2949120 | tf_op jit(solution)/shard_map/pairs/pallas_call | solution.py:291
  116.1 0.1 collective-permute-start.11
  116.2 3.3 %collective-permute-start.12 = (bf16[2,384,384]{2,1,0:T(8,128)(2,1)S(1)}, bf16[2,384,384]{2,1,0:T(8,128)(2,1)S(1)}, u32[]{:S(2)}, u32[]{:S(2)}) collective-permute-start(bf16[2,384,384]{2,1,0:T(8,128)(2,1)S(1)} %get-tuple-element.108), channel_id=1, source_target_pairs={{0,0},{24,24},{8,16},{16,8},{1,1},{25,25},{9,17},{17,9},{2,2},{26,... | collective-permute-start | bytes 1769480 | tf_op jit(solution)/shard_map/ppermute | solution.py:437
  119.5 0.4 collective-permute-done.16.rest_0_
  119.9 1.3 collective-permute-start.17
  121.2 0.0 collective-permute-done.14.far
  121.2 1.9 %collective-permute-start.18 = (bf16[384,384]{1,0:T(8,128)(2,1)S(1)}, bf16[384,384]{1,0:T(8,128)(2,1)S(1)}, u32[]{:S(2)}, u32[]{:S(2)}) collective-permute-start(bf16[384,384]{1,0:T(8,128)(2,1)S(1)} %get-tuple-element.125), channel_id=1, source_target_pairs={{0,0},{7,7},{1,2},{2,1},{3,4},{4,3},{5,6},{6,5},{8,8},{15,15},{9,1... | collective-permute-start | bytes 884744 | tf_op jit(solution)/shard_map/ppermute | solution.py:437
  123.1 1.3 finish.3
  124.4 1.7 %finish.4 = (bf16[384,1536]{1,0:T(8,128)(2,1)}, bf16[384,1536]{1,0:T(8,128)(2,1)}, bf16[384,1536]{1,0:T(8,128)(2,1)}) custom-call(f32[2,384,640]{2,1,0:T(8,128)S(1)} %get-tuple-element.94.own_kv, bf16[2,384,640]{2,1,0:T(8,128)(2,1)S(1)} %collective-permute-done.13.near, ...), custom_call_target="tpu_custom_call", output_to_operand_aliasing={{0}: (5, {}), {1}: (6, {}), {2}: (7, {})} | custom-call | flops 1966080 | bytes 7372800 | tf_op jit(solution)/shard_map/finish/pallas_call | solution.py:340
  126.1 8.1 %collective-permute-done.17.rest_0_ = bf16[384,384]{1,0:T(8,128)(2,1)S(1)} collective-permute-done((bf16[384,384]{1,0:T(8,128)(2,1)S(1)}, bf16[384,384]{1,0:T(8,128)(2,1)S(1)}, u32[]{:S(2)}, u32[]{:S(2)}) %collective-permute-start.17) | collective-permute-done | bytes 294944 | tf_op jit(solution)/shard_map/ppermute | solution.py:437
  134.2 1.1 finish.5
  (11 shorter events, 0.0 us)
Async XLA Ops:
  0.6 2.6 %copy-start = (f32[1,1,12,384]{3,1,2,0:T(1,128)S(1)}, f32[1,1,12,384]{3,1,2,0:T(1,128)}, u32[]{:S(2)}) copy-start(f32[1,1,12,384]{3,1,2,0:T(1,128)} %param.12) | copy-start | bytes 55300
  0.6 2.5 %copy-start.1 = (s32[1,1,9]{2,1,0:T(1,128)S(1)}, s32[1,1,9]{2,1,0:T(1,128)}, u32[]{:S(2)}) copy-start(s32[1,1,9]{2,1,0:T(1,128)} %param.13) | copy-start | bytes 112
  2.4 13.1 %collective-permute-start.2 = (bf16[2,384,1536]{2,1,0:T(8,128)(2,1)S(1)}, bf16[2,384,1536]{2,1,0:T(8,128)(2,1)}, u32[]{:S(2)}, u32[]{:S(2)}) collective-permute-start(bf16[2,384,1536]{2,1,0:T(8,128)(2,1)S(1)} %pack.1.refs_1_.refs_3_.refs_2_), channel_id=1, source_target_pairs={{0,8},{8,0},{16,24},{24,16},{1,9},{9,1},{17,25},{25,17},{2,10},{10... | collective-permute-start | bytes 7077896 | tf_op jit(solution)/shard_map/ppermute | solution.py:390
  5.4 22.2 %collective-permute-start.1 = (bf16[800,512]{1,0:T(8,128)(2,1)S(1)}, bf16[800,512]{1,0:T(8,128)(2,1)}, u32[]{:S(2)}, u32[]{:S(2)}) collective-permute-start(bf16[800,512]{1,0:T(8,128)(2,1)S(1)} %prep.2.refs_0_.refs_1_), channel_id=1, source_target_pairs={{0,1},{1,0},{2,3},{3,2},{4,5},{5,4},{6,7},{7,6},{8,9},{9,8},{10,11... | collective-permute-start | bytes 2457608 | tf_op jit(solution)/shard_map/ppermute | solution.py:395
  6.7 42.0 %collective-permute-start.4 = (bf16[2,384,1536]{2,1,0:T(8,128)(2,1)S(1)}, bf16[2,384,1536]{2,1,0:T(8,128)(2,1)}, u32[]{:S(2)}, u32[]{:S(2)}) collective-permute-start(bf16[2,384,1536]{2,1,0:T(8,128)(2,1)S(1)} %pack.1.refs_1_.refs_3_.refs_2_), channel_id=1, source_target_pairs={{0,0},{24,24},{8,16},{16,8},{1,1},{25,25},{9,17},{17,9},{2,2},{26,... | collective-permute-start | bytes 7077896 | tf_op jit(solution)/shard_map/ppermute | solution.py:396
  14.1 33.3 %collective-permute-start.6 = (bf16[800,640]{1,0:T(8,128)(2,1)}, bf16[800,640]{1,0:T(8,128)(2,1)}, u32[]{:S(2)}, u32[]{:S(2)}) collective-permute-start(bf16[800,640]{1,0:T(8,128)(2,1)} %get-tuple-element.71.refs_0_.refs_1_), channel_id=1, source_target_pairs={{0,1},{1,0},{2,3},{3,2},{4,5},{5,4},{6,7},{7,6},{8,9},{9,8},{10,11... | collective-permute-start | bytes 3072008 | tf_op jit(solution)/shard_map/ppermute | solution.py:461
  14.3 48.4 %collective-permute-start = (bf16[800,384]{1,0:T(8,128)(2,1)}, bf16[800,384]{1,0:T(8,128)(2,1)}, u32[]{:S(2)}, u32[]{:S(2)}) collective-permute-start(bf16[800,384]{1,0:T(8,128)(2,1)} %get-tuple-element.76.refs_0_.refs_1_), channel_id=1, source_target_pairs={{0,1},{1,0},{2,3},{3,2},{4,5},{5,4},{6,7},{7,6},{8,9},{9,8},{10,11... | collective-permute-start | bytes 1843208 | tf_op jit(solution)/shard_map/ppermute | solution.py:461
  27.7 21.0 %collective-permute-start.3 = (bf16[800,512]{1,0:T(8,128)(2,1)}, bf16[800,512]{1,0:T(8,128)(2,1)S(1)}, u32[]{:S(2)}, u32[]{:S(2)}) collective-permute-start(bf16[800,512]{1,0:T(8,128)(2,1)} %collective-permute-done.1.refs_0_.refs_2_), channel_id=1, source_target_pairs={{0,2},{2,4},{4,6},{6,0},{1,7},{3,1},{5,3},{7,5},{8,10},{10,12},{12... | collective-permute-start | bytes 2457608 | tf_op jit(solution)/shard_map/ppermute | solution.py:443
  47.4 23.1 %collective-permute-start.7 = (bf16[800,640]{1,0:T(8,128)(2,1)}, bf16[800,640]{1,0:T(8,128)(2,1)S(1)}, u32[]{:S(2)}, u32[]{:S(2)}) collective-permute-start(bf16[800,640]{1,0:T(8,128)(2,1)} %collective-permute-done.6.refs_0_.refs_2_), channel_id=1, source_target_pairs={{0,2},{2,4},{4,6},{6,0},{1,7},{3,1},{5,3},{7,5},{8,10},{10,12},{12... | collective-permute-start | bytes 3072008 | tf_op jit(solution)/shard_map/ppermute | solution.py:443
  61.2 33.6 %collective-permute-start.8 = (bf16[384,512]{1,0:T(8,128)(2,1)S(1)}, bf16[384,512]{1,0:T(8,128)(2,1)S(1)}, u32[]{:S(2)}, u32[]{:S(2)}) collective-permute-start(bf16[384,512]{1,0:T(8,128)(2,1)S(1)} %get-tuple-element.99), channel_id=1, source_target_pairs={{2,0},{4,2},{6,4},{1,3},{3,5},{5,7},{0,1},{7,6},{10,8},{12,10},{14... | collective-permute-start | bytes 1179656 | tf_op jit(solution)/shard_map/ppermute | solution.py:437
  62.7 45.6 %collective-permute-start.10 = (bf16[2,384,512]{2,1,0:T(8,128)(2,1)S(1)}, bf16[2,384,512]{2,1,0:T(8,128)(2,1)S(1)}, u32[]{:S(2)}, u32[]{:S(2)}) collective-permute-start(bf16[2,384,512]{2,1,0:T(8,128)(2,1)S(1)} %get-tuple-element.101), channel_id=1, source_target_pairs={{0,8},{8,0},{16,24},{24,16},{1,9},{9,1},{17,25},{25,17},{2,10},{10... | collective-permute-start | bytes 2359304 | tf_op jit(solution)/shard_map/ppermute | solution.py:437
  62.7 42.9 %collective-permute-start.5 = (bf16[800,384]{1,0:T(8,128)(2,1)}, bf16[800,384]{1,0:T(8,128)(2,1)S(1)}, u32[]{:S(2)}, u32[]{:S(2)}) collective-permute-start(bf16[800,384]{1,0:T(8,128)(2,1)} %collective-permute-done.refs_0_), channel_id=1, source_target_pairs={{0,2},{2,4},{4,6},{6,0},{1,7},{3,1},{5,3},{7,5},{8,10},{10,12},{12... | collective-permute-start | bytes 1843208 | tf_op jit(solution)/shard_map/ppermute | solution.py:443
  85.5 19.6 %collective-permute-start.15 = (bf16[384,640]{1,0:T(8,128)(2,1)S(1)}, bf16[384,640]{1,0:T(8,128)(2,1)S(1)}, u32[]{:S(2)}, u32[]{:S(2)}) collective-permute-start(bf16[384,640]{1,0:T(8,128)(2,1)S(1)} %get-tuple-element.118), channel_id=1, source_target_pairs={{2,0},{4,2},{6,4},{1,3},{3,5},{5,7},{0,1},{7,6},{10,8},{12,10},{14... | collective-permute-start | bytes 1474568 | tf_op jit(solution)/shard_map/ppermute | solution.py:437
  87.9 33.3 %collective-permute-start.14 = (bf16[2,384,1152]{2,1,0:T(8,128)(2,1)S(1)}, bf16[2,384,1152]{2,1,0:T(8,128)(2,1)S(1)}, u32[]{:S(2)}, u32[]{:S(2)}) collective-permute-start(bf16[2,384,1152]{2,1,0:T(8,128)(2,1)S(1)} %get-tuple-element.111), channel_id=1, source_target_pairs={{0,0},{24,24},{8,16},{16,8},{1,1},{25,25},{9,17},{17,9},{2,2},{26,... | collective-permute-start | bytes 5308424 | tf_op jit(solution)/shard_map/ppermute | solution.py:437
  94.9 13.4 %collective-permute-start.9 = (bf16[384,512]{1,0:T(8,128)(2,1)S(1)}, bf16[384,512]{1,0:T(8,128)(2,1)S(1)}, u32[]{:S(2)}, u32[]{:S(2)}) collective-permute-start(bf16[384,512]{1,0:T(8,128)(2,1)S(1)} %add_convert_fusion.1), channel_id=1, source_target_pairs={{0,1},{1,0},{2,3},{3,2},{4,5},{5,4},{6,7},{7,6},{8,9},{9,8},{10,11... | collective-permute-start | bytes 1179656 | tf_op jit(solution)/shard_map/ppermute | solution.py:447
  105.1 19.3 %collective-permute-start.13 = (bf16[2,384,640]{2,1,0:T(8,128)(2,1)S(1)}, bf16[2,384,640]{2,1,0:T(8,128)(2,1)S(1)}, u32[]{:S(2)}, u32[]{:S(2)}) collective-permute-start(bf16[2,384,640]{2,1,0:T(8,128)(2,1)S(1)} %get-tuple-element.110), channel_id=1, source_target_pairs={{0,8},{8,0},{16,24},{24,16},{1,9},{9,1},{17,25},{25,17},{2,10},{10... | collective-permute-start | bytes 2949128 | tf_op jit(solution)/shard_map/ppermute | solution.py:437
  105.7 14.2 %collective-permute-start.16 = (bf16[384,640]{1,0:T(8,128)(2,1)S(1)}, bf16[384,640]{1,0:T(8,128)(2,1)S(1)}, u32[]{:S(2)}, u32[]{:S(2)}) collective-permute-start(bf16[384,640]{1,0:T(8,128)(2,1)S(1)} %add_convert_fusion), channel_id=1, source_target_pairs={{0,1},{1,0},{2,3},{3,2},{4,5},{5,4},{6,7},{7,6},{8,9},{9,8},{10,11... | collective-permute-start | bytes 1474568 | tf_op jit(solution)/shard_map/ppermute | solution.py:447
  116.1 18.1 %collective-permute-start.11 = (bf16[2,384,384]{2,1,0:T(8,128)(2,1)S(1)}, bf16[2,384,384]{2,1,0:T(8,128)(2,1)S(1)}, u32[]{:S(2)}, u32[]{:S(2)}) collective-permute-start(bf16[2,384,384]{2,1,0:T(8,128)(2,1)S(1)} %get-tuple-element.107), channel_id=1, source_target_pairs={{0,8},{8,0},{16,24},{24,16},{1,9},{9,1},{17,25},{25,17},{2,10},{10... | collective-permute-start | bytes 1769480 | tf_op jit(solution)/shard_map/ppermute | solution.py:437
  116.2 18.0 %collective-permute-start.12 = (bf16[2,384,384]{2,1,0:T(8,128)(2,1)S(1)}, bf16[2,384,384]{2,1,0:T(8,128)(2,1)S(1)}, u32[]{:S(2)}, u32[]{:S(2)}) collective-permute-start(bf16[2,384,384]{2,1,0:T(8,128)(2,1)S(1)} %get-tuple-element.108), channel_id=1, source_target_pairs={{0,0},{24,24},{8,16},{16,8},{1,1},{25,25},{9,17},{17,9},{2,2},{26,... | collective-permute-start | bytes 1769480 | tf_op jit(solution)/shard_map/ppermute | solution.py:437
  119.9 14.3 %collective-permute-start.17 = (bf16[384,384]{1,0:T(8,128)(2,1)S(1)}, bf16[384,384]{1,0:T(8,128)(2,1)S(1)}, u32[]{:S(2)}, u32[]{:S(2)}) collective-permute-start(bf16[384,384]{1,0:T(8,128)(2,1)S(1)} %get-tuple-element.124), channel_id=1, source_target_pairs={{0,1},{1,0},{2,3},{3,2},{4,5},{5,4},{6,7},{7,6},{8,9},{9,8},{10,11... | collective-permute-start | bytes 884744 | tf_op jit(solution)/shard_map/ppermute | solution.py:437
  121.2 13.0 %collective-permute-start.18 = (bf16[384,384]{1,0:T(8,128)(2,1)S(1)}, bf16[384,384]{1,0:T(8,128)(2,1)S(1)}, u32[]{:S(2)}, u32[]{:S(2)}) collective-permute-start(bf16[384,384]{1,0:T(8,128)(2,1)S(1)} %get-tuple-element.125), channel_id=1, source_target_pairs={{0,0},{7,7},{1,2},{2,1},{3,4},{4,3},{5,6},{6,5},{8,8},{15,15},{9,1... | collective-permute-start | bytes 884744 | tf_op jit(solution)/shard_map/ppermute | solution.py:437

commit v3 on v2

--- a/solution.py
+++ b/solution.py
@@ -26,10 +26,12 @@
     STAGES[1] + ((FAR, (PARTNER,)),),
     ((HERE, (OUTER,)), (NEAR, (OUTER,)), (FAR, (OWN, OUTER))),
 )
-ORDER = (('stage', 0, 0), ('stage', 1, 0), ('hand', 0), ('stage', 0, 1), ('stage', 2, 0), ('hand', 1), ('stage', 0, 2), ('hand', 2), ('stage', 1, 1), ('back', 0), ('stage', 1, 2), ('stage', 2, 1), ('back', 1), ('stage', 2, 2, (0, 'q2'), (0, 'kv1')), ('finish', 0), ('finish', 1), ('finish', 2))
+DIRECT = 2
+ORDER = (('stage', 0, 0), ('stage', 1, 0), ('hand', 0), ('stage', 0, 1), ('stage', 2, 0), ('hand', 1), ('stage', 0, 2), ('hand', 2), ('stage', 1, 1), ('back', 0), ('stage', 1, 2), ('stage', 2, 1), ('send', 1, 'kv2'), ('back', 1), ('stage', 2, 2, (0, 'q2'), (0, 'kv1')), ('finish', 0), ('finish', 1), ('finish', 2))
 JOINED = ('kv2',)
 WEIGHTS = ((60, 60, 60), (60, 30, 60), (240, 120, 60))
-EXTRA = 32
+EXTRA = 16
+TERMS = 2
 VMEM_LIMIT = 20 * 1024 * 1024
 GROUP = 1
 
@@ -38,9 +40,9 @@
     return lax.dot_general(a, b, (dims, ((), ())), preferred_element_type=F32)
 
 
-def three_terms(row):
+def split_terms(row):
     terms = []
-    for _ in range(3):
+    for _ in range(TERMS):
         term = row.astype(BF16).astype(F32)
         terms.append(term)
         row = row - term
@@ -94,7 +96,7 @@
             delta = dot(ones, high, ((1,), (1,))) + dot(ones, low, ((1,), (1,)))
             lines = []
             for line in (lse_ref[head] * LOG2E, delta[0:1, :]):
-                for term in three_terms(line):
+                for term in split_terms(line):
                     lines += fold(term)
             lines.append(flags)
             lines.append(jnp.zeros((EXTRA - len(lines), width), F32))
@@ -162,13 +164,14 @@
     extra = message[2 * tile : 2 * tile + EXTRA, :].astype(F32)
     parts = tile // 128
     rows = []
-    for base in (0, 3 * parts):
+    for base in (0, TERMS * parts):
         pieces = []
         for p in range(parts):
-            a, b, c = (extra[base + i * parts + p : base + i * parts + p + 1] for i in range(3))
-            pieces.append(a + b + c)
+            first = base + p
+            terms = [extra[first + i * parts : first + i * parts + 1] for i in range(TERMS)]
+            pieces.append(sum(terms[1:], terms[0]))
         rows.append(jnp.concatenate(pieces, axis=1))
-    return (rows[0], rows[1], extra[6 * parts : 6 * parts + 1])
+    return (rows[0], rows[1], extra[2 * TERMS * parts : 2 * TERMS * parts + 1])
 
 
 def stage_kernel(work, names, factor, group, far_ref, *refs):
@@ -405,7 +408,7 @@
 
     def stage(c, step, *awaited):
         messages = {OUTER: outers.get(c), OWN: mine[c], PARTNER: theirs.get(c)}
-        stages = LATER_STAGES if c == last else STAGES
+        stages = LATER_STAGES if c >= DIRECT else STAGES
         work = stages[step]
         needed = {j: messages[j] for _, js in work for j in js}
         first_used = min(needed)
@@ -413,7 +416,7 @@
         needed[first_used] = after(needed[first_used], *done[-1:], *arrived)
         later = {j for other in stages[step + 1 :] for _, js in other for j in js}
         slots = {slot for other in stages[step + 1 :] for slot, _ in other}
-        straight = (OUTER, PARTNER) if c == last else (OUTER,)
+        straight = (OUTER, PARTNER) if c >= DIRECT else (OUTER,)
         final = {"q%d" % j for j in straight if j not in later}
         final |= {"kv%d" % slot for slot in (NEAR, FAR) if slot not in slots}
         joined = {}
@@ -425,20 +428,26 @@
         )
         done.append(sums[c]["kv0"])
         for name, axis, pairs in (
-            ("q0", "space", owners if c == last else homeward),
+            ("q0", "space", owners if c >= DIRECT else homeward),
             ("q2", "space", partner),
             ("kv1", "tm", near_pairs),
             ("kv2", "tm", far_pairs),
         ):
             if name not in final or name not in sums[c] or name in backs[c]:
                 continue
-            if name in joined and c + 1 < last:
+            if name in joined and (c + 1 < last or ("send", c, name) in ORDER):
                 continue
             backs[c][name] = lax.ppermute(sums[c][name], axis, pairs)
             if name in joined:
                 for earlier in range(c):
                     backs[earlier][name] = backs[c][name]
 
+    def send_joined(c, name):
+        axis_pairs = near_pairs if name == "kv1" else far_pairs
+        joined = lax.ppermute(after(sums[c][name], *done[-1:]), "tm", axis_pairs)
+        for earlier in range(c + 1):
+            backs[earlier][name] = joined
+
     def hand_on(c):
         outers[c] = lax.ppermute(after(theirs[c], *done[-1:]), "space", onward)
 
@@ -449,7 +458,7 @@
     def complete(c, so_far):
         back = backs[c]
         own = after(sums[c]["q1"], *done[-1:])
-        from_others = [back["q2"]] + ([back["q0"]] if c == last else [])
+        from_others = [back["q2"]] + ([back["q0"]] if c >= DIRECT else [])
         so_far = finish(
             firsts[c], CHUNKS[c], width, full,
             (sums[c]["kv0"], back["kv1"], back["kv2"], own, *from_others), so_far,
@@ -466,6 +475,8 @@
             hand_on(c)
         elif kind == "back":
             send_back(c)
+        elif kind == "send":
+            send_joined(c, *rest)
         else:
             out = complete(c, out)
     return tuple(a.reshape(queries.shape) for a in out)

time: 137 us -> 135 us (0.985)
  waiting for transfers between devices: 20.9 us -> 17.6 us
  starting transfers between devices: 30.6 us -> 32.8 us
    ppermute x0 -> x1, starting transfers between devices: none -> 7.54 us  [send_joined(): joined = lax.ppermute(after(sums[c][name], *done[-1:]), 'tm', axis_pairs)]
    ppermute x9 -> x8, starting transfers between devices: 17.8 us -> 12.9 us  [stage(): backs[c][name] = lax.ppermute(sums[c][name], axis, pairs)]
    ppermute x9 -> x8, waiting for transfers between devices: 11.3 us -> 7.98 us  [stage(): backs[c][name] = lax.ppermute(sums[c][name], axis, pairs)]
    ppermute x0 -> x1, waiting for transfers between devices: none -> 1.45 us  [send_joined(): joined = lax.ppermute(after(sums[c][name], *done[-1:]), 'tm', axis_pairs)]
  transfers between devices with their start and end apart: 19 -> 19, of which waited for: 5 -> 7; matrix products, arithmetic and copies ran while one was open for 0% -> 0% of each run, Pallas kernels for 59% -> 59%
where the time goes in v3:
time: 135 us; the launch traced here: 134 us
  Pallas kernels  82.5 us (61%)
  starting transfers between devices  32.8 us (24%)
  waiting for transfers between devices  17.6 us (13%)
    pallas_call x9, Pallas kernels, run_stage(): pl.pallas_call(functools.partial(stage_kernel, work, names, head_width **...  70.5 us
    ppermute x8, starting transfers between devices, stage(): backs[c][name] = lax.ppermute(sums[c][name], axis, pairs)  12.9 us
    ppermute x8, waiting for transfers between devices, stage(): backs[c][name] = lax.ppermute(sums[c][name], axis, pairs)  7.98 us
    ppermute x2, waiting for transfers between devices, per_device(): theirs[c] = lax.ppermute(mine[c], 'space', partner)  7.56 us
    ppermute x1, starting transfers between devices, send_joined(): joined = lax.ppermute(after(sums[c][name], *done[-1:]), 'tm', axis_pairs)  7.54 us
    pallas_call x2, Pallas kernels, prep(): pl.pallas_call(functools.partial(prep_kernel, counts, *sizes), grid_spec=...  6.22 us
    pallas_call x3, Pallas kernels, finish(): pl.pallas_call(functools.partial(finish_kernel, head_width ** (-0.5), len...  4.03 us
    ppermute x1, starting transfers between devices, per_device(): far_kv = lax.ppermute(after(own_kv, mine[0]), 'tm', far_pairs)  3.34 us
  transfers between devices with their start and end apart: 19, of which 7 were waited for; matrix products, arithmetic and copies ran while one was open for 0% of the time, Pallas kernels for 59%

profile of v3, /device:TPU:9, one launch (start us, length us, event | category | flops | bytes accessed | tf_op | source)
XLA Modules:
  0.0 134.0 jit_solution(11200351772571384402)
XLA Ops:
  0.7 1.8 %pack.1.refs_1_.refs_3_.refs_2_ = bf16[2,384,1536]{2,1,0:T(8,128)(2,1)S(1)} custom-call(bf16[384,1536]{1,0:T(8,128)(2,1)} %bitcast.26, bf16[384,1536]{1,0:T(8,128)(2,1)} %bitcast.27), custom_call_target="tpu_custom_call" | custom-call | bytes 4718592 | tf_op jit(solution)/shard_map/pack/pallas_call | solution.py:151
  2.4 0.7 collective-permute-start.2
  3.2 2.2 %prep.2.refs_0_.refs_1_ = bf16[784,512]{1,0:T(8,128)(2,1)S(1)} custom-call(s32[1]{0:T(128)} %bitcast.1.frame_ref, s32[1]{0:T(128)} %bitcast.2.row_ref, s32[9]{0:T(128)S(1)} %bitcast.15, bf16[384,1536]{1,0:T(8,128)(2,1)} %bitcast.20, bf16[384,1536]{1,0:T(8,128)(2,1)} %bitcast.22, bf16[384,1536]{1,0:T(8,128)(2,1)} %bitcast.24, f32[12,1,384]{2,1,0:T(1,128)S(1)} %bitcast.13), custom_call_target="tpu_custom_call" | custom-call | flops 393216 | bytes 1966080 | tf_op jit(solution)/shard_map/prep/pallas_call | solution.py:116
  5.4 1.3 collective-permute-start.1
  6.7 3.3 %collective-permute-start.4 = (bf16[2,384,1536]{2,1,0:T(8,128)(2,1)S(1)}, bf16[2,384,1536]{2,1,0:T(8,128)(2,1)}, u32[]{:S(2)}, u32[]{:S(2)}) collective-permute-start(bf16[2,384,1536]{2,1,0:T(8,128)(2,1)S(1)} %pack.1.refs_1_.refs_3_.refs_2_), channel_id=1, source_target_pairs={{0,0},{24,24},{8,16},{16,8},{1,1},{25,25},{9,17},{17,9},{2,2},{26,... | collective-permute-start | bytes 7077896 | tf_op jit(solution)/shard_map/ppermute | solution.py:399
  10.0 4.0 %prep.3 = (bf16[784,640]{1,0:T(8,128)(2,1)}, bf16[784,384]{1,0:T(8,128)(2,1)}) custom-call(s32[1]{0:T(128)} %bitcast.1.frame_ref, s32[1]{0:T(128)} %bitcast.2.row_ref, s32[9]{0:T(128)S(1)} %bitcast.16, bf16[384,1536]{1,0:T(8,128)(2,1)} %bitcast.21, bf16[384,1536]{1,0:T(8,128)(2,1)} %bitcast.23, bf16[384,1536]{1,0:T(8,128)(2,1)} %bitcast.25, ...), custom_call_target="tpu_custom_call" | custom-call | flops 786432 | bytes 3932160 | tf_op jit(solution)/shard_map/prep/pallas_call | solution.py:116
  14.0 0.3 collective-permute-start.6
  14.3 1.2 collective-permute-start
  15.5 0.0 collective-permute-done.2.refs_2_.refs_4_.refs_3_
  15.5 5.6 %pairs.9 = (f32[384,512]{1,0:T(8,128)S(1)}, f32[2,384,512]{2,1,0:T(8,128)S(1)}, f32[2,384,512]{2,1,0:T(8,128)S(1)}) custom-call(s32[1]{0:T(128)} %bitcast.far_ref, bf16[784,512]{1,0:T(8,128)(2,1)S(1)} %prep.2.refs_0_.refs_1_, bf16[2,384,1536]{2,1,0:T(8,128)(2,1)S(1)} %pack.1.refs_1_.refs_3_.refs_2_, ...), custom_call_target="tpu_custom_call" | custom-call | flops 9059696640 | bytes 3932160 | tf_op jit(solution)/shard_map/pairs/pallas_call | solution.py:294
  21.1 6.5 %pairs.10 = (f32[384,640]{1,0:T(8,128)S(1)}, f32[2,384,640]{2,1,0:T(8,128)S(1)}, f32[2,384,640]{2,1,0:T(8,128)S(1)}) custom-call(s32[1]{0:T(128)} %bitcast.far_ref, bf16[784,640]{1,0:T(8,128)(2,1)} %get-tuple-element.72.refs_0_.refs_1_, bf16[2,384,1536]{2,1,0:T(8,128)(2,1)S(1)} %pack.1.refs_1_.refs_3_.refs_2_, ...), custom_call_target="tpu_custom_call" | custom-call | flops 11324620800 | bytes 4915200 | tf_op jit(solution)/shard_map/pairs/pallas_call | solution.py:294
  27.6 1.3 collective-permute-start.3
  29.0 5.8 %pairs.11 = (f32[384,512]{1,0:T(8,128)S(1)}, f32[2,384,512]{2,1,0:T(8,128)S(1)}, f32[2,384,512]{2,1,0:T(8,128)S(1)}) custom-call(s32[1]{0:T(128)} %bitcast.far_ref, bf16[784,512]{1,0:T(8,128)(2,1)} %collective-permute-done.1.refs_0_.refs_2_, bf16[2,384,1536]{2,1,0:T(8,128)(2,1)S(1)} %pack.1.refs_1_.refs_3_.refs_2_, ...), custom_call_target="tpu_custom_call" | custom-call | flops 9059696640 | bytes 3932160 | tf_op jit(solution)/shard_map/pairs/pallas_call | solution.py:294
  34.7 4.3 %pairs.12 = (f32[384,384]{1,0:T(8,128)S(1)}, f32[2,384,384]{2,1,0:T(8,128)S(1)}, f32[2,384,384]{2,1,0:T(8,128)S(1)}) custom-call(s32[1]{0:T(128)} %bitcast.far_ref, bf16[784,384]{1,0:T(8,128)(2,1)} %get-tuple-element.77.refs_0_.refs_1_, bf16[2,384,1536]{2,1,0:T(8,128)(2,1)S(1)} %pack.1.refs_1_.refs_3_.refs_2_, ...), custom_call_target="tpu_custom_call" | custom-call | flops 27179089920 | bytes 2949120 | tf_op jit(solution)/shard_map/pairs/pallas_call | solution.py:294
  39.0 7.6 %collective-permute-done.6.refs_0_.refs_2_ = bf16[784,640]{1,0:T(8,128)(2,1)} collective-permute-done((bf16[784,640]{1,0:T(8,128)(2,1)}, bf16[784,640]{1,0:T(8,128)(2,1)}, u32[]{:S(2)}, u32[]{:S(2)}) %collective-permute-start.6) | collective-permute-done | bytes 1003552 | tf_op jit(solution)/shard_map/ppermute | solution.py:470
  46.6 1.3 collective-permute-start.7
  47.9 0.0 collective-permute-done.3.refs_0_
  47.9 0.0 collective-permute-done.4.refs_5_.refs_3_.refs_4_
  47.9 12.5 %pairs.13 = (bf16[384,512]{1,0:T(8,128)(2,1)S(1)}, f32[384,512]{1,0:T(8,128)S(1)}, f32[384,512]{1,0:T(8,128)S(1)}, f32[2,384,512]{2,1,0:T(8,128)S(1)}, bf16[2,38...) custom-call(s32[1]{0:T(128)} %bitcast.far_ref, bf16[784,512]{1,0:T(8,128)(2,1)S(1)} %collective-permute-done.3.refs_0_, ...), custom_call_target="tpu_custom_call" | custom-call | flops 22649241600 | bytes 3932160 | tf_op jit(solution)/shard_map/pairs/pallas_call | solution.py:294
  60.4 2.0 %collective-permute-start.8 = (bf16[384,512]{1,0:T(8,128)(2,1)S(1)}, bf16[384,512]{1,0:T(8,128)(2,1)S(1)}, u32[]{:S(2)}, u32[]{:S(2)}) collective-permute-start(bf16[384,512]{1,0:T(8,128)(2,1)S(1)} %get-tuple-element.100), channel_id=1, source_target_pairs={{2,0},{4,2},{6,4},{1,3},{3,5},{5,7},{0,1},{7,6},{10,8},{12,10},{14... | collective-permute-start | bytes 1179656 | tf_op jit(solution)/shard_map/ppermute | solution.py:440
  62.3 0.0 collective-permute-start.10
  62.3 0.0 collective-permute-done.refs_0_
  62.3 0.0 collective-permute-start.5
  62.3 6.7 %pairs.14 = (f32[384,640]{1,0:T(8,128)S(1)}, f32[2,384,640]{2,1,0:T(8,128)S(1)}, f32[2,384,640]{2,1,0:T(8,128)S(1)}) custom-call(s32[1]{0:T(128)} %bitcast.far_ref, bf16[784,640]{1,0:T(8,128)(2,1)} %collective-permute-done.6.refs_0_.refs_2_, bf16[2,384,1536]{2,1,0:T(8,128)(2,1)S(1)} %pack.1.refs_1_.refs_3_.refs_2_, ...), custom_call_target="tpu_custom_call" | custom-call | flops 5662310400 | bytes 4915200 | tf_op jit(solution)/shard_map/pairs/pallas_call | solution.py:294
  69.1 0.2 collective-permute-done.7.refs_0_
  69.2 15.0 %pairs.15 = (bf16[384,640]{1,0:T(8,128)(2,1)S(1)}, f32[384,640]{1,0:T(8,128)S(1)}, f32[384,640]{1,0:T(8,128)S(1)}, f32[2,384,640]{2,1,0:T(8,128)S(1)}, bf16[2,38...) custom-call(s32[1]{0:T(128)} %bitcast.far_ref, ...), custom_call_target="tpu_custom_call", output_to_operand_aliasing={{5}: (11, {})} | custom-call | flops 28311552000 | bytes 4915200 | tf_op jit(solution)/shard_map/pairs/pallas_call | solution.py:294
  84.2 2.4 %collective-permute-start.15 = (bf16[384,640]{1,0:T(8,128)(2,1)S(1)}, bf16[384,640]{1,0:T(8,128)(2,1)S(1)}, u32[]{:S(2)}, u32[]{:S(2)}) collective-permute-start(bf16[384,640]{1,0:T(8,128)(2,1)S(1)} %get-tuple-element.120), channel_id=1, source_target_pairs={{2,0},{4,2},{6,4},{1,3},{3,5},{5,7},{0,1},{7,6},{10,8},{12,10},{14... | collective-permute-start | bytes 1474568 | tf_op jit(solution)/shard_map/ppermute | solution.py:440
  86.7 0.1 add_convert_fusion.1
  86.8 0.2 collective-permute-start.9
  87.0 6.4 %pairs.16 = (bf16[384,384]{1,0:T(8,128)(2,1)S(1)}, f32[2,384,384]{2,1,0:T(8,128)S(1)}, f32[2,384,384]{2,1,0:T(8,128)S(1)}, f32[2,384,384]{2,1,0:T(8,128)S(1)}) custom-call(s32[1]{0:T(128)} %bitcast.far_ref, bf16[784,384]{1,0:T(8,128)(2,1)} %collective-permute-done.refs_0_, bf16[2,384,1536]{2,1,0:T(8,128)(2,1)S(1)} %pack.1.refs_1_.refs_3_.refs_2_, ...), custom_call_target="tpu_custom_call" | custom-call | flops 20384317440 | bytes 2949120 | tf_op jit(solution)/shard_map/pairs/pallas_call | solution.py:294
  93.4 7.5 %collective-permute-start.14 = (bf16[2,384,1152]{2,1,0:T(8,128)(2,1)S(1)}, bf16[2,384,1152]{2,1,0:T(8,128)(2,1)S(1)}, u32[]{:S(2)}, u32[]{:S(2)}) collective-permute-start(bf16[2,384,1152]{2,1,0:T(8,128)(2,1)S(1)} %get-tuple-element.113), channel_id=1, source_target_pairs={{0,0},{24,24},{8,16},{16,8},{1,1},{25,25},{9,17},{17,9},{2,2},{26,... | collective-permute-start | bytes 5308424 | tf_op jit(solution)/shard_map/ppermute | solution.py:447
  101.0 2.7 %collective-permute-done.15 = bf16[384,640]{1,0:T(8,128)(2,1)S(1)} collective-permute-done((bf16[384,640]{1,0:T(8,128)(2,1)S(1)}, bf16[384,640]{1,0:T(8,128)(2,1)S(1)}, u32[]{:S(2)}, u32[]{:S(2)}) %collective-permute-start.15) | collective-permute-done | bytes 491552 | tf_op jit(solution)/shard_map/ppermute | solution.py:440
  103.7 0.4 collective-permute-start.13
  104.0 0.1 add_convert_fusion
  104.2 0.0 collective-permute-done.5.refs_0_
  104.2 2.7 %collective-permute-start.16 = (bf16[384,640]{1,0:T(8,128)(2,1)S(1)}, bf16[384,640]{1,0:T(8,128)(2,1)S(1)}, u32[]{:S(2)}, u32[]{:S(2)}) collective-permute-start(bf16[384,640]{1,0:T(8,128)(2,1)S(1)} %add_convert_fusion), channel_id=1, source_target_pairs={{0,1},{1,0},{2,3},{3,2},{4,5},{5,4},{6,7},{7,6},{8,9},{9,8},{10,11... | collective-permute-start | bytes 1474568 | tf_op jit(solution)/shard_map/ppermute | solution.py:456
  106.9 7.8 %pairs.17 = (bf16[384,384]{1,0:T(8,128)(2,1)S(1)}, f32[384,384]{1,0:T(8,128)S(1)}, f32[2,384,384]{2,1,0:T(8,128)S(1)}, bf16[2,384,384]{2,1,0:T(8,128)(2,1)S(1)}, bf16[2,384,384]{2,1,0:T(8,128)(2,1)S(1)}) custom-call(s32[1]{0:T(128)} %bitcast.far_ref, bf16[784,384]{1,0:T(8,128)(2,1)S(1)} %collective-permute-done.5.refs_0_, ...), custom_call_target="tpu_custom_call" | custom-call | flops 13589544960 | bytes 2949120 | tf_op jit(solution)/shard_map/pairs/pallas_call | solution.py:294
  114.6 0.1 collective-permute-start.11
  114.7 3.3 %collective-permute-start.12 = (bf16[2,384,384]{2,1,0:T(8,128)(2,1)S(1)}, bf16[2,384,384]{2,1,0:T(8,128)(2,1)S(1)}, u32[]{:S(2)}, u32[]{:S(2)}) collective-permute-start(bf16[2,384,384]{2,1,0:T(8,128)(2,1)S(1)} %get-tuple-element.109), channel_id=1, source_target_pairs={{0,0},{24,24},{8,16},{16,8},{1,1},{25,25},{9,17},{17,9},{2,2},{26,... | collective-permute-start | bytes 1769480 | tf_op jit(solution)/shard_map/ppermute | solution.py:440
  118.0 0.4 collective-permute-done.16.rest_0_
  118.4 1.3 collective-permute-start.17
  119.7 1.5 %collective-permute-done.14.far = bf16[2,384,1152]{2,1,0:T(8,128)(2,1)S(1)} collective-permute-done((bf16[2,384,1152]{2,1,0:T(8,128)(2,1)S(1)}, bf16[2,384,1152]{2,1,0:T(8,128)(2,1)S(1)}, u32[]{:S(2)}, u32[]{:S(2)}) %collective-permute-start.14) | collective-permute-done | bytes 1769504 | tf_op jit(solution)/shard_map/ppermute | solution.py:447
  121.1 3.5 %collective-permute-start.18 = (bf16[384,384]{1,0:T(8,128)(2,1)S(1)}, bf16[384,384]{1,0:T(8,128)(2,1)S(1)}, u32[]{:S(2)}, u32[]{:S(2)}) collective-permute-start(bf16[384,384]{1,0:T(8,128)(2,1)S(1)} %get-tuple-element.127), channel_id=1, source_target_pairs={{0,0},{7,7},{1,2},{2,1},{3,4},{4,3},{5,6},{6,5},{8,8},{15,15},{9,1... | collective-permute-start | bytes 884744 | tf_op jit(solution)/shard_map/ppermute | solution.py:440
  124.7 1.3 finish.3
  126.0 1.7 %finish.4 = (bf16[384,1536]{1,0:T(8,128)(2,1)}, bf16[384,1536]{1,0:T(8,128)(2,1)}, bf16[384,1536]{1,0:T(8,128)(2,1)}) custom-call(f32[2,384,640]{2,1,0:T(8,128)S(1)} %get-tuple-element.95.own_kv, bf16[2,384,640]{2,1,0:T(8,128)(2,1)S(1)} %collective-permute-done.13.near, ...), custom_call_target="tpu_custom_call", output_to_operand_aliasing={{0}: (5, {}), {1}: (6, {}), {2}: (7, {})} | custom-call | flops 1966080 | bytes 7372800 | tf_op jit(solution)/shard_map/finish/pallas_call | solution.py:343
  127.7 3.8 %collective-permute-done.17.rest_0_ = bf16[384,384]{1,0:T(8,128)(2,1)S(1)} collective-permute-done((bf16[384,384]{1,0:T(8,128)(2,1)S(1)}, bf16[384,384]{1,0:T(8,128)(2,1)S(1)}, u32[]{:S(2)}, u32[]{:S(2)}) %collective-permute-start.17) | collective-permute-done | bytes 294944 | tf_op jit(solution)/shard_map/ppermute | solution.py:440
  131.4 1.5 %collective-permute-done.18.rest_1_ = bf16[384,384]{1,0:T(8,128)(2,1)S(1)} collective-permute-done((bf16[384,384]{1,0:T(8,128)(2,1)S(1)}, bf16[384,384]{1,0:T(8,128)(2,1)S(1)}, u32[]{:S(2)}, u32[]{:S(2)}) %collective-permute-start.18) | collective-permute-done | bytes 294944 | tf_op jit(solution)/shard_map/ppermute | solution.py:440
  132.9 1.0 finish.5
  (11 shorter events, 0.0 us)
Async XLA Ops:
  0.6 2.6 %copy-start = (f32[1,1,12,384]{3,1,2,0:T(1,128)S(1)}, f32[1,1,12,384]{3,1,2,0:T(1,128)}, u32[]{:S(2)}) copy-start(f32[1,1,12,384]{3,1,2,0:T(1,128)} %param.12) | copy-start | bytes 55300
  0.6 2.5 %copy-start.1 = (s32[1,1,9]{2,1,0:T(1,128)S(1)}, s32[1,1,9]{2,1,0:T(1,128)}, u32[]{:S(2)}) copy-start(s32[1,1,9]{2,1,0:T(1,128)} %param.13) | copy-start | bytes 112
  2.4 13.1 %collective-permute-start.2 = (bf16[2,384,1536]{2,1,0:T(8,128)(2,1)S(1)}, bf16[2,384,1536]{2,1,0:T(8,128)(2,1)}, u32[]{:S(2)}, u32[]{:S(2)}) collective-permute-start(bf16[2,384,1536]{2,1,0:T(8,128)(2,1)S(1)} %pack.1.refs_1_.refs_3_.refs_2_), channel_id=1, source_target_pairs={{0,8},{8,0},{16,24},{24,16},{1,9},{9,1},{17,25},{25,17},{2,10},{10... | collective-permute-start | bytes 7077896 | tf_op jit(solution)/shard_map/ppermute | solution.py:393
  5.4 22.2 %collective-permute-start.1 = (bf16[784,512]{1,0:T(8,128)(2,1)S(1)}, bf16[784,512]{1,0:T(8,128)(2,1)}, u32[]{:S(2)}, u32[]{:S(2)}) collective-permute-start(bf16[784,512]{1,0:T(8,128)(2,1)S(1)} %prep.2.refs_0_.refs_1_), channel_id=1, source_target_pairs={{0,1},{1,0},{2,3},{3,2},{4,5},{5,4},{6,7},{7,6},{8,9},{9,8},{10,11... | collective-permute-start | bytes 2408456 | tf_op jit(solution)/shard_map/ppermute | solution.py:398
  6.7 41.2 %collective-permute-start.4 = (bf16[2,384,1536]{2,1,0:T(8,128)(2,1)S(1)}, bf16[2,384,1536]{2,1,0:T(8,128)(2,1)}, u32[]{:S(2)}, u32[]{:S(2)}) collective-permute-start(bf16[2,384,1536]{2,1,0:T(8,128)(2,1)S(1)} %pack.1.refs_1_.refs_3_.refs_2_), channel_id=1, source_target_pairs={{0,0},{24,24},{8,16},{16,8},{1,1},{25,25},{9,17},{17,9},{2,2},{26,... | collective-permute-start | bytes 7077896 | tf_op jit(solution)/shard_map/ppermute | solution.py:399
  14.0 32.5 %collective-permute-start.6 = (bf16[784,640]{1,0:T(8,128)(2,1)}, bf16[784,640]{1,0:T(8,128)(2,1)}, u32[]{:S(2)}, u32[]{:S(2)}) collective-permute-start(bf16[784,640]{1,0:T(8,128)(2,1)} %get-tuple-element.72.refs_0_.refs_1_), channel_id=1, source_target_pairs={{0,1},{1,0},{2,3},{3,2},{4,5},{5,4},{6,7},{7,6},{8,9},{9,8},{10,11... | collective-permute-start | bytes 3010568 | tf_op jit(solution)/shard_map/ppermute | solution.py:470
  14.3 48.0 %collective-permute-start = (bf16[784,384]{1,0:T(8,128)(2,1)}, bf16[784,384]{1,0:T(8,128)(2,1)}, u32[]{:S(2)}, u32[]{:S(2)}) collective-permute-start(bf16[784,384]{1,0:T(8,128)(2,1)} %get-tuple-element.77.refs_0_.refs_1_), channel_id=1, source_target_pairs={{0,1},{1,0},{2,3},{3,2},{4,5},{5,4},{6,7},{7,6},{8,9},{9,8},{10,11... | collective-permute-start | bytes 1806344 | tf_op jit(solution)/shard_map/ppermute | solution.py:470
  27.6 20.2 %collective-permute-start.3 = (bf16[784,512]{1,0:T(8,128)(2,1)}, bf16[784,512]{1,0:T(8,128)(2,1)S(1)}, u32[]{:S(2)}, u32[]{:S(2)}) collective-permute-start(bf16[784,512]{1,0:T(8,128)(2,1)} %collective-permute-done.1.refs_0_.refs_2_), channel_id=1, source_target_pairs={{0,2},{2,4},{4,6},{6,0},{1,7},{3,1},{5,3},{7,5},{8,10},{10,12},{12... | collective-permute-start | bytes 2408456 | tf_op jit(solution)/shard_map/ppermute | solution.py:452
  46.6 22.7 %collective-permute-start.7 = (bf16[784,640]{1,0:T(8,128)(2,1)}, bf16[784,640]{1,0:T(8,128)(2,1)S(1)}, u32[]{:S(2)}, u32[]{:S(2)}) collective-permute-start(bf16[784,640]{1,0:T(8,128)(2,1)} %collective-permute-done.6.refs_0_.refs_2_), channel_id=1, source_target_pairs={{0,2},{2,4},{4,6},{6,0},{1,7},{3,1},{5,3},{7,5},{8,10},{10,12},{12... | collective-permute-start | bytes 3010568 | tf_op jit(solution)/shard_map/ppermute | solution.py:452
  60.4 26.3 %collective-permute-start.8 = (bf16[384,512]{1,0:T(8,128)(2,1)S(1)}, bf16[384,512]{1,0:T(8,128)(2,1)S(1)}, u32[]{:S(2)}, u32[]{:S(2)}) collective-permute-start(bf16[384,512]{1,0:T(8,128)(2,1)S(1)} %get-tuple-element.100), channel_id=1, source_target_pairs={{2,0},{4,2},{6,4},{1,3},{3,5},{5,7},{0,1},{7,6},{10,8},{12,10},{14... | collective-permute-start | bytes 1179656 | tf_op jit(solution)/shard_map/ppermute | solution.py:440
  62.3 44.5 %collective-permute-start.10 = (bf16[2,384,512]{2,1,0:T(8,128)(2,1)S(1)}, bf16[2,384,512]{2,1,0:T(8,128)(2,1)S(1)}, u32[]{:S(2)}, u32[]{:S(2)}) collective-permute-start(bf16[2,384,512]{2,1,0:T(8,128)(2,1)S(1)} %get-tuple-element.102), channel_id=1, source_target_pairs={{0,8},{8,0},{16,24},{24,16},{1,9},{9,1},{17,25},{25,17},{2,10},{10... | collective-permute-start | bytes 2359304 | tf_op jit(solution)/shard_map/ppermute | solution.py:440
  62.3 41.9 %collective-permute-start.5 = (bf16[784,384]{1,0:T(8,128)(2,1)}, bf16[784,384]{1,0:T(8,128)(2,1)S(1)}, u32[]{:S(2)}, u32[]{:S(2)}) collective-permute-start(bf16[784,384]{1,0:T(8,128)(2,1)} %collective-permute-done.refs_0_), channel_id=1, source_target_pairs={{0,2},{2,4},{4,6},{6,0},{1,7},{3,1},{5,3},{7,5},{8,10},{10,12},{12... | collective-permute-start | bytes 1806344 | tf_op jit(solution)/shard_map/ppermute | solution.py:452
  84.2 19.4 %collective-permute-start.15 = (bf16[384,640]{1,0:T(8,128)(2,1)S(1)}, bf16[384,640]{1,0:T(8,128)(2,1)S(1)}, u32[]{:S(2)}, u32[]{:S(2)}) collective-permute-start(bf16[384,640]{1,0:T(8,128)(2,1)S(1)} %get-tuple-element.120), channel_id=1, source_target_pairs={{2,0},{4,2},{6,4},{1,3},{3,5},{5,7},{0,1},{7,6},{10,8},{12,10},{14... | collective-permute-start | bytes 1474568 | tf_op jit(solution)/shard_map/ppermute | solution.py:440
  86.8 20.1 %collective-permute-start.9 = (bf16[384,512]{1,0:T(8,128)(2,1)S(1)}, bf16[384,512]{1,0:T(8,128)(2,1)S(1)}, u32[]{:S(2)}, u32[]{:S(2)}) collective-permute-start(bf16[384,512]{1,0:T(8,128)(2,1)S(1)} %add_convert_fusion.1), channel_id=1, source_target_pairs={{0,1},{1,0},{2,3},{3,2},{4,5},{5,4},{6,7},{7,6},{8,9},{9,8},{10,11... | collective-permute-start | bytes 1179656 | tf_op jit(solution)/shard_map/ppermute | solution.py:456
  93.4 27.7 %collective-permute-start.14 = (bf16[2,384,1152]{2,1,0:T(8,128)(2,1)S(1)}, bf16[2,384,1152]{2,1,0:T(8,128)(2,1)S(1)}, u32[]{:S(2)}, u32[]{:S(2)}) collective-permute-start(bf16[2,384,1152]{2,1,0:T(8,128)(2,1)S(1)} %get-tuple-element.113), channel_id=1, source_target_pairs={{0,0},{24,24},{8,16},{16,8},{1,1},{25,25},{9,17},{17,9},{2,2},{26,... | collective-permute-start | bytes 5308424 | tf_op jit(solution)/shard_map/ppermute | solution.py:447
  103.7 22.3 %collective-permute-start.13 = (bf16[2,384,640]{2,1,0:T(8,128)(2,1)S(1)}, bf16[2,384,640]{2,1,0:T(8,128)(2,1)S(1)}, u32[]{:S(2)}, u32[]{:S(2)}) collective-permute-start(bf16[2,384,640]{2,1,0:T(8,128)(2,1)S(1)} %get-tuple-element.111), channel_id=1, source_target_pairs={{0,8},{8,0},{16,24},{24,16},{1,9},{9,1},{17,25},{25,17},{2,10},{10... | collective-permute-start | bytes 2949128 | tf_op jit(solution)/shard_map/ppermute | solution.py:440
  104.2 14.3 %collective-permute-start.16 = (bf16[384,640]{1,0:T(8,128)(2,1)S(1)}, bf16[384,640]{1,0:T(8,128)(2,1)S(1)}, u32[]{:S(2)}, u32[]{:S(2)}) collective-permute-start(bf16[384,640]{1,0:T(8,128)(2,1)S(1)} %add_convert_fusion), channel_id=1, source_target_pairs={{0,1},{1,0},{2,3},{3,2},{4,5},{5,4},{6,7},{7,6},{8,9},{9,8},{10,11... | collective-permute-start | bytes 1474568 | tf_op jit(solution)/shard_map/ppermute | solution.py:456
  114.6 18.3 %collective-permute-start.11 = (bf16[2,384,384]{2,1,0:T(8,128)(2,1)S(1)}, bf16[2,384,384]{2,1,0:T(8,128)(2,1)S(1)}, u32[]{:S(2)}, u32[]{:S(2)}) collective-permute-start(bf16[2,384,384]{2,1,0:T(8,128)(2,1)S(1)} %get-tuple-element.108), channel_id=1, source_target_pairs={{0,8},{8,0},{16,24},{24,16},{1,9},{9,1},{17,25},{25,17},{2,10},{10... | collective-permute-start | bytes 1769480 | tf_op jit(solution)/shard_map/ppermute | solution.py:440
  114.7 18.2 %collective-permute-start.12 = (bf16[2,384,384]{2,1,0:T(8,128)(2,1)S(1)}, bf16[2,384,384]{2,1,0:T(8,128)(2,1)S(1)}, u32[]{:S(2)}, u32[]{:S(2)}) collective-permute-start(bf16[2,384,384]{2,1,0:T(8,128)(2,1)S(1)} %get-tuple-element.109), channel_id=1, source_target_pairs={{0,0},{24,24},{8,16},{16,8},{1,1},{25,25},{9,17},{17,9},{2,2},{26,... | collective-permute-start | bytes 1769480 | tf_op jit(solution)/shard_map/ppermute | solution.py:440
  118.4 13.0 %collective-permute-start.17 = (bf16[384,384]{1,0:T(8,128)(2,1)S(1)}, bf16[384,384]{1,0:T(8,128)(2,1)S(1)}, u32[]{:S(2)}, u32[]{:S(2)}) collective-permute-start(bf16[384,384]{1,0:T(8,128)(2,1)S(1)} %get-tuple-element.126), channel_id=1, source_target_pairs={{0,1},{1,0},{2,3},{3,2},{4,5},{5,4},{6,7},{7,6},{8,9},{9,8},{10,11... | collective-permute-start | bytes 884744 | tf_op jit(solution)/shard_map/ppermute | solution.py:440
  121.1 11.8 %collective-permute-start.18 = (bf16[384,384]{1,0:T(8,128)(2,1)S(1)}, bf16[384,384]{1,0:T(8,128)(2,1)S(1)}, u32[]{:S(2)}, u32[]{:S(2)}) collective-permute-start(bf16[384,384]{1,0:T(8,128)(2,1)S(1)} %get-tuple-element.127), channel_id=1, source_target_pairs={{0,0},{7,7},{1,2},{2,1},{3,4},{4,3},{5,6},{6,5},{8,8},{15,15},{9,1... | collective-permute-start | bytes 884744 | tf_op jit(solution)/shard_map/ppermute | solution.py:440

commit v4 on v3

--- a/solution.py
+++ b/solution.py
@@ -26,10 +26,16 @@
     STAGES[1] + ((FAR, (PARTNER,)),),
     ((HERE, (OUTER,)), (NEAR, (OUTER,)), (FAR, (OWN, OUTER))),
 )
+SECOND_STAGES = (
+    STAGES[0],
+    ((FAR, (OWN,)),),
+    STAGES[1],
+    ((HERE, (OUTER,)), (NEAR, (OUTER,)), (FAR, (PARTNER, OUTER))),
+)
 DIRECT = 2
-ORDER = (('stage', 0, 0), ('stage', 1, 0), ('hand', 0), ('stage', 0, 1), ('stage', 2, 0), ('hand', 1), ('stage', 0, 2), ('hand', 2), ('stage', 1, 1), ('back', 0), ('stage', 1, 2), ('stage', 2, 1), ('send', 1, 'kv2'), ('back', 1), ('stage', 2, 2, (0, 'q2'), (0, 'kv1')), ('finish', 0), ('finish', 1), ('finish', 2))
+ORDER = (('stage', 0, 0), ('stage', 1, 0), ('hand', 0), ('stage', 0, 1), ('stage', 2, 0), ('stage', 1, 1), ('hand', 1), ('stage', 0, 2), ('hand', 2), ('stage', 1, 2), ('back', 0), ('stage', 1, 3), ('stage', 2, 1), ('send', 1, 'kv2'), ('back', 1), ('stage', 2, 2, (0, 'q2'), (0, 'kv1')), ('finish', 0), ('finish', 1), ('finish', 2))
 JOINED = ('kv2',)
-WEIGHTS = ((60, 60, 60), (60, 30, 60), (240, 120, 60))
+WEIGHTS = ((60, 60, 60), (60, 60, 30, 60), (240, 120, 60))
 EXTRA = 16
 TERMS = 2
 VMEM_LIMIT = 20 * 1024 * 1024
@@ -408,7 +414,7 @@
 
     def stage(c, step, *awaited):
         messages = {OUTER: outers.get(c), OWN: mine[c], PARTNER: theirs.get(c)}
-        stages = LATER_STAGES if c >= DIRECT else STAGES
+        stages = LATER_STAGES if c >= DIRECT else SECOND_STAGES if c == 1 else STAGES
         work = stages[step]
         needed = {j: messages[j] for _, js in work for j in js}
         first_used = min(needed)
@@ -426,7 +432,7 @@
         sums[c] = run_stage(
             work, WEIGHTS[c][step], final, joined, firsts[c], CHUNKS[c], width, has_far, frames_kv, needed, sums[c]
         )
-        done.append(sums[c]["kv0"])
+        done.append(sums[c]["kv%d" % work[0][0]])
         for name, axis, pairs in (
             ("q0", "space", owners if c >= DIRECT else homeward),
             ("q2", "space", partner),

time: 135 us -> 135 us (level)
  Pallas kernels: 82.5 us -> 85.3 us
  starting transfers between devices: 32.8 us -> 31.3 us
  waiting for transfers between devices: 17.6 us -> 16.2 us
    ppermute x2, waiting for transfers between devices: 7.56 us -> 2.3 us  [per_device(): theirs[c] = lax.ppermute(mine[c], 'space', partner)]
    ppermute x8, waiting for transfers between devices: 7.98 us -> 13.2 us  [stage(): backs[c][name] = lax.ppermute(sums[c][name], axis, pairs)]
    pallas_call x9 -> x10, Pallas kernels: 70.5 us -> 73.2 us  [run_stage(): pl.pallas_call(functools.partial(stage_kernel, work, names, head_width **...]
    ppermute x8, starting transfers between devices: 12.9 us -> 11.5 us  [stage(): backs[c][name] = lax.ppermute(sums[c][name], axis, pairs)]
    ppermute x1, waiting for transfers between devices: 1.45 us -> 0.01 us  [send_joined(): joined = lax.ppermute(after(sums[c][name], *done[-1:]), 'tm', axis_pairs)]
  transfers between devices with their start and end apart: 19 -> 19, of which waited for: 7 -> 5; matrix products, arithmetic and copies ran while one was open for 0% -> 0% of each run, Pallas kernels for 59% -> 62%
where the time goes in v4:
time: 135 us; the launch traced here: 134 us
  Pallas kernels  85.3 us (63%)
  starting transfers between devices  31.3 us (23%)
  waiting for transfers between devices  16.2 us (12%)
    pallas_call x10, Pallas kernels, run_stage(): pl.pallas_call(functools.partial(stage_kernel, work, names, head_width **...  73.2 us
    ppermute x8, waiting for transfers between devices, stage(): backs[c][name] = lax.ppermute(sums[c][name], axis, pairs)  13.2 us
    ppermute x8, starting transfers between devices, stage(): backs[c][name] = lax.ppermute(sums[c][name], axis, pairs)  11.5 us
    ppermute x1, starting transfers between devices, send_joined(): joined = lax.ppermute(after(sums[c][name], *done[-1:]), 'tm', axis_pairs)  7.47 us
    pallas_call x2, Pallas kernels, prep(): pl.pallas_call(functools.partial(prep_kernel, counts, *sizes), grid_spec=...  6.22 us
    pallas_call x3, Pallas kernels, finish(): pl.pallas_call(functools.partial(finish_kernel, head_width ** (-0.5), len...  4.05 us
    ppermute x1, starting transfers between devices, per_device(): far_kv = lax.ppermute(after(own_kv, mine[0]), 'tm', far_pairs)  3.34 us
    ppermute x2, starting transfers between devices, send_back(): backs[c]['q2'] = lax.ppermute(total.astype(BF16), 'space', partner)  2.85 us
  transfers between devices with their start and end apart: 19, of which 5 were waited for; matrix products, arithmetic and copies ran while one was open for 0% of the time, Pallas kernels for 62%

profile of v4, /device:TPU:9, one launch (start us, length us, event | category | flops | bytes accessed | tf_op | source)
XLA Modules:
  0.0 133.8 jit_solution(2046549488700880484)
XLA Ops:
  0.7 1.8 %pack.1.refs_1_.refs_3_.refs_2_ = bf16[2,384,1536]{2,1,0:T(8,128)(2,1)S(1)} custom-call(bf16[384,1536]{1,0:T(8,128)(2,1)} %bitcast.26, bf16[384,1536]{1,0:T(8,128)(2,1)} %bitcast.27), custom_call_target="tpu_custom_call" | custom-call | bytes 4718592 | tf_op jit(solution)/shard_map/pack/pallas_call | solution.py:157
  2.4 0.7 collective-permute-start.2
  3.2 2.2 %prep.2.refs_0_.refs_1_ = bf16[784,512]{1,0:T(8,128)(2,1)S(1)} custom-call(s32[1]{0:T(128)} %bitcast.1.frame_ref, s32[1]{0:T(128)} %bitcast.2.row_ref, s32[9]{0:T(128)S(1)} %bitcast.15, bf16[384,1536]{1,0:T(8,128)(2,1)} %bitcast.20, bf16[384,1536]{1,0:T(8,128)(2,1)} %bitcast.22, bf16[384,1536]{1,0:T(8,128)(2,1)} %bitcast.24, f32[12,1,384]{2,1,0:T(1,128)S(1)} %bitcast.13), custom_call_target="tpu_custom_call" | custom-call | flops 393216 | bytes 1966080 | tf_op jit(solution)/shard_map/prep/pallas_call | solution.py:122
  5.4 1.3 collective-permute-start.1
  6.7 3.3 %collective-permute-start.4 = (bf16[2,384,1536]{2,1,0:T(8,128)(2,1)S(1)}, bf16[2,384,1536]{2,1,0:T(8,128)(2,1)}, u32[]{:S(2)}, u32[]{:S(2)}) collective-permute-start(bf16[2,384,1536]{2,1,0:T(8,128)(2,1)S(1)} %pack.1.refs_1_.refs_3_.refs_2_), channel_id=1, source_target_pairs={{0,0},{24,24},{8,16},{16,8},{1,1},{25,25},{9,17},{17,9},{2,2},{26,... | collective-permute-start | bytes 7077896 | tf_op jit(solution)/shard_map/ppermute | solution.py:405
  10.0 4.0 %prep.3 = (bf16[784,640]{1,0:T(8,128)(2,1)}, bf16[784,384]{1,0:T(8,128)(2,1)}) custom-call(s32[1]{0:T(128)} %bitcast.1.frame_ref, s32[1]{0:T(128)} %bitcast.2.row_ref, s32[9]{0:T(128)S(1)} %bitcast.16, bf16[384,1536]{1,0:T(8,128)(2,1)} %bitcast.21, bf16[384,1536]{1,0:T(8,128)(2,1)} %bitcast.23, bf16[384,1536]{1,0:T(8,128)(2,1)} %bitcast.25, ...), custom_call_target="tpu_custom_call" | custom-call | flops 786432 | bytes 3932160 | tf_op jit(solution)/shard_map/prep/pallas_call | solution.py:122
  14.0 0.3 collective-permute-start.6
  14.3 1.2 collective-permute-start
  15.5 0.0 collective-permute-done.2.refs_2_.refs_4_.refs_3_
  15.5 5.6 %pairs.10 = (f32[384,512]{1,0:T(8,128)S(1)}, f32[2,384,512]{2,1,0:T(8,128)S(1)}, f32[2,384,512]{2,1,0:T(8,128)S(1)}) custom-call(s32[1]{0:T(128)} %bitcast.far_ref, bf16[784,512]{1,0:T(8,128)(2,1)S(1)} %prep.2.refs_0_.refs_1_, bf16[2,384,1536]{2,1,0:T(8,128)(2,1)S(1)} %pack.1.refs_1_.refs_3_.refs_2_, ...), custom_call_target="tpu_custom_call" | custom-call | flops 9059696640 | bytes 3932160 | tf_op jit(solution)/shard_map/pairs/pallas_call | solution.py:300
  21.1 6.5 %pairs.11 = (f32[384,640]{1,0:T(8,128)S(1)}, f32[2,384,640]{2,1,0:T(8,128)S(1)}, f32[2,384,640]{2,1,0:T(8,128)S(1)}) custom-call(s32[1]{0:T(128)} %bitcast.far_ref, bf16[784,640]{1,0:T(8,128)(2,1)} %get-tuple-element.81.refs_0_, bf16[2,384,1536]{2,1,0:T(8,128)(2,1)S(1)} %pack.1.refs_1_.refs_3_.refs_2_, ...), custom_call_target="tpu_custom_call" | custom-call | flops 11324620800 | bytes 4915200 | tf_op jit(solution)/shard_map/pairs/pallas_call | solution.py:300
  27.6 0.0 collective-permute-done.1.refs_0_.refs_2_
  27.6 1.4 %collective-permute-start.3 = (bf16[784,512]{1,0:T(8,128)(2,1)}, bf16[784,512]{1,0:T(8,128)(2,1)S(1)}, u32[]{:S(2)}, u32[]{:S(2)}) collective-permute-start(bf16[784,512]{1,0:T(8,128)(2,1)} %collective-permute-done.1.refs_0_.refs_2_), channel_id=1, source_target_pairs={{0,2},{2,4},{4,6},{6,0},{1,7},{3,1},{5,3},{7,5},{8,10},{10,12},{12... | collective-permute-start | bytes 2408456 | tf_op jit(solution)/shard_map/ppermute | solution.py:458
  29.0 5.8 %pairs.12 = (f32[384,512]{1,0:T(8,128)S(1)}, f32[2,384,512]{2,1,0:T(8,128)S(1)}, f32[2,384,512]{2,1,0:T(8,128)S(1)}) custom-call(s32[1]{0:T(128)} %bitcast.far_ref, bf16[784,512]{1,0:T(8,128)(2,1)} %collective-permute-done.1.refs_0_.refs_2_, bf16[2,384,1536]{2,1,0:T(8,128)(2,1)S(1)} %pack.1.refs_1_.refs_3_.refs_2_, ...), custom_call_target="tpu_custom_call" | custom-call | flops 9059696640 | bytes 3932160 | tf_op jit(solution)/shard_map/pairs/pallas_call | solution.py:300
  34.8 4.3 %pairs.13 = (f32[384,384]{1,0:T(8,128)S(1)}, f32[2,384,384]{2,1,0:T(8,128)S(1)}, f32[2,384,384]{2,1,0:T(8,128)S(1)}) custom-call(s32[1]{0:T(128)} %bitcast.far_ref, bf16[784,384]{1,0:T(8,128)(2,1)} %get-tuple-element.79.refs_0_.refs_1_, bf16[2,384,1536]{2,1,0:T(8,128)(2,1)S(1)} %pack.1.refs_1_.refs_3_.refs_2_, ...), custom_call_target="tpu_custom_call" | custom-call | flops 27179089920 | bytes 2949120 | tf_op jit(solution)/shard_map/pairs/pallas_call | solution.py:300
  39.1 0.0 collective-permute-done.4.refs_1_.refs_5_.refs_4_.refs_3_
  39.1 5.2 %pairs.14 = (f32[384,640]{1,0:T(8,128)S(1)}, f32[2,384,640]{2,1,0:T(8,128)S(1)}) custom-call(s32[1]{0:T(128)} %bitcast.far_ref, bf16[784,640]{1,0:T(8,128)(2,1)} %get-tuple-element.81.refs_0_, bf16[2,384,1536]{2,1,0:T(8,128)(2,1)} %collective-permute-done.4.refs_1_.refs_5_.refs_4_.refs_3_, f32[384,640]{1,0:T(8,128)S(1)} %get-tuple-element.83.refs_2_), custom_call_target="tpu_custom_call" | custom-call | flops 5662310400 | bytes 4915200 | tf_op jit(solution)/shard_map/pairs/pallas_call | solution.py:300
  44.3 2.3 %collective-permute-done.6.refs_0_.refs_1_ = bf16[784,640]{1,0:T(8,128)(2,1)} collective-permute-done((bf16[784,640]{1,0:T(8,128)(2,1)}, bf16[784,640]{1,0:T(8,128)(2,1)}, u32[]{:S(2)}, u32[]{:S(2)}) %collective-permute-start.6) | collective-permute-done | bytes 1003552 | tf_op jit(solution)/shard_map/ppermute | solution.py:476
  46.6 1.3 collective-permute-start.7
  47.9 0.0 collective-permute-done.3.refs_0_
  47.9 12.5 %pairs.15 = (bf16[384,512]{1,0:T(8,128)(2,1)S(1)}, f32[384,512]{1,0:T(8,128)S(1)}, f32[384,512]{1,0:T(8,128)S(1)}, f32[2,384,512]{2,1,0:T(8,128)S(1)}, bf16[2,38...) custom-call(s32[1]{0:T(128)} %bitcast.far_ref, bf16[784,512]{1,0:T(8,128)(2,1)S(1)} %collective-permute-done.3.refs_0_, ...), custom_call_target="tpu_custom_call" | custom-call | flops 22649241600 | bytes 3932160 | tf_op jit(solution)/shard_map/pairs/pallas_call | solution.py:300
  60.4 2.0 %collective-permute-start.8 = (bf16[384,512]{1,0:T(8,128)(2,1)S(1)}, bf16[384,512]{1,0:T(8,128)(2,1)S(1)}, u32[]{:S(2)}, u32[]{:S(2)}) collective-permute-start(bf16[384,512]{1,0:T(8,128)(2,1)S(1)} %get-tuple-element.104), channel_id=1, source_target_pairs={{2,0},{4,2},{6,4},{1,3},{3,5},{5,7},{0,1},{7,6},{10,8},{12,10},{14... | collective-permute-start | bytes 1179656 | tf_op jit(solution)/shard_map/ppermute | solution.py:446
  62.3 0.0 collective-permute-start.5
  62.3 6.7 %pairs.16 = (f32[384,640]{1,0:T(8,128)S(1)}, f32[2,384,640]{2,1,0:T(8,128)S(1)}, f32[2,384,640]{2,1,0:T(8,128)S(1)}) custom-call(s32[1]{0:T(128)} %bitcast.far_ref, bf16[784,640]{1,0:T(8,128)(2,1)} %collective-permute-done.6.refs_0_.refs_1_, bf16[2,384,1536]{2,1,0:T(8,128)(2,1)S(1)} %pack.1.refs_1_.refs_3_.refs_2_, ...), custom_call_target="tpu_custom_call" | custom-call | flops 5662310400 | bytes 4915200 | tf_op jit(solution)/shard_map/pairs/pallas_call | solution.py:300
  69.1 0.2 collective-permute-done.7.refs_0_
  69.2 12.4 %pairs.17 = (bf16[384,640]{1,0:T(8,128)(2,1)S(1)}, f32[384,640]{1,0:T(8,128)S(1)}, f32[2,384,640]{2,1,0:T(8,128)S(1)}, bf16[2,384,640]{2,1,0:T(8,128)(2,1)S(1)}, bf16[2,384,1152]{2,1,0:T(8,128)(2,1)S(1)}) custom-call(s32[1]{0:T(128)} %bitcast.far_ref, bf16[784,640]{1,0:T(8,128)(2,1)S(1)} %collective-permute-done.7.refs_0_, ...), custom_call_target="tpu_custom_call", output_to_operand_aliasing={{4}: (10, {})} | custom-call | flops 22649241600 | bytes 4915200 | tf_op jit(solution)/shard_map/pairs/pallas_call | solution.py:300
  81.7 2.4 %collective-permute-start.15 = (bf16[384,640]{1,0:T(8,128)(2,1)S(1)}, bf16[384,640]{1,0:T(8,128)(2,1)S(1)}, u32[]{:S(2)}, u32[]{:S(2)}) collective-permute-start(bf16[384,640]{1,0:T(8,128)(2,1)S(1)} %get-tuple-element.124), channel_id=1, source_target_pairs={{2,0},{4,2},{6,4},{1,3},{3,5},{5,7},{0,1},{7,6},{10,8},{12,10},{14... | collective-permute-start | bytes 1474568 | tf_op jit(solution)/shard_map/ppermute | solution.py:446
  84.1 0.1 add_convert_fusion.1
  84.2 0.3 collective-permute-start.9
  84.5 6.5 %pairs.18 = (bf16[384,384]{1,0:T(8,128)(2,1)S(1)}, f32[2,384,384]{2,1,0:T(8,128)S(1)}, f32[2,384,384]{2,1,0:T(8,128)S(1)}, f32[2,384,384]{2,1,0:T(8,128)S(1)}) custom-call(s32[1]{0:T(128)} %bitcast.far_ref, bf16[784,384]{1,0:T(8,128)(2,1)} %collective-permute-done.refs_0_, bf16[2,384,1536]{2,1,0:T(8,128)(2,1)S(1)} %pack.1.refs_1_.refs_3_.refs_2_, ...), custom_call_target="tpu_custom_call" | custom-call | flops 20384317440 | bytes 2949120 | tf_op jit(solution)/shard_map/pairs/pallas_call | solution.py:300
  90.9 7.5 %collective-permute-start.14 = (bf16[2,384,1152]{2,1,0:T(8,128)(2,1)S(1)}, bf16[2,384,1152]{2,1,0:T(8,128)(2,1)S(1)}, u32[]{:S(2)}, u32[]{:S(2)}) collective-permute-start(bf16[2,384,1152]{2,1,0:T(8,128)(2,1)S(1)} %get-tuple-element.117), channel_id=1, source_target_pairs={{0,0},{24,24},{8,16},{16,8},{1,1},{25,25},{9,17},{17,9},{2,2},{26,... | collective-permute-start | bytes 5308424 | tf_op jit(solution)/shard_map/ppermute | solution.py:453
  98.4 5.3 %collective-permute-done.15 = bf16[384,640]{1,0:T(8,128)(2,1)S(1)} collective-permute-done((bf16[384,640]{1,0:T(8,128)(2,1)S(1)}, bf16[384,640]{1,0:T(8,128)(2,1)S(1)}, u32[]{:S(2)}, u32[]{:S(2)}) %collective-permute-start.15) | collective-permute-done | bytes 491552 | tf_op jit(solution)/shard_map/ppermute | solution.py:446
  103.7 0.4 collective-permute-start.13
  104.1 0.1 add_convert_fusion
  104.2 0.0 collective-permute-done.5.refs_0_
  104.3 2.6 %collective-permute-start.16 = (bf16[384,640]{1,0:T(8,128)(2,1)S(1)}, bf16[384,640]{1,0:T(8,128)(2,1)S(1)}, u32[]{:S(2)}, u32[]{:S(2)}) collective-permute-start(bf16[384,640]{1,0:T(8,128)(2,1)S(1)} %add_convert_fusion), channel_id=1, source_target_pairs={{0,1},{1,0},{2,3},{3,2},{4,5},{5,4},{6,7},{7,6},{8,9},{9,8},{10,11... | collective-permute-start | bytes 1474568 | tf_op jit(solution)/shard_map/ppermute | solution.py:462
  106.9 7.8 %pairs.19 = (bf16[384,384]{1,0:T(8,128)(2,1)S(1)}, f32[384,384]{1,0:T(8,128)S(1)}, f32[2,384,384]{2,1,0:T(8,128)S(1)}, bf16[2,384,384]{2,1,0:T(8,128)(2,1)S(1)}, bf16[2,384,384]{2,1,0:T(8,128)(2,1)S(1)}) custom-call(s32[1]{0:T(128)} %bitcast.far_ref, bf16[784,384]{1,0:T(8,128)(2,1)S(1)} %collective-permute-done.5.refs_0_, ...), custom_call_target="tpu_custom_call" | custom-call | flops 13589544960 | bytes 2949120 | tf_op jit(solution)/shard_map/pairs/pallas_call | solution.py:300
  114.7 0.1 collective-permute-start.11
  114.7 3.2 %collective-permute-start.12 = (bf16[2,384,384]{2,1,0:T(8,128)(2,1)S(1)}, bf16[2,384,384]{2,1,0:T(8,128)(2,1)S(1)}, u32[]{:S(2)}, u32[]{:S(2)}) collective-permute-start(bf16[2,384,384]{2,1,0:T(8,128)(2,1)S(1)} %get-tuple-element.113), channel_id=1, source_target_pairs={{0,0},{24,24},{8,16},{16,8},{1,1},{25,25},{9,17},{17,9},{2,2},{26,... | collective-permute-start | bytes 1769480 | tf_op jit(solution)/shard_map/ppermute | solution.py:446
  118.0 0.5 collective-permute-done.16.rest_0_
  118.5 1.3 collective-permute-start.17
  119.7 0.0 collective-permute-done.14.far
  119.7 2.1 %collective-permute-start.18 = (bf16[384,384]{1,0:T(8,128)(2,1)S(1)}, bf16[384,384]{1,0:T(8,128)(2,1)S(1)}, u32[]{:S(2)}, u32[]{:S(2)}) collective-permute-start(bf16[384,384]{1,0:T(8,128)(2,1)S(1)} %get-tuple-element.131), channel_id=1, source_target_pairs={{0,0},{7,7},{1,2},{2,1},{3,4},{4,3},{5,6},{6,5},{8,8},{15,15},{9,1... | collective-permute-start | bytes 884744 | tf_op jit(solution)/shard_map/ppermute | solution.py:446
  121.8 1.3 finish.3
  123.1 1.7 %finish.4 = (bf16[384,1536]{1,0:T(8,128)(2,1)}, bf16[384,1536]{1,0:T(8,128)(2,1)}, bf16[384,1536]{1,0:T(8,128)(2,1)}) custom-call(f32[2,384,640]{2,1,0:T(8,128)S(1)} %get-tuple-element.99.own_kv, bf16[2,384,640]{2,1,0:T(8,128)(2,1)S(1)} %collective-permute-done.13.near, ...), custom_call_target="tpu_custom_call", output_to_operand_aliasing={{0}: (5, {}), {1}: (6, {}), {2}: (7, {})} | custom-call | flops 1966080 | bytes 7372800 | tf_op jit(solution)/shard_map/finish/pallas_call | solution.py:349
  124.9 7.9 %collective-permute-done.17.rest_0_ = bf16[384,384]{1,0:T(8,128)(2,1)S(1)} collective-permute-done((bf16[384,384]{1,0:T(8,128)(2,1)S(1)}, bf16[384,384]{1,0:T(8,128)(2,1)S(1)}, u32[]{:S(2)}, u32[]{:S(2)}) %collective-permute-start.17) | collective-permute-done | bytes 294944 | tf_op jit(solution)/shard_map/ppermute | solution.py:446
  132.8 0.0 collective-permute-done.12.far
  132.8 1.0 finish.5
  (12 shorter events, 0.0 us)
Async XLA Ops:
  0.6 2.6 %copy-start = (f32[1,1,12,384]{3,1,2,0:T(1,128)S(1)}, f32[1,1,12,384]{3,1,2,0:T(1,128)}, u32[]{:S(2)}) copy-start(f32[1,1,12,384]{3,1,2,0:T(1,128)} %param.12) | copy-start | bytes 55300
  0.6 2.5 %copy-start.1 = (s32[1,1,9]{2,1,0:T(1,128)S(1)}, s32[1,1,9]{2,1,0:T(1,128)}, u32[]{:S(2)}) copy-start(s32[1,1,9]{2,1,0:T(1,128)} %param.13) | copy-start | bytes 112
  2.4 13.1 %collective-permute-start.2 = (bf16[2,384,1536]{2,1,0:T(8,128)(2,1)S(1)}, bf16[2,384,1536]{2,1,0:T(8,128)(2,1)}, u32[]{:S(2)}, u32[]{:S(2)}) collective-permute-start(bf16[2,384,1536]{2,1,0:T(8,128)(2,1)S(1)} %pack.1.refs_1_.refs_3_.refs_2_), channel_id=1, source_target_pairs={{0,8},{8,0},{16,24},{24,16},{1,9},{9,1},{17,25},{25,17},{2,10},{10... | collective-permute-start | bytes 7077896 | tf_op jit(solution)/shard_map/ppermute | solution.py:399
  5.4 22.2 %collective-permute-start.1 = (bf16[784,512]{1,0:T(8,128)(2,1)S(1)}, bf16[784,512]{1,0:T(8,128)(2,1)}, u32[]{:S(2)}, u32[]{:S(2)}) collective-permute-start(bf16[784,512]{1,0:T(8,128)(2,1)S(1)} %prep.2.refs_0_.refs_1_), channel_id=1, source_target_pairs={{0,1},{1,0},{2,3},{3,2},{4,5},{5,4},{6,7},{7,6},{8,9},{9,8},{10,11... | collective-permute-start | bytes 2408456 | tf_op jit(solution)/shard_map/ppermute | solution.py:404
  6.7 32.4 %collective-permute-start.4 = (bf16[2,384,1536]{2,1,0:T(8,128)(2,1)S(1)}, bf16[2,384,1536]{2,1,0:T(8,128)(2,1)}, u32[]{:S(2)}, u32[]{:S(2)}) collective-permute-start(bf16[2,384,1536]{2,1,0:T(8,128)(2,1)S(1)} %pack.1.refs_1_.refs_3_.refs_2_), channel_id=1, source_target_pairs={{0,0},{24,24},{8,16},{16,8},{1,1},{25,25},{9,17},{17,9},{2,2},{26,... | collective-permute-start | bytes 7077896 | tf_op jit(solution)/shard_map/ppermute | solution.py:405
  14.0 32.5 %collective-permute-start.6 = (bf16[784,640]{1,0:T(8,128)(2,1)}, bf16[784,640]{1,0:T(8,128)(2,1)}, u32[]{:S(2)}, u32[]{:S(2)}) collective-permute-start(bf16[784,640]{1,0:T(8,128)(2,1)} %get-tuple-element.81.refs_0_), channel_id=1, source_target_pairs={{0,1},{1,0},{2,3},{3,2},{4,5},{5,4},{6,7},{7,6},{8,9},{9,8},{10,11... | collective-permute-start | bytes 3010568 | tf_op jit(solution)/shard_map/ppermute | solution.py:476
  14.3 48.0 %collective-permute-start = (bf16[784,384]{1,0:T(8,128)(2,1)}, bf16[784,384]{1,0:T(8,128)(2,1)}, u32[]{:S(2)}, u32[]{:S(2)}) collective-permute-start(bf16[784,384]{1,0:T(8,128)(2,1)} %get-tuple-element.79.refs_0_.refs_1_), channel_id=1, source_target_pairs={{0,1},{1,0},{2,3},{3,2},{4,5},{5,4},{6,7},{7,6},{8,9},{9,8},{10,11... | collective-permute-start | bytes 1806344 | tf_op jit(solution)/shard_map/ppermute | solution.py:476
  27.6 20.2 %collective-permute-start.3 = (bf16[784,512]{1,0:T(8,128)(2,1)}, bf16[784,512]{1,0:T(8,128)(2,1)S(1)}, u32[]{:S(2)}, u32[]{:S(2)}) collective-permute-start(bf16[784,512]{1,0:T(8,128)(2,1)} %collective-permute-done.1.refs_0_.refs_2_), channel_id=1, source_target_pairs={{0,2},{2,4},{4,6},{6,0},{1,7},{3,1},{5,3},{7,5},{8,10},{10,12},{12... | collective-permute-start | bytes 2408456 | tf_op jit(solution)/shard_map/ppermute | solution.py:458
  46.6 22.7 %collective-permute-start.7 = (bf16[784,640]{1,0:T(8,128)(2,1)}, bf16[784,640]{1,0:T(8,128)(2,1)S(1)}, u32[]{:S(2)}, u32[]{:S(2)}) collective-permute-start(bf16[784,640]{1,0:T(8,128)(2,1)} %collective-permute-done.6.refs_0_.refs_1_), channel_id=1, source_target_pairs={{0,2},{2,4},{4,6},{6,0},{1,7},{3,1},{5,3},{7,5},{8,10},{10,12},{12... | collective-permute-start | bytes 3010568 | tf_op jit(solution)/shard_map/ppermute | solution.py:458
  60.4 23.7 %collective-permute-start.8 = (bf16[384,512]{1,0:T(8,128)(2,1)S(1)}, bf16[384,512]{1,0:T(8,128)(2,1)S(1)}, u32[]{:S(2)}, u32[]{:S(2)}) collective-permute-start(bf16[384,512]{1,0:T(8,128)(2,1)S(1)} %get-tuple-element.104), channel_id=1, source_target_pairs={{2,0},{4,2},{6,4},{1,3},{3,5},{5,7},{0,1},{7,6},{10,8},{12,10},{14... | collective-permute-start | bytes 1179656 | tf_op jit(solution)/shard_map/ppermute | solution.py:446
  62.3 44.5 %collective-permute-start.10 = (bf16[2,384,512]{2,1,0:T(8,128)(2,1)S(1)}, bf16[2,384,512]{2,1,0:T(8,128)(2,1)S(1)}, u32[]{:S(2)}, u32[]{:S(2)}) collective-permute-start(bf16[2,384,512]{2,1,0:T(8,128)(2,1)S(1)} %get-tuple-element.106), channel_id=1, source_target_pairs={{0,8},{8,0},{16,24},{24,16},{1,9},{9,1},{17,25},{25,17},{2,10},{10... | collective-permute-start | bytes 2359304 | tf_op jit(solution)/shard_map/ppermute | solution.py:446
  62.3 41.9 %collective-permute-start.5 = (bf16[784,384]{1,0:T(8,128)(2,1)}, bf16[784,384]{1,0:T(8,128)(2,1)S(1)}, u32[]{:S(2)}, u32[]{:S(2)}) collective-permute-start(bf16[784,384]{1,0:T(8,128)(2,1)} %collective-permute-done.refs_0_), channel_id=1, source_target_pairs={{0,2},{2,4},{4,6},{6,0},{1,7},{3,1},{5,3},{7,5},{8,10},{10,12},{12... | collective-permute-start | bytes 1806344 | tf_op jit(solution)/shard_map/ppermute | solution.py:458
  81.7 22.1 %collective-permute-start.15 = (bf16[384,640]{1,0:T(8,128)(2,1)S(1)}, bf16[384,640]{1,0:T(8,128)(2,1)S(1)}, u32[]{:S(2)}, u32[]{:S(2)}) collective-permute-start(bf16[384,640]{1,0:T(8,128)(2,1)S(1)} %get-tuple-element.124), channel_id=1, source_target_pairs={{2,0},{4,2},{6,4},{1,3},{3,5},{5,7},{0,1},{7,6},{10,8},{12,10},{14... | collective-permute-start | bytes 1474568 | tf_op jit(solution)/shard_map/ppermute | solution.py:446
  84.2 22.6 %collective-permute-start.9 = (bf16[384,512]{1,0:T(8,128)(2,1)S(1)}, bf16[384,512]{1,0:T(8,128)(2,1)S(1)}, u32[]{:S(2)}, u32[]{:S(2)}) collective-permute-start(bf16[384,512]{1,0:T(8,128)(2,1)S(1)} %add_convert_fusion.1), channel_id=1, source_target_pairs={{0,1},{1,0},{2,3},{3,2},{4,5},{5,4},{6,7},{7,6},{8,9},{9,8},{10,11... | collective-permute-start | bytes 1179656 | tf_op jit(solution)/shard_map/ppermute | solution.py:462
  90.9 28.8 %collective-permute-start.14 = (bf16[2,384,1152]{2,1,0:T(8,128)(2,1)S(1)}, bf16[2,384,1152]{2,1,0:T(8,128)(2,1)S(1)}, u32[]{:S(2)}, u32[]{:S(2)}) collective-permute-start(bf16[2,384,1152]{2,1,0:T(8,128)(2,1)S(1)} %get-tuple-element.117), channel_id=1, source_target_pairs={{0,0},{24,24},{8,16},{16,8},{1,1},{25,25},{9,17},{17,9},{2,2},{26,... | collective-permute-start | bytes 5308424 | tf_op jit(solution)/shard_map/ppermute | solution.py:453
  103.7 19.4 %collective-permute-start.13 = (bf16[2,384,640]{2,1,0:T(8,128)(2,1)S(1)}, bf16[2,384,640]{2,1,0:T(8,128)(2,1)S(1)}, u32[]{:S(2)}, u32[]{:S(2)}) collective-permute-start(bf16[2,384,640]{2,1,0:T(8,128)(2,1)S(1)} %get-tuple-element.115), channel_id=1, source_target_pairs={{0,8},{8,0},{16,24},{24,16},{1,9},{9,1},{17,25},{25,17},{2,10},{10... | collective-permute-start | bytes 2949128 | tf_op jit(solution)/shard_map/ppermute | solution.py:446
  104.3 14.2 %collective-permute-start.16 = (bf16[384,640]{1,0:T(8,128)(2,1)S(1)}, bf16[384,640]{1,0:T(8,128)(2,1)S(1)}, u32[]{:S(2)}, u32[]{:S(2)}) collective-permute-start(bf16[384,640]{1,0:T(8,128)(2,1)S(1)} %add_convert_fusion), channel_id=1, source_target_pairs={{0,1},{1,0},{2,3},{3,2},{4,5},{5,4},{6,7},{7,6},{8,9},{9,8},{10,11... | collective-permute-start | bytes 1474568 | tf_op jit(solution)/shard_map/ppermute | solution.py:462
  114.7 18.1 %collective-permute-start.11 = (bf16[2,384,384]{2,1,0:T(8,128)(2,1)S(1)}, bf16[2,384,384]{2,1,0:T(8,128)(2,1)S(1)}, u32[]{:S(2)}, u32[]{:S(2)}) collective-permute-start(bf16[2,384,384]{2,1,0:T(8,128)(2,1)S(1)} %get-tuple-element.112), channel_id=1, source_target_pairs={{0,8},{8,0},{16,24},{24,16},{1,9},{9,1},{17,25},{25,17},{2,10},{10... | collective-permute-start | bytes 1769480 | tf_op jit(solution)/shard_map/ppermute | solution.py:446
  114.7 18.0 %collective-permute-start.12 = (bf16[2,384,384]{2,1,0:T(8,128)(2,1)S(1)}, bf16[2,384,384]{2,1,0:T(8,128)(2,1)S(1)}, u32[]{:S(2)}, u32[]{:S(2)}) collective-permute-start(bf16[2,384,384]{2,1,0:T(8,128)(2,1)S(1)} %get-tuple-element.113), channel_id=1, source_target_pairs={{0,0},{24,24},{8,16},{16,8},{1,1},{25,25},{9,17},{17,9},{2,2},{26,... | collective-permute-start | bytes 1769480 | tf_op jit(solution)/shard_map/ppermute | solution.py:446
  118.5 14.3 %collective-permute-start.17 = (bf16[384,384]{1,0:T(8,128)(2,1)S(1)}, bf16[384,384]{1,0:T(8,128)(2,1)S(1)}, u32[]{:S(2)}, u32[]{:S(2)}) collective-permute-start(bf16[384,384]{1,0:T(8,128)(2,1)S(1)} %get-tuple-element.130), channel_id=1, source_target_pairs={{0,1},{1,0},{2,3},{3,2},{4,5},{5,4},{6,7},{7,6},{8,9},{9,8},{10,11... | collective-permute-start | bytes 884744 | tf_op jit(solution)/shard_map/ppermute | solution.py:446
  119.7 13.0 %collective-permute-start.18 = (bf16[384,384]{1,0:T(8,128)(2,1)S(1)}, bf16[384,384]{1,0:T(8,128)(2,1)S(1)}, u32[]{:S(2)}, u32[]{:S(2)}) collective-permute-start(bf16[384,384]{1,0:T(8,128)(2,1)S(1)} %get-tuple-element.131), channel_id=1, source_target_pairs={{0,0},{7,7},{1,2},{2,1},{3,4},{4,3},{5,6},{6,5},{8,8},{15,15},{9,1... | collective-permute-start | bytes 884744 | tf_op jit(solution)/shard_map/ppermute | solution.py:446

commit v5 on v4

--- a/solution.py
+++ b/solution.py
@@ -376,6 +376,8 @@
     partner = [(i, i ^ 1) for i in range(rows)]
     onward = [(i, (i + 2) % rows) for i in range(0, rows, 2)]
     onward += [(i, (i - 2) % rows) for i in range(1, rows, 2)]
+    onward_open = [(i, i + 2) for i in range(0, rows - 2, 2)]
+    onward_open += [(i, i - 2) for i in range(3, rows, 2)]
     homeward = [(i + 2, i) for i in range(0, rows - 2, 2)]
     homeward += [(i, i + 2) for i in range(1, rows - 2, 2)]
     homeward += [(0, 1), (rows - 1, rows - 2)]
@@ -455,7 +457,8 @@
             backs[earlier][name] = joined
 
     def hand_on(c):
-        outers[c] = lax.ppermute(after(theirs[c], *done[-1:]), "space", onward)
+        chain = onward_open if c == last else onward
+        outers[c] = lax.ppermute(after(theirs[c], *done[-1:]), "space", chain)
 
     def send_back(c):
         total = sums[c]["q2"] + after(backs[c]["q0"], *done[-1:]).astype(F32)

time: 135 us -> 132 us (0.978)
  the two profiles are of different devices: /device:TPU:9 before, /device:TPU:0 now
where the time goes in v5:
time: 132 us; the launch traced here: 131 us
  Pallas kernels  68.7 us (52%)
  starting transfers between devices  38.1 us (29%)
  waiting for transfers between devices  23.5 us (18%)
    pallas_call x10, Pallas kernels, run_stage(): pl.pallas_call(functools.partial(stage_kernel, work, names, head_width **...  56.7 us
    ppermute x8, starting transfers between devices, stage(): backs[c][name] = lax.ppermute(sums[c][name], axis, pairs)  22.2 us
    ppermute x8, waiting for transfers between devices, stage(): backs[c][name] = lax.ppermute(sums[c][name], axis, pairs)  14.7 us
    pallas_call x2, Pallas kernels, prep(): pl.pallas_call(functools.partial(prep_kernel, counts, *sizes), grid_spec=...  6.21 us
    ppermute x3, starting transfers between devices, hand_on(): outers[c] = lax.ppermute(after(theirs[c], *done[-1:]), 'space', chain)  6.02 us
    ppermute x2, waiting for transfers between devices, per_device(): theirs[c] = lax.ppermute(mine[c], 'space', partner)  4.9 us
    pallas_call x3, Pallas kernels, finish(): pl.pallas_call(functools.partial(finish_kernel, head_width ** (-0.5), len...  4.05 us
  transfers between devices with their start and end apart: 19, of which 6 were waited for; matrix products, arithmetic and copies ran while one was open for 0% of the time, Pallas kernels for 50%

profile of v5, /device:TPU:0, one launch (start us, length us, event | category | flops | bytes accessed | tf_op | source)
XLA Modules:
  0.0 131.4 jit_solution(11066805852605206074)
XLA Ops:
  0.7 1.8 %pack.1.refs_1_.refs_3_.refs_2_ = bf16[2,384,1536]{2,1,0:T(8,128)(2,1)S(1)} custom-call(bf16[384,1536]{1,0:T(8,128)(2,1)} %bitcast.26, bf16[384,1536]{1,0:T(8,128)(2,1)} %bitcast.27), custom_call_target="tpu_custom_call" | custom-call | bytes 4718592 | tf_op jit(solution)/shard_map/pack/pallas_call | solution.py:157
  2.4 0.5 collective-permute-start.2
  3.0 2.2 %prep.2.refs_0_.refs_1_ = bf16[784,512]{1,0:T(8,128)(2,1)S(1)} custom-call(s32[1]{0:T(128)} %bitcast.1.frame_ref, s32[1]{0:T(128)} %bitcast.2.row_ref, s32[9]{0:T(128)S(1)} %bitcast.15, bf16[384,1536]{1,0:T(8,128)(2,1)} %bitcast.20, bf16[384,1536]{1,0:T(8,128)(2,1)} %bitcast.22, bf16[384,1536]{1,0:T(8,128)(2,1)} %bitcast.24, f32[12,1,384]{2,1,0:T(1,128)S(1)} %bitcast.13), custom_call_target="tpu_custom_call" | custom-call | flops 393216 | bytes 1966080 | tf_op jit(solution)/shard_map/prep/pallas_call | solution.py:122
  5.2 2.6 %collective-permute-start.1 = (bf16[784,512]{1,0:T(8,128)(2,1)S(1)}, bf16[784,512]{1,0:T(8,128)(2,1)}, u32[]{:S(2)}, u32[]{:S(2)}) collective-permute-start(bf16[784,512]{1,0:T(8,128)(2,1)S(1)} %prep.2.refs_0_.refs_1_), channel_id=1, source_target_pairs={{0,1},{1,0},{2,3},{3,2},{4,5},{5,4},{6,7},{7,6},{8,9},{9,8},{10,11... | collective-permute-start | bytes 2408456 | tf_op jit(solution)/shard_map/ppermute | solution.py:406
  7.8 2.1 %collective-permute-start.4 = (bf16[2,384,1536]{2,1,0:T(8,128)(2,1)S(1)}, bf16[2,384,1536]{2,1,0:T(8,128)(2,1)}, u32[]{:S(2)}, u32[]{:S(2)}) collective-permute-start(bf16[2,384,1536]{2,1,0:T(8,128)(2,1)S(1)} %pack.1.refs_1_.refs_3_.refs_2_), channel_id=1, source_target_pairs={{0,0},{24,24},{8,16},{16,8},{1,1},{25,25},{9,17},{17,9},{2,2},{26,... | collective-permute-start | bytes 7077896 | tf_op jit(solution)/shard_map/ppermute | solution.py:407
  9.9 4.0 %prep.3 = (bf16[784,640]{1,0:T(8,128)(2,1)}, bf16[784,384]{1,0:T(8,128)(2,1)}) custom-call(s32[1]{0:T(128)} %bitcast.1.frame_ref, s32[1]{0:T(128)} %bitcast.2.row_ref, s32[9]{0:T(128)S(1)} %bitcast.16, bf16[384,1536]{1,0:T(8,128)(2,1)} %bitcast.21, bf16[384,1536]{1,0:T(8,128)(2,1)} %bitcast.23, bf16[384,1536]{1,0:T(8,128)(2,1)} %bitcast.25, ...), custom_call_target="tpu_custom_call" | custom-call | flops 786432 | bytes 3932160 | tf_op jit(solution)/shard_map/prep/pallas_call | solution.py:122
  13.9 0.0 collective-permute-start.6
  13.9 2.0 %collective-permute-start = (bf16[784,384]{1,0:T(8,128)(2,1)}, bf16[784,384]{1,0:T(8,128)(2,1)}, u32[]{:S(2)}, u32[]{:S(2)}) collective-permute-start(bf16[784,384]{1,0:T(8,128)(2,1)} %get-tuple-element.79.refs_0_.refs_1_), channel_id=1, source_target_pairs={{0,1},{1,0},{2,3},{3,2},{4,5},{5,4},{6,7},{7,6},{8,9},{9,8},{10,11... | collective-permute-start | bytes 1806344 | tf_op jit(solution)/shard_map/ppermute | solution.py:479
  15.9 0.0 collective-permute-done.2.refs_2_.refs_4_.refs_3_
  15.9 5.6 %pairs.10 = (f32[384,512]{1,0:T(8,128)S(1)}, f32[2,384,512]{2,1,0:T(8,128)S(1)}, f32[2,384,512]{2,1,0:T(8,128)S(1)}) custom-call(s32[1]{0:T(128)} %bitcast.far_ref, bf16[784,512]{1,0:T(8,128)(2,1)S(1)} %prep.2.refs_0_.refs_1_, bf16[2,384,1536]{2,1,0:T(8,128)(2,1)S(1)} %pack.1.refs_1_.refs_3_.refs_2_, ...), custom_call_target="tpu_custom_call" | custom-call | flops 9059696640 | bytes 3932160 | tf_op jit(solution)/shard_map/pairs/pallas_call | solution.py:300
  21.5 6.5 %pairs.11 = (f32[384,640]{1,0:T(8,128)S(1)}, f32[2,384,640]{2,1,0:T(8,128)S(1)}, f32[2,384,640]{2,1,0:T(8,128)S(1)}) custom-call(s32[1]{0:T(128)} %bitcast.far_ref, bf16[784,640]{1,0:T(8,128)(2,1)} %get-tuple-element.81.refs_0_, bf16[2,384,1536]{2,1,0:T(8,128)(2,1)S(1)} %pack.1.refs_1_.refs_3_.refs_2_, ...), custom_call_target="tpu_custom_call" | custom-call | flops 11324620800 | bytes 4915200 | tf_op jit(solution)/shard_map/pairs/pallas_call | solution.py:300
  28.0 0.0 collective-permute-done.1.refs_0_.refs_2_
  28.0 1.6 %collective-permute-start.3 = (bf16[784,512]{1,0:T(8,128)(2,1)}, bf16[784,512]{1,0:T(8,128)(2,1)S(1)}, u32[]{:S(2)}, u32[]{:S(2)}) collective-permute-start(bf16[784,512]{1,0:T(8,128)(2,1)} %collective-permute-done.1.refs_0_.refs_2_), channel_id=1, source_target_pairs={{0,2},{2,4},{4,6},{6,0},{1,7},{3,1},{5,3},{7,5},{8,10},{10,12},{12... | collective-permute-start | bytes 2408456 | tf_op jit(solution)/shard_map/ppermute | solution.py:461
  29.6 5.8 %pairs.12 = (f32[384,512]{1,0:T(8,128)S(1)}, f32[2,384,512]{2,1,0:T(8,128)S(1)}, f32[2,384,512]{2,1,0:T(8,128)S(1)}) custom-call(s32[1]{0:T(128)} %bitcast.far_ref, bf16[784,512]{1,0:T(8,128)(2,1)} %collective-permute-done.1.refs_0_.refs_2_, bf16[2,384,1536]{2,1,0:T(8,128)(2,1)S(1)} %pack.1.refs_1_.refs_3_.refs_2_, ...), custom_call_target="tpu_custom_call" | custom-call | flops 9059696640 | bytes 3932160 | tf_op jit(solution)/shard_map/pairs/pallas_call | solution.py:300
  35.4 4.3 %pairs.13 = (f32[384,384]{1,0:T(8,128)S(1)}, f32[2,384,384]{2,1,0:T(8,128)S(1)}, f32[2,384,384]{2,1,0:T(8,128)S(1)}) custom-call(s32[1]{0:T(128)} %bitcast.far_ref, bf16[784,384]{1,0:T(8,128)(2,1)} %get-tuple-element.79.refs_0_.refs_1_, bf16[2,384,1536]{2,1,0:T(8,128)(2,1)S(1)} %pack.1.refs_1_.refs_3_.refs_2_, ...), custom_call_target="tpu_custom_call" | custom-call | flops 27179089920 | bytes 2949120 | tf_op jit(solution)/shard_map/pairs/pallas_call | solution.py:300
  39.7 0.0 collective-permute-done.4.refs_1_.refs_5_.refs_4_.refs_3_
  39.7 3.5 %pairs.14 = (f32[384,640]{1,0:T(8,128)S(1)}, f32[2,384,640]{2,1,0:T(8,128)S(1)}) custom-call(s32[1]{0:T(128)} %bitcast.far_ref, bf16[784,640]{1,0:T(8,128)(2,1)} %get-tuple-element.81.refs_0_, bf16[2,384,1536]{2,1,0:T(8,128)(2,1)} %collective-permute-done.4.refs_1_.refs_5_.refs_4_.refs_3_, f32[384,640]{1,0:T(8,128)S(1)} %get-tuple-element.83.refs_2_), custom_call_target="tpu_custom_call" | custom-call | flops 5662310400 | bytes 4915200 | tf_op jit(solution)/shard_map/pairs/pallas_call | solution.py:300
  43.2 4.9 %collective-permute-done.6.refs_0_.refs_1_ = bf16[784,640]{1,0:T(8,128)(2,1)} collective-permute-done((bf16[784,640]{1,0:T(8,128)(2,1)}, bf16[784,640]{1,0:T(8,128)(2,1)}, u32[]{:S(2)}, u32[]{:S(2)}) %collective-permute-start.6) | collective-permute-done | bytes 1003552 | tf_op jit(solution)/shard_map/ppermute | solution.py:479
  48.1 2.0 %collective-permute-start.7 = (bf16[784,640]{1,0:T(8,128)(2,1)}, bf16[784,640]{1,0:T(8,128)(2,1)S(1)}, u32[]{:S(2)}, u32[]{:S(2)}) collective-permute-start(bf16[784,640]{1,0:T(8,128)(2,1)} %collective-permute-done.6.refs_0_.refs_1_), channel_id=1, source_target_pairs={{0,2},{2,4},{4,6},{6,0},{1,7},{3,1},{5,3},{7,5},{8,10},{10,12},{12... | collective-permute-start | bytes 3010568 | tf_op jit(solution)/shard_map/ppermute | solution.py:461
  50.2 0.7 collective-permute-done.3.refs_0_
  50.8 6.9 %pairs.15 = (bf16[384,512]{1,0:T(8,128)(2,1)S(1)}, f32[384,512]{1,0:T(8,128)S(1)}, f32[384,512]{1,0:T(8,128)S(1)}, f32[2,384,512]{2,1,0:T(8,128)S(1)}, bf16[2,38...) custom-call(s32[1]{0:T(128)} %bitcast.far_ref, bf16[784,512]{1,0:T(8,128)(2,1)S(1)} %collective-permute-done.3.refs_0_, ...), custom_call_target="tpu_custom_call" | custom-call | flops 22649241600 | bytes 3932160 | tf_op jit(solution)/shard_map/pairs/pallas_call | solution.py:300
  57.7 2.9 %collective-permute-start.8 = (bf16[384,512]{1,0:T(8,128)(2,1)S(1)}, bf16[384,512]{1,0:T(8,128)(2,1)S(1)}, u32[]{:S(2)}, u32[]{:S(2)}) collective-permute-start(bf16[384,512]{1,0:T(8,128)(2,1)S(1)} %get-tuple-element.104), channel_id=1, source_target_pairs={{2,0},{4,2},{6,4},{1,3},{3,5},{5,7},{0,1},{7,6},{10,8},{12,10},{14... | collective-permute-start | bytes 1179656 | tf_op jit(solution)/shard_map/ppermute | solution.py:448
  60.7 4.3 %collective-permute-start.10 = (bf16[2,384,512]{2,1,0:T(8,128)(2,1)S(1)}, bf16[2,384,512]{2,1,0:T(8,128)(2,1)S(1)}, u32[]{:S(2)}, u32[]{:S(2)}) collective-permute-start(bf16[2,384,512]{2,1,0:T(8,128)(2,1)S(1)} %get-tuple-element.106), channel_id=1, source_target_pairs={{0,8},{8,0},{16,24},{24,16},{1,9},{9,1},{17,25},{25,17},{2,10},{10... | collective-permute-start | bytes 2359304 | tf_op jit(solution)/shard_map/ppermute | solution.py:448
  64.9 2.4 %collective-permute-start.5 = (bf16[784,384]{1,0:T(8,128)(2,1)}, bf16[784,384]{1,0:T(8,128)(2,1)S(1)}, u32[]{:S(2)}, u32[]{:S(2)}) collective-permute-start(bf16[784,384]{1,0:T(8,128)(2,1)} %collective-permute-done.refs_0_), channel_id=1, source_target_pairs={{0,2},{2,4},{4,6},{3,1},{5,3},{7,5},{8,10},{10,12},{12,14},{11,9},... | collective-permute-start | bytes 1806344 | tf_op jit(solution)/shard_map/ppermute | solution.py:461
  67.3 6.7 %pairs.16 = (f32[384,640]{1,0:T(8,128)S(1)}, f32[2,384,640]{2,1,0:T(8,128)S(1)}, f32[2,384,640]{2,1,0:T(8,128)S(1)}) custom-call(s32[1]{0:T(128)} %bitcast.far_ref, bf16[784,640]{1,0:T(8,128)(2,1)} %collective-permute-done.6.refs_0_.refs_1_, bf16[2,384,1536]{2,1,0:T(8,128)(2,1)S(1)} %pack.1.refs_1_.refs_3_.refs_2_, ...), custom_call_target="tpu_custom_call" | custom-call | flops 5662310400 | bytes 4915200 | tf_op jit(solution)/shard_map/pairs/pallas_call | solution.py:300
  74.0 1.5 %collective-permute-done.7.refs_0_ = bf16[784,640]{1,0:T(8,128)(2,1)S(1)} collective-permute-done((bf16[784,640]{1,0:T(8,128)(2,1)}, bf16[784,640]{1,0:T(8,128)(2,1)S(1)}, u32[]{:S(2)}, u32[]{:S(2)}) %collective-permute-start.7) | collective-permute-done | bytes 1003552 | tf_op jit(solution)/shard_map/ppermute | solution.py:461
  75.5 7.7 %pairs.17 = (bf16[384,640]{1,0:T(8,128)(2,1)S(1)}, f32[384,640]{1,0:T(8,128)S(1)}, f32[2,384,640]{2,1,0:T(8,128)S(1)}, bf16[2,384,640]{2,1,0:T(8,128)(2,1)S(1)}, bf16[2,384,1152]{2,1,0:T(8,128)(2,1)S(1)}) custom-call(s32[1]{0:T(128)} %bitcast.far_ref, bf16[784,640]{1,0:T(8,128)(2,1)S(1)} %collective-permute-done.7.refs_0_, ...), custom_call_target="tpu_custom_call", output_to_operand_aliasing={{4}: (10, {})} | custom-call | flops 22649241600 | bytes 4915200 | tf_op jit(solution)/shard_map/pairs/pallas_call | solution.py:300
  83.3 1.2 collective-permute-start.15
  84.5 0.0 collective-permute-done.8
  84.5 0.1 add_convert_fusion.1
  84.7 0.3 collective-permute-start.9
  85.0 4.7 %pairs.18 = (bf16[384,384]{1,0:T(8,128)(2,1)S(1)}, f32[2,384,384]{2,1,0:T(8,128)S(1)}, f32[2,384,384]{2,1,0:T(8,128)S(1)}, f32[2,384,384]{2,1,0:T(8,128)S(1)}) custom-call(s32[1]{0:T(128)} %bitcast.far_ref, bf16[784,384]{1,0:T(8,128)(2,1)} %collective-permute-done.refs_0_, bf16[2,384,1536]{2,1,0:T(8,128)(2,1)S(1)} %pack.1.refs_1_.refs_3_.refs_2_, ...), custom_call_target="tpu_custom_call" | custom-call | flops 20384317440 | bytes 2949120 | tf_op jit(solution)/shard_map/pairs/pallas_call | solution.py:300
  89.7 0.8 collective-permute-start.14
  90.5 4.9 %collective-permute-done.15 = bf16[384,640]{1,0:T(8,128)(2,1)S(1)} collective-permute-done((bf16[384,640]{1,0:T(8,128)(2,1)S(1)}, bf16[384,640]{1,0:T(8,128)(2,1)S(1)}, u32[]{:S(2)}, u32[]{:S(2)}) %collective-permute-start.15) | collective-permute-done | bytes 491552 | tf_op jit(solution)/shard_map/ppermute | solution.py:448
  95.4 4.6 %collective-permute-start.13 = (bf16[2,384,640]{2,1,0:T(8,128)(2,1)S(1)}, bf16[2,384,640]{2,1,0:T(8,128)(2,1)S(1)}, u32[]{:S(2)}, u32[]{:S(2)}) collective-permute-start(bf16[2,384,640]{2,1,0:T(8,128)(2,1)S(1)} %get-tuple-element.115), channel_id=1, source_target_pairs={{0,8},{8,0},{16,24},{24,16},{1,9},{9,1},{17,25},{25,17},{2,10},{10... | collective-permute-start | bytes 2949128 | tf_op jit(solution)/shard_map/ppermute | solution.py:448
  100.0 0.1 add_convert_fusion
  100.1 0.0 collective-permute-done.5.refs_0_
  100.1 1.6 %collective-permute-start.16 = (bf16[384,640]{1,0:T(8,128)(2,1)S(1)}, bf16[384,640]{1,0:T(8,128)(2,1)S(1)}, u32[]{:S(2)}, u32[]{:S(2)}) collective-permute-start(bf16[384,640]{1,0:T(8,128)(2,1)S(1)} %add_convert_fusion), channel_id=1, source_target_pairs={{0,1},{1,0},{2,3},{3,2},{4,5},{5,4},{6,7},{7,6},{8,9},{9,8},{10,11... | collective-permute-start | bytes 1474568 | tf_op jit(solution)/shard_map/ppermute | solution.py:465
  101.7 1.7 %collective-permute-done.9.rest_0_ = bf16[384,512]{1,0:T(8,128)(2,1)S(1)} collective-permute-done((bf16[384,512]{1,0:T(8,128)(2,1)S(1)}, bf16[384,512]{1,0:T(8,128)(2,1)S(1)}, u32[]{:S(2)}, u32[]{:S(2)}) %collective-permute-start.9) | collective-permute-done | bytes 393248 | tf_op jit(solution)/shard_map/ppermute | solution.py:465
  103.4 5.0 %pairs.19 = (bf16[384,384]{1,0:T(8,128)(2,1)S(1)}, f32[384,384]{1,0:T(8,128)S(1)}, f32[2,384,384]{2,1,0:T(8,128)S(1)}, bf16[2,384,384]{2,1,0:T(8,128)(2,1)S(1)}, bf16[2,384,384]{2,1,0:T(8,128)(2,1)S(1)}) custom-call(s32[1]{0:T(128)} %bitcast.far_ref, bf16[784,384]{1,0:T(8,128)(2,1)S(1)} %collective-permute-done.5.refs_0_, ...), custom_call_target="tpu_custom_call" | custom-call | flops 13589544960 | bytes 2949120 | tf_op jit(solution)/shard_map/pairs/pallas_call | solution.py:300
  108.4 5.2 %collective-permute-start.11 = (bf16[2,384,384]{2,1,0:T(8,128)(2,1)S(1)}, bf16[2,384,384]{2,1,0:T(8,128)(2,1)S(1)}, u32[]{:S(2)}, u32[]{:S(2)}) collective-permute-start(bf16[2,384,384]{2,1,0:T(8,128)(2,1)S(1)} %get-tuple-element.112), channel_id=1, source_target_pairs={{0,8},{8,0},{16,24},{24,16},{1,9},{9,1},{17,25},{25,17},{2,10},{10... | collective-permute-start | bytes 1769480 | tf_op jit(solution)/shard_map/ppermute | solution.py:448
  113.7 0.7 collective-permute-start.12
  114.4 2.5 %collective-permute-start.17 = (bf16[384,384]{1,0:T(8,128)(2,1)S(1)}, bf16[384,384]{1,0:T(8,128)(2,1)S(1)}, u32[]{:S(2)}, u32[]{:S(2)}) collective-permute-start(bf16[384,384]{1,0:T(8,128)(2,1)S(1)} %get-tuple-element.130), channel_id=1, source_target_pairs={{0,1},{1,0},{2,3},{3,2},{4,5},{5,4},{6,7},{7,6},{8,9},{9,8},{10,11... | collective-permute-start | bytes 884744 | tf_op jit(solution)/shard_map/ppermute | solution.py:448
  116.9 0.7 collective-permute-start.18
  117.6 1.3 finish.3
  118.9 1.7 %finish.4 = (bf16[384,1536]{1,0:T(8,128)(2,1)}, bf16[384,1536]{1,0:T(8,128)(2,1)}, bf16[384,1536]{1,0:T(8,128)(2,1)}) custom-call(f32[2,384,640]{2,1,0:T(8,128)S(1)} %get-tuple-element.99.own_kv, bf16[2,384,640]{2,1,0:T(8,128)(2,1)S(1)} %collective-permute-done.13.near, ...), custom_call_target="tpu_custom_call", output_to_operand_aliasing={{0}: (5, {}), {1}: (6, {}), {2}: (7, {})} | custom-call | flops 1966080 | bytes 7372800 | tf_op jit(solution)/shard_map/finish/pallas_call | solution.py:349
  120.6 9.8 %collective-permute-done.17.rest_0_ = bf16[384,384]{1,0:T(8,128)(2,1)S(1)} collective-permute-done((bf16[384,384]{1,0:T(8,128)(2,1)S(1)}, bf16[384,384]{1,0:T(8,128)(2,1)S(1)}, u32[]{:S(2)}, u32[]{:S(2)}) %collective-permute-start.17) | collective-permute-done | bytes 294944 | tf_op jit(solution)/shard_map/ppermute | solution.py:448
  130.4 1.0 finish.5
  (12 shorter events, 0.0 us)
Async XLA Ops:
  0.6 2.3 %copy-start = (f32[1,1,12,384]{3,1,2,0:T(1,128)S(1)}, f32[1,1,12,384]{3,1,2,0:T(1,128)}, u32[]{:S(2)}) copy-start(f32[1,1,12,384]{3,1,2,0:T(1,128)} %param.12) | copy-start | bytes 55300
  0.6 2.3 %copy-start.1 = (s32[1,1,9]{2,1,0:T(1,128)S(1)}, s32[1,1,9]{2,1,0:T(1,128)}, u32[]{:S(2)}) copy-start(s32[1,1,9]{2,1,0:T(1,128)} %param.13) | copy-start | bytes 112
  2.4 13.4 %collective-permute-start.2 = (bf16[2,384,1536]{2,1,0:T(8,128)(2,1)S(1)}, bf16[2,384,1536]{2,1,0:T(8,128)(2,1)}, u32[]{:S(2)}, u32[]{:S(2)}) collective-permute-start(bf16[2,384,1536]{2,1,0:T(8,128)(2,1)S(1)} %pack.1.refs_1_.refs_3_.refs_2_), channel_id=1, source_target_pairs={{0,8},{8,0},{16,24},{24,16},{1,9},{9,1},{17,25},{25,17},{2,10},{10... | collective-permute-start | bytes 7077896 | tf_op jit(solution)/shard_map/ppermute | solution.py:401
  5.2 22.8 %collective-permute-start.1 = (bf16[784,512]{1,0:T(8,128)(2,1)S(1)}, bf16[784,512]{1,0:T(8,128)(2,1)}, u32[]{:S(2)}, u32[]{:S(2)}) collective-permute-start(bf16[784,512]{1,0:T(8,128)(2,1)S(1)} %prep.2.refs_0_.refs_1_), channel_id=1, source_target_pairs={{0,1},{1,0},{2,3},{3,2},{4,5},{5,4},{6,7},{7,6},{8,9},{9,8},{10,11... | collective-permute-start | bytes 2408456 | tf_op jit(solution)/shard_map/ppermute | solution.py:406
  7.8 31.9 %collective-permute-start.4 = (bf16[2,384,1536]{2,1,0:T(8,128)(2,1)S(1)}, bf16[2,384,1536]{2,1,0:T(8,128)(2,1)}, u32[]{:S(2)}, u32[]{:S(2)}) collective-permute-start(bf16[2,384,1536]{2,1,0:T(8,128)(2,1)S(1)} %pack.1.refs_1_.refs_3_.refs_2_), channel_id=1, source_target_pairs={{0,0},{24,24},{8,16},{16,8},{1,1},{25,25},{9,17},{17,9},{2,2},{26,... | collective-permute-start | bytes 7077896 | tf_op jit(solution)/shard_map/ppermute | solution.py:407
  13.9 34.3 %collective-permute-start.6 = (bf16[784,640]{1,0:T(8,128)(2,1)}, bf16[784,640]{1,0:T(8,128)(2,1)}, u32[]{:S(2)}, u32[]{:S(2)}) collective-permute-start(bf16[784,640]{1,0:T(8,128)(2,1)} %get-tuple-element.81.refs_0_), channel_id=1, source_target_pairs={{0,1},{1,0},{2,3},{3,2},{4,5},{5,4},{6,7},{7,6},{8,9},{9,8},{10,11... | collective-permute-start | bytes 3010568 | tf_op jit(solution)/shard_map/ppermute | solution.py:479
  13.9 51.0 %collective-permute-start = (bf16[784,384]{1,0:T(8,128)(2,1)}, bf16[784,384]{1,0:T(8,128)(2,1)}, u32[]{:S(2)}, u32[]{:S(2)}) collective-permute-start(bf16[784,384]{1,0:T(8,128)(2,1)} %get-tuple-element.79.refs_0_.refs_1_), channel_id=1, source_target_pairs={{0,1},{1,0},{2,3},{3,2},{4,5},{5,4},{6,7},{7,6},{8,9},{9,8},{10,11... | collective-permute-start | bytes 1806344 | tf_op jit(solution)/shard_map/ppermute | solution.py:479
  28.0 22.8 %collective-permute-start.3 = (bf16[784,512]{1,0:T(8,128)(2,1)}, bf16[784,512]{1,0:T(8,128)(2,1)S(1)}, u32[]{:S(2)}, u32[]{:S(2)}) collective-permute-start(bf16[784,512]{1,0:T(8,128)(2,1)} %collective-permute-done.1.refs_0_.refs_2_), channel_id=1, source_target_pairs={{0,2},{2,4},{4,6},{6,0},{1,7},{3,1},{5,3},{7,5},{8,10},{10,12},{12... | collective-permute-start | bytes 2408456 | tf_op jit(solution)/shard_map/ppermute | solution.py:461
  48.1 27.4 %collective-permute-start.7 = (bf16[784,640]{1,0:T(8,128)(2,1)}, bf16[784,640]{1,0:T(8,128)(2,1)S(1)}, u32[]{:S(2)}, u32[]{:S(2)}) collective-permute-start(bf16[784,640]{1,0:T(8,128)(2,1)} %collective-permute-done.6.refs_0_.refs_1_), channel_id=1, source_target_pairs={{0,2},{2,4},{4,6},{6,0},{1,7},{3,1},{5,3},{7,5},{8,10},{10,12},{12... | collective-permute-start | bytes 3010568 | tf_op jit(solution)/shard_map/ppermute | solution.py:461
  57.7 26.8 %collective-permute-start.8 = (bf16[384,512]{1,0:T(8,128)(2,1)S(1)}, bf16[384,512]{1,0:T(8,128)(2,1)S(1)}, u32[]{:S(2)}, u32[]{:S(2)}) collective-permute-start(bf16[384,512]{1,0:T(8,128)(2,1)S(1)} %get-tuple-element.104), channel_id=1, source_target_pairs={{2,0},{4,2},{6,4},{1,3},{3,5},{5,7},{0,1},{7,6},{10,8},{12,10},{14... | collective-permute-start | bytes 1179656 | tf_op jit(solution)/shard_map/ppermute | solution.py:448
  60.7 41.1 %collective-permute-start.10 = (bf16[2,384,512]{2,1,0:T(8,128)(2,1)S(1)}, bf16[2,384,512]{2,1,0:T(8,128)(2,1)S(1)}, u32[]{:S(2)}, u32[]{:S(2)}) collective-permute-start(bf16[2,384,512]{2,1,0:T(8,128)(2,1)S(1)} %get-tuple-element.106), channel_id=1, source_target_pairs={{0,8},{8,0},{16,24},{24,16},{1,9},{9,1},{17,25},{25,17},{2,10},{10... | collective-permute-start | bytes 2359304 | tf_op jit(solution)/shard_map/ppermute | solution.py:448
  64.9 35.2 %collective-permute-start.5 = (bf16[784,384]{1,0:T(8,128)(2,1)}, bf16[784,384]{1,0:T(8,128)(2,1)S(1)}, u32[]{:S(2)}, u32[]{:S(2)}) collective-permute-start(bf16[784,384]{1,0:T(8,128)(2,1)} %collective-permute-done.refs_0_), channel_id=1, source_target_pairs={{0,2},{2,4},{4,6},{3,1},{5,3},{7,5},{8,10},{10,12},{12,14},{11,9},... | collective-permute-start | bytes 1806344 | tf_op jit(solution)/shard_map/ppermute | solution.py:461
  83.3 12.1 %collective-permute-start.15 = (bf16[384,640]{1,0:T(8,128)(2,1)S(1)}, bf16[384,640]{1,0:T(8,128)(2,1)S(1)}, u32[]{:S(2)}, u32[]{:S(2)}) collective-permute-start(bf16[384,640]{1,0:T(8,128)(2,1)S(1)} %get-tuple-element.124), channel_id=1, source_target_pairs={{2,0},{4,2},{6,4},{1,3},{3,5},{5,7},{0,1},{7,6},{10,8},{12,10},{14... | collective-permute-start | bytes 1474568 | tf_op jit(solution)/shard_map/ppermute | solution.py:448
  84.7 18.8 %collective-permute-start.9 = (bf16[384,512]{1,0:T(8,128)(2,1)S(1)}, bf16[384,512]{1,0:T(8,128)(2,1)S(1)}, u32[]{:S(2)}, u32[]{:S(2)}) collective-permute-start(bf16[384,512]{1,0:T(8,128)(2,1)S(1)} %add_convert_fusion.1), channel_id=1, source_target_pairs={{0,1},{1,0},{2,3},{3,2},{4,5},{5,4},{6,7},{7,6},{8,9},{9,8},{10,11... | collective-permute-start | bytes 1179656 | tf_op jit(solution)/shard_map/ppermute | solution.py:465
  89.7 27.2 %collective-permute-start.14 = (bf16[2,384,1152]{2,1,0:T(8,128)(2,1)S(1)}, bf16[2,384,1152]{2,1,0:T(8,128)(2,1)S(1)}, u32[]{:S(2)}, u32[]{:S(2)}) collective-permute-start(bf16[2,384,1152]{2,1,0:T(8,128)(2,1)S(1)} %get-tuple-element.117), channel_id=1, source_target_pairs={{0,0},{24,24},{8,16},{16,8},{1,1},{25,25},{9,17},{17,9},{2,2},{26,... | collective-permute-start | bytes 5308424 | tf_op jit(solution)/shard_map/ppermute | solution.py:455
  95.4 23.5 %collective-permute-start.13 = (bf16[2,384,640]{2,1,0:T(8,128)(2,1)S(1)}, bf16[2,384,640]{2,1,0:T(8,128)(2,1)S(1)}, u32[]{:S(2)}, u32[]{:S(2)}) collective-permute-start(bf16[2,384,640]{2,1,0:T(8,128)(2,1)S(1)} %get-tuple-element.115), channel_id=1, source_target_pairs={{0,8},{8,0},{16,24},{24,16},{1,9},{9,1},{17,25},{25,17},{2,10},{10... | collective-permute-start | bytes 2949128 | tf_op jit(solution)/shard_map/ppermute | solution.py:448
  100.1 14.2 %collective-permute-start.16 = (bf16[384,640]{1,0:T(8,128)(2,1)S(1)}, bf16[384,640]{1,0:T(8,128)(2,1)S(1)}, u32[]{:S(2)}, u32[]{:S(2)}) collective-permute-start(bf16[384,640]{1,0:T(8,128)(2,1)S(1)} %add_convert_fusion), channel_id=1, source_target_pairs={{0,1},{1,0},{2,3},{3,2},{4,5},{5,4},{6,7},{7,6},{8,9},{9,8},{10,11... | collective-permute-start | bytes 1474568 | tf_op jit(solution)/shard_map/ppermute | solution.py:465
  108.4 21.9 %collective-permute-start.11 = (bf16[2,384,384]{2,1,0:T(8,128)(2,1)S(1)}, bf16[2,384,384]{2,1,0:T(8,128)(2,1)S(1)}, u32[]{:S(2)}, u32[]{:S(2)}) collective-permute-start(bf16[2,384,384]{2,1,0:T(8,128)(2,1)S(1)} %get-tuple-element.112), channel_id=1, source_target_pairs={{0,8},{8,0},{16,24},{24,16},{1,9},{9,1},{17,25},{25,17},{2,10},{10... | collective-permute-start | bytes 1769480 | tf_op jit(solution)/shard_map/ppermute | solution.py:448
  113.7 16.7 %collective-permute-start.12 = (bf16[2,384,384]{2,1,0:T(8,128)(2,1)S(1)}, bf16[2,384,384]{2,1,0:T(8,128)(2,1)S(1)}, u32[]{:S(2)}, u32[]{:S(2)}) collective-permute-start(bf16[2,384,384]{2,1,0:T(8,128)(2,1)S(1)} %get-tuple-element.113), channel_id=1, source_target_pairs={{0,0},{24,24},{8,16},{16,8},{1,1},{25,25},{9,17},{17,9},{2,2},{26,... | collective-permute-start | bytes 1769480 | tf_op jit(solution)/shard_map/ppermute | solution.py:448
  114.4 16.0 %collective-permute-start.17 = (bf16[384,384]{1,0:T(8,128)(2,1)S(1)}, bf16[384,384]{1,0:T(8,128)(2,1)S(1)}, u32[]{:S(2)}, u32[]{:S(2)}) collective-permute-start(bf16[384,384]{1,0:T(8,128)(2,1)S(1)} %get-tuple-element.130), channel_id=1, source_target_pairs={{0,1},{1,0},{2,3},{3,2},{4,5},{5,4},{6,7},{7,6},{8,9},{9,8},{10,11... | collective-permute-start | bytes 884744 | tf_op jit(solution)/shard_map/ppermute | solution.py:448
  116.9 13.4 %collective-permute-start.18 = (bf16[384,384]{1,0:T(8,128)(2,1)S(1)}, bf16[384,384]{1,0:T(8,128)(2,1)S(1)}, u32[]{:S(2)}, u32[]{:S(2)}) collective-permute-start(bf16[384,384]{1,0:T(8,128)(2,1)S(1)} %get-tuple-element.131), channel_id=1, source_target_pairs={{0,0},{7,7},{1,2},{2,1},{3,4},{4,3},{5,6},{6,5},{8,8},{15,15},{9,1... | collective-permute-start | bytes 884744 | tf_op jit(solution)/shard_map/ppermute | solution.py:448

commit v6 on v5

--- a/solution.py
+++ b/solution.py
@@ -33,7 +33,7 @@
     ((HERE, (OUTER,)), (NEAR, (OUTER,)), (FAR, (PARTNER, OUTER))),
 )
 DIRECT = 2
-ORDER = (('stage', 0, 0), ('stage', 1, 0), ('hand', 0), ('stage', 0, 1), ('stage', 2, 0), ('stage', 1, 1), ('hand', 1), ('stage', 0, 2), ('hand', 2), ('stage', 1, 2), ('back', 0), ('stage', 1, 3), ('stage', 2, 1), ('send', 1, 'kv2'), ('back', 1), ('stage', 2, 2, (0, 'q2'), (0, 'kv1')), ('finish', 0), ('finish', 1), ('finish', 2))
+ORDER = (('stage', 0, 0), ('stage', 1, 0), ('hand', 0), ('stage', 0, 1), ('stage', 2, 0), ('stage', 1, 1), ('hand', 1), ('stage', 0, 2), ('hand', 2), ('stage', 1, 2), ('back', 0), ('stage', 1, 3), ('stage', 2, 1), ('back', 1), ('stage', 2, 2, (0, 'q2'), (0, 'kv1')), ('finish', 0), ('finish', 1), ('finish', 2))
 JOINED = ('kv2',)
 WEIGHTS = ((60, 60, 60), (60, 60, 30, 60), (240, 120, 60))
 EXTRA = 16
@@ -380,7 +380,6 @@
     onward_open += [(i, i - 2) for i in range(3, rows, 2)]
     homeward = [(i + 2, i) for i in range(0, rows - 2, 2)]
     homeward += [(i, i + 2) for i in range(1, rows - 2, 2)]
-    homeward += [(0, 1), (rows - 1, rows - 2)]
     owners = [(0, 0), (rows - 1, rows - 1)]
     for i in range(1, rows - 1, 2):
         owners += [(i, i + 1), (i + 1, i)]

time: 132 us -> 131 us (level)
  the two profiles are of different devices: /device:TPU:0 before, /device:TPU:16 now
where the time goes in v6:
time: 131 us
  Pallas kernels  68.7 us (52%)
  starting transfers between devices  41.7 us (32%)
  waiting for transfers between devices  19 us (15%)
    pallas_call x10, Pallas kernels, run_stage(): pl.pallas_call(functools.partial(stage_kernel, work, names, head_width **...  56.7 us
    ppermute x9, starting transfers between devices, stage(): backs[c][name] = lax.ppermute(sums[c][name], axis, pairs)  24.6 us
    ppermute x9, waiting for transfers between devices, stage(): backs[c][name] = lax.ppermute(sums[c][name], axis, pairs)  9.09 us
    ppermute x3, starting transfers between devices, hand_on(): outers[c] = lax.ppermute(after(theirs[c], *done[-1:]), 'space', chain)  6.89 us
    pallas_call x2, Pallas kernels, prep(): pl.pallas_call(functools.partial(prep_kernel, counts, *sizes), grid_spec=...  6.22 us
    ppermute x2, waiting for transfers between devices, per_device(): theirs[c] = lax.ppermute(mine[c], 'space', partner)  5.35 us
    ppermute x2, waiting for transfers between devices, send_back(): backs[c]['q2'] = lax.ppermute(total.astype(BF16), 'space', partner)  4.52 us
    ppermute x2, starting transfers between devices, send_back(): backs[c]['q2'] = lax.ppermute(total.astype(BF16), 'space', partner)  4.48 us
  transfers between devices with their start and end apart: 19, of which 4 were waited for; matrix products, arithmetic and copies ran while one was open for 0% of the time, Pallas kernels for 50%

profile of v6, /device:TPU:16, one launch (start us, length us, event | category | flops | bytes accessed | tf_op | source)
XLA Modules:
  0.0 130.6 jit_solution(1099200089595699748)
XLA Ops:
  0.7 1.8 %pack.1.refs_1_.refs_3_.refs_2_ = bf16[2,384,1536]{2,1,0:T(8,128)(2,1)S(1)} custom-call(bf16[384,1536]{1,0:T(8,128)(2,1)} %bitcast.26, bf16[384,1536]{1,0:T(8,128)(2,1)} %bitcast.27), custom_call_target="tpu_custom_call" | custom-call | bytes 4718592 | tf_op jit(solution)/shard_map/pack/pallas_call | solution.py:157
  2.4 0.1 collective-permute-start.2
  2.6 2.2 %prep.2.refs_0_.refs_1_ = bf16[784,512]{1,0:T(8,128)(2,1)S(1)} custom-call(s32[1]{0:T(128)} %bitcast.1.frame_ref, s32[1]{0:T(128)} %bitcast.2.row_ref, s32[9]{0:T(128)S(1)} %bitcast.15, bf16[384,1536]{1,0:T(8,128)(2,1)} %bitcast.20, bf16[384,1536]{1,0:T(8,128)(2,1)} %bitcast.22, bf16[384,1536]{1,0:T(8,128)(2,1)} %bitcast.24, f32[12,1,384]{2,1,0:T(1,128)S(1)} %bitcast.13), custom_call_target="tpu_custom_call" | custom-call | flops 393216 | bytes 1966080 | tf_op jit(solution)/shard_map/prep/pallas_call | solution.py:122
  4.8 1.6 %collective-permute-start.1 = (bf16[784,512]{1,0:T(8,128)(2,1)S(1)}, bf16[784,512]{1,0:T(8,128)(2,1)}, u32[]{:S(2)}, u32[]{:S(2)}) collective-permute-start(bf16[784,512]{1,0:T(8,128)(2,1)S(1)} %prep.2.refs_0_.refs_1_), channel_id=1, source_target_pairs={{0,1},{1,0},{2,3},{3,2},{4,5},{5,4},{6,7},{7,6},{8,9},{9,8},{10,11... | collective-permute-start | bytes 2408456 | tf_op jit(solution)/shard_map/ppermute | solution.py:405
  6.3 2.1 %collective-permute-start.4 = (bf16[2,384,1536]{2,1,0:T(8,128)(2,1)S(1)}, bf16[2,384,1536]{2,1,0:T(8,128)(2,1)}, u32[]{:S(2)}, u32[]{:S(2)}) collective-permute-start(bf16[2,384,1536]{2,1,0:T(8,128)(2,1)S(1)} %pack.1.refs_1_.refs_3_.refs_2_), channel_id=1, source_target_pairs={{0,0},{24,24},{8,16},{16,8},{1,1},{25,25},{9,17},{17,9},{2,2},{26,... | collective-permute-start | bytes 7077896 | tf_op jit(solution)/shard_map/ppermute | solution.py:406
  8.4 4.0 %prep.3 = (bf16[784,640]{1,0:T(8,128)(2,1)}, bf16[784,384]{1,0:T(8,128)(2,1)}) custom-call(s32[1]{0:T(128)} %bitcast.1.frame_ref, s32[1]{0:T(128)} %bitcast.2.row_ref, s32[9]{0:T(128)S(1)} %bitcast.16, bf16[384,1536]{1,0:T(8,128)(2,1)} %bitcast.21, bf16[384,1536]{1,0:T(8,128)(2,1)} %bitcast.23, bf16[384,1536]{1,0:T(8,128)(2,1)} %bitcast.25, ...), custom_call_target="tpu_custom_call" | custom-call | flops 786432 | bytes 3932160 | tf_op jit(solution)/shard_map/prep/pallas_call | solution.py:122
  12.4 0.5 collective-permute-start.6
  12.9 1.5 %collective-permute-start = (bf16[784,384]{1,0:T(8,128)(2,1)}, bf16[784,384]{1,0:T(8,128)(2,1)}, u32[]{:S(2)}, u32[]{:S(2)}) collective-permute-start(bf16[784,384]{1,0:T(8,128)(2,1)} %get-tuple-element.78.refs_0_.refs_1_), channel_id=1, source_target_pairs={{0,1},{1,0},{2,3},{3,2},{4,5},{5,4},{6,7},{7,6},{8,9},{9,8},{10,11... | collective-permute-start | bytes 1806344 | tf_op jit(solution)/shard_map/ppermute | solution.py:478
  14.4 0.0 collective-permute-done.2.refs_2_.refs_4_.refs_3_
  14.4 5.6 %pairs.10 = (f32[384,512]{1,0:T(8,128)S(1)}, f32[2,384,512]{2,1,0:T(8,128)S(1)}, f32[2,384,512]{2,1,0:T(8,128)S(1)}) custom-call(s32[1]{0:T(128)} %bitcast.far_ref, bf16[784,512]{1,0:T(8,128)(2,1)S(1)} %prep.2.refs_0_.refs_1_, bf16[2,384,1536]{2,1,0:T(8,128)(2,1)S(1)} %pack.1.refs_1_.refs_3_.refs_2_, ...), custom_call_target="tpu_custom_call" | custom-call | flops 9059696640 | bytes 3932160 | tf_op jit(solution)/shard_map/pairs/pallas_call | solution.py:300
  20.0 6.5 %pairs.11 = (f32[384,640]{1,0:T(8,128)S(1)}, f32[2,384,640]{2,1,0:T(8,128)S(1)}, f32[2,384,640]{2,1,0:T(8,128)S(1)}) custom-call(s32[1]{0:T(128)} %bitcast.far_ref, bf16[784,640]{1,0:T(8,128)(2,1)} %get-tuple-element.80.refs_0_, bf16[2,384,1536]{2,1,0:T(8,128)(2,1)S(1)} %pack.1.refs_1_.refs_3_.refs_2_, ...), custom_call_target="tpu_custom_call" | custom-call | flops 11324620800 | bytes 4915200 | tf_op jit(solution)/shard_map/pairs/pallas_call | solution.py:300
  26.5 0.0 collective-permute-done.1.refs_0_.refs_2_
  26.6 1.6 %collective-permute-start.3 = (bf16[784,512]{1,0:T(8,128)(2,1)}, bf16[784,512]{1,0:T(8,128)(2,1)S(1)}, u32[]{:S(2)}, u32[]{:S(2)}) collective-permute-start(bf16[784,512]{1,0:T(8,128)(2,1)} %collective-permute-done.1.refs_0_.refs_2_), channel_id=1, source_target_pairs={{0,2},{2,4},{4,6},{6,0},{1,7},{3,1},{5,3},{7,5},{8,10},{10,12},{12... | collective-permute-start | bytes 2408456 | tf_op jit(solution)/shard_map/ppermute | solution.py:460
  28.2 5.8 %pairs.12 = (f32[384,512]{1,0:T(8,128)S(1)}, f32[2,384,512]{2,1,0:T(8,128)S(1)}, f32[2,384,512]{2,1,0:T(8,128)S(1)}) custom-call(s32[1]{0:T(128)} %bitcast.far_ref, bf16[784,512]{1,0:T(8,128)(2,1)} %collective-permute-done.1.refs_0_.refs_2_, bf16[2,384,1536]{2,1,0:T(8,128)(2,1)S(1)} %pack.1.refs_1_.refs_3_.refs_2_, ...), custom_call_target="tpu_custom_call" | custom-call | flops 9059696640 | bytes 3932160 | tf_op jit(solution)/shard_map/pairs/pallas_call | solution.py:300
  34.0 4.3 %pairs.13 = (f32[384,384]{1,0:T(8,128)S(1)}, f32[2,384,384]{2,1,0:T(8,128)S(1)}, f32[2,384,384]{2,1,0:T(8,128)S(1)}) custom-call(s32[1]{0:T(128)} %bitcast.far_ref, bf16[784,384]{1,0:T(8,128)(2,1)} %get-tuple-element.78.refs_0_.refs_1_, bf16[2,384,1536]{2,1,0:T(8,128)(2,1)S(1)} %pack.1.refs_1_.refs_3_.refs_2_, ...), custom_call_target="tpu_custom_call" | custom-call | flops 27179089920 | bytes 2949120 | tf_op jit(solution)/shard_map/pairs/pallas_call | solution.py:300
  38.3 3.5 %pairs.14 = (f32[384,640]{1,0:T(8,128)S(1)}, f32[2,384,640]{2,1,0:T(8,128)S(1)}) custom-call(s32[1]{0:T(128)} %bitcast.far_ref, bf16[784,640]{1,0:T(8,128)(2,1)} %get-tuple-element.80.refs_0_, bf16[2,384,1536]{2,1,0:T(8,128)(2,1)} %collective-permute-done.4.refs_1_.refs_5_.refs_4_.refs_3_, f32[384,640]{1,0:T(8,128)S(1)} %get-tuple-element.82.refs_2_), custom_call_target="tpu_custom_call" | custom-call | flops 5662310400 | bytes 4915200 | tf_op jit(solution)/shard_map/pairs/pallas_call | solution.py:300
  41.8 5.3 %collective-permute-done.6.refs_0_.refs_1_ = bf16[784,640]{1,0:T(8,128)(2,1)} collective-permute-done((bf16[784,640]{1,0:T(8,128)(2,1)}, bf16[784,640]{1,0:T(8,128)(2,1)}, u32[]{:S(2)}, u32[]{:S(2)}) %collective-permute-start.6) | collective-permute-done | bytes 1003552 | tf_op jit(solution)/shard_map/ppermute | solution.py:478
  47.1 1.6 %collective-permute-start.7 = (bf16[784,640]{1,0:T(8,128)(2,1)}, bf16[784,640]{1,0:T(8,128)(2,1)S(1)}, u32[]{:S(2)}, u32[]{:S(2)}) collective-permute-start(bf16[784,640]{1,0:T(8,128)(2,1)} %collective-permute-done.6.refs_0_.refs_1_), channel_id=1, source_target_pairs={{0,2},{2,4},{4,6},{6,0},{1,7},{3,1},{5,3},{7,5},{8,10},{10,12},{12... | collective-permute-start | bytes 3010568 | tf_op jit(solution)/shard_map/ppermute | solution.py:460
  48.7 0.0 collective-permute-done.3.refs_0_
  48.7 6.9 %pairs.15 = (bf16[384,512]{1,0:T(8,128)(2,1)S(1)}, f32[384,512]{1,0:T(8,128)S(1)}, f32[384,512]{1,0:T(8,128)S(1)}, f32[2,384,512]{2,1,0:T(8,128)S(1)}, bf16[2,38...) custom-call(s32[1]{0:T(128)} %bitcast.far_ref, bf16[784,512]{1,0:T(8,128)(2,1)S(1)} %collective-permute-done.3.refs_0_, ...), custom_call_target="tpu_custom_call" | custom-call | flops 22649241600 | bytes 3932160 | tf_op jit(solution)/shard_map/pairs/pallas_call | solution.py:300
  55.6 2.4 %collective-permute-start.8 = (bf16[384,512]{1,0:T(8,128)(2,1)S(1)}, bf16[384,512]{1,0:T(8,128)(2,1)S(1)}, u32[]{:S(2)}, u32[]{:S(2)}) collective-permute-start(bf16[384,512]{1,0:T(8,128)(2,1)S(1)} %get-tuple-element.103), channel_id=1, source_target_pairs={{2,0},{4,2},{6,4},{1,3},{3,5},{5,7},{10,8},{12,10},{14,12},{9,11},... | collective-permute-start | bytes 1179656 | tf_op jit(solution)/shard_map/ppermute | solution.py:447
  58.0 4.3 %collective-permute-start.10 = (bf16[2,384,512]{2,1,0:T(8,128)(2,1)S(1)}, bf16[2,384,512]{2,1,0:T(8,128)(2,1)S(1)}, u32[]{:S(2)}, u32[]{:S(2)}) collective-permute-start(bf16[2,384,512]{2,1,0:T(8,128)(2,1)S(1)} %get-tuple-element.105), channel_id=1, source_target_pairs={{0,8},{8,0},{16,24},{24,16},{1,9},{9,1},{17,25},{25,17},{2,10},{10... | collective-permute-start | bytes 2359304 | tf_op jit(solution)/shard_map/ppermute | solution.py:447
  62.3 0.0 collective-permute-done.refs_0_
  62.3 3.7 %collective-permute-start.5 = (bf16[784,384]{1,0:T(8,128)(2,1)}, bf16[784,384]{1,0:T(8,128)(2,1)S(1)}, u32[]{:S(2)}, u32[]{:S(2)}) collective-permute-start(bf16[784,384]{1,0:T(8,128)(2,1)} %collective-permute-done.refs_0_), channel_id=1, source_target_pairs={{0,2},{2,4},{4,6},{3,1},{5,3},{7,5},{8,10},{10,12},{12,14},{11,9},... | collective-permute-start | bytes 1806344 | tf_op jit(solution)/shard_map/ppermute | solution.py:460
  66.0 6.7 %pairs.16 = (f32[384,640]{1,0:T(8,128)S(1)}, f32[2,384,640]{2,1,0:T(8,128)S(1)}, f32[2,384,640]{2,1,0:T(8,128)S(1)}) custom-call(s32[1]{0:T(128)} %bitcast.far_ref, bf16[784,640]{1,0:T(8,128)(2,1)} %collective-permute-done.6.refs_0_.refs_1_, bf16[2,384,1536]{2,1,0:T(8,128)(2,1)S(1)} %pack.1.refs_1_.refs_3_.refs_2_, ...), custom_call_target="tpu_custom_call" | custom-call | flops 5662310400 | bytes 4915200 | tf_op jit(solution)/shard_map/pairs/pallas_call | solution.py:300
  72.8 7.8 %pairs.17 = (bf16[384,640]{1,0:T(8,128)(2,1)S(1)}, f32[384,640]{1,0:T(8,128)S(1)}, f32[2,384,640]{2,1,0:T(8,128)S(1)}, bf16[2,384,640]{2,1,0:T(8,128)(2,1)S(1)}, bf16[2,384,1152]{2,1,0:T(8,128)(2,1)S(1)}) custom-call(s32[1]{0:T(128)} %bitcast.far_ref, bf16[784,640]{1,0:T(8,128)(2,1)S(1)} %collective-permute-done.7.refs_0_, ...), custom_call_target="tpu_custom_call", output_to_operand_aliasing={{4}: (10, {})} | custom-call | flops 22649241600 | bytes 4915200 | tf_op jit(solution)/shard_map/pairs/pallas_call | solution.py:300
  80.5 2.5 %collective-permute-start.15 = (bf16[384,640]{1,0:T(8,128)(2,1)S(1)}, bf16[384,640]{1,0:T(8,128)(2,1)S(1)}, u32[]{:S(2)}, u32[]{:S(2)}) collective-permute-start(bf16[384,640]{1,0:T(8,128)(2,1)S(1)} %get-tuple-element.122), channel_id=1, source_target_pairs={{2,0},{4,2},{6,4},{1,3},{3,5},{5,7},{10,8},{12,10},{14,12},{9,11},... | collective-permute-start | bytes 1474568 | tf_op jit(solution)/shard_map/ppermute | solution.py:447
  83.1 0.8 collective-permute-start.14
  83.9 0.1 add_convert_fusion.1
  84.0 4.1 %collective-permute-start.9 = (bf16[384,512]{1,0:T(8,128)(2,1)S(1)}, bf16[384,512]{1,0:T(8,128)(2,1)S(1)}, u32[]{:S(2)}, u32[]{:S(2)}) collective-permute-start(bf16[384,512]{1,0:T(8,128)(2,1)S(1)} %add_convert_fusion.1), channel_id=1, source_target_pairs={{0,1},{1,0},{2,3},{3,2},{4,5},{5,4},{6,7},{7,6},{8,9},{9,8},{10,11... | collective-permute-start | bytes 1179656 | tf_op jit(solution)/shard_map/ppermute | solution.py:464
  88.1 4.7 %pairs.18 = (bf16[384,384]{1,0:T(8,128)(2,1)S(1)}, f32[2,384,384]{2,1,0:T(8,128)S(1)}, f32[2,384,384]{2,1,0:T(8,128)S(1)}, f32[2,384,384]{2,1,0:T(8,128)S(1)}) custom-call(s32[1]{0:T(128)} %bitcast.far_ref, bf16[784,384]{1,0:T(8,128)(2,1)} %collective-permute-done.refs_0_, bf16[2,384,1536]{2,1,0:T(8,128)(2,1)S(1)} %pack.1.refs_1_.refs_3_.refs_2_, ...), custom_call_target="tpu_custom_call" | custom-call | flops 20384317440 | bytes 2949120 | tf_op jit(solution)/shard_map/pairs/pallas_call | solution.py:300
  92.8 0.1 collective-permute-done.15
  92.9 8.9 %collective-permute-start.13 = (bf16[2,384,640]{2,1,0:T(8,128)(2,1)S(1)}, bf16[2,384,640]{2,1,0:T(8,128)(2,1)S(1)}, u32[]{:S(2)}, u32[]{:S(2)}) collective-permute-start(bf16[2,384,640]{2,1,0:T(8,128)(2,1)S(1)} %get-tuple-element.114), channel_id=1, source_target_pairs={{0,8},{8,0},{16,24},{24,16},{1,9},{9,1},{17,25},{25,17},{2,10},{10... | collective-permute-start | bytes 2949128 | tf_op jit(solution)/shard_map/ppermute | solution.py:447
  101.8 0.1 add_convert_fusion
  101.9 0.0 collective-permute-done.5.refs_0_
  101.9 0.4 collective-permute-start.16
  102.3 0.0 collective-permute-done.10.near
  102.3 5.0 %pairs.19 = (bf16[384,384]{1,0:T(8,128)(2,1)S(1)}, f32[384,384]{1,0:T(8,128)S(1)}, f32[2,384,384]{2,1,0:T(8,128)S(1)}, bf16[2,384,384]{2,1,0:T(8,128)(2,1)S(1)}, bf16[2,384,384]{2,1,0:T(8,128)(2,1)S(1)}) custom-call(s32[1]{0:T(128)} %bitcast.far_ref, bf16[784,384]{1,0:T(8,128)(2,1)S(1)} %collective-permute-done.5.refs_0_, ...), custom_call_target="tpu_custom_call" | custom-call | flops 13589544960 | bytes 2949120 | tf_op jit(solution)/shard_map/pairs/pallas_call | solution.py:300
  107.3 2.6 %collective-permute-start.11 = (bf16[2,384,384]{2,1,0:T(8,128)(2,1)S(1)}, bf16[2,384,384]{2,1,0:T(8,128)(2,1)S(1)}, u32[]{:S(2)}, u32[]{:S(2)}) collective-permute-start(bf16[2,384,384]{2,1,0:T(8,128)(2,1)S(1)} %get-tuple-element.111), channel_id=1, source_target_pairs={{0,8},{8,0},{16,24},{24,16},{1,9},{9,1},{17,25},{25,17},{2,10},{10... | collective-permute-start | bytes 1769480 | tf_op jit(solution)/shard_map/ppermute | solution.py:447
  109.9 0.7 collective-permute-start.12
  110.6 4.5 %collective-permute-done.16.rest_0_ = bf16[384,640]{1,0:T(8,128)(2,1)S(1)} collective-permute-done((bf16[384,640]{1,0:T(8,128)(2,1)S(1)}, bf16[384,640]{1,0:T(8,128)(2,1)S(1)}, u32[]{:S(2)}, u32[]{:S(2)}) %collective-permute-start.16) | collective-permute-done | bytes 491552 | tf_op jit(solution)/shard_map/ppermute | solution.py:464
  115.1 0.3 collective-permute-start.17
  115.5 2.1 %collective-permute-start.18 = (bf16[384,384]{1,0:T(8,128)(2,1)S(1)}, bf16[384,384]{1,0:T(8,128)(2,1)S(1)}, u32[]{:S(2)}, u32[]{:S(2)}) collective-permute-start(bf16[384,384]{1,0:T(8,128)(2,1)S(1)} %get-tuple-element.129), channel_id=1, source_target_pairs={{0,0},{7,7},{1,2},{2,1},{3,4},{4,3},{5,6},{6,5},{8,8},{15,15},{9,1... | collective-permute-start | bytes 884744 | tf_op jit(solution)/shard_map/ppermute | solution.py:447
  117.6 1.3 finish.3
  118.9 0.0 collective-permute-done.13.near
  118.9 1.7 %finish.4 = (bf16[384,1536]{1,0:T(8,128)(2,1)}, bf16[384,1536]{1,0:T(8,128)(2,1)}, bf16[384,1536]{1,0:T(8,128)(2,1)}) custom-call(f32[2,384,640]{2,1,0:T(8,128)S(1)} %get-tuple-element.98.own_kv, bf16[2,384,640]{2,1,0:T(8,128)(2,1)S(1)} %collective-permute-done.13.near, ...), custom_call_target="tpu_custom_call", output_to_operand_aliasing={{0}: (5, {}), {1}: (6, {}), {2}: (7, {})} | custom-call | flops 1966080 | bytes 7372800 | tf_op jit(solution)/shard_map/finish/pallas_call | solution.py:349
  120.6 8.9 %collective-permute-done.17.rest_0_ = bf16[384,384]{1,0:T(8,128)(2,1)S(1)} collective-permute-done((bf16[384,384]{1,0:T(8,128)(2,1)S(1)}, bf16[384,384]{1,0:T(8,128)(2,1)S(1)}, u32[]{:S(2)}, u32[]{:S(2)}) %collective-permute-start.17) | collective-permute-done | bytes 294944 | tf_op jit(solution)/shard_map/ppermute | solution.py:447
  129.5 1.0 finish.5
  (12 shorter events, 0.0 us)
Async XLA Ops:
  0.6 1.9 %copy-start = (f32[1,1,12,384]{3,1,2,0:T(1,128)S(1)}, f32[1,1,12,384]{3,1,2,0:T(1,128)}, u32[]{:S(2)}) copy-start(f32[1,1,12,384]{3,1,2,0:T(1,128)} %param.12) | copy-start | bytes 55300
  0.6 1.9 %copy-start.1 = (s32[1,1,9]{2,1,0:T(1,128)S(1)}, s32[1,1,9]{2,1,0:T(1,128)}, u32[]{:S(2)}) copy-start(s32[1,1,9]{2,1,0:T(1,128)} %param.13) | copy-start | bytes 112
  2.4 12.0 %collective-permute-start.2 = (bf16[2,384,1536]{2,1,0:T(8,128)(2,1)S(1)}, bf16[2,384,1536]{2,1,0:T(8,128)(2,1)}, u32[]{:S(2)}, u32[]{:S(2)}) collective-permute-start(bf16[2,384,1536]{2,1,0:T(8,128)(2,1)S(1)} %pack.1.refs_1_.refs_3_.refs_2_), channel_id=1, source_target_pairs={{0,8},{8,0},{16,24},{24,16},{1,9},{9,1},{17,25},{25,17},{2,10},{10... | collective-permute-start | bytes 7077896 | tf_op jit(solution)/shard_map/ppermute | solution.py:400
  4.8 21.8 %collective-permute-start.1 = (bf16[784,512]{1,0:T(8,128)(2,1)S(1)}, bf16[784,512]{1,0:T(8,128)(2,1)}, u32[]{:S(2)}, u32[]{:S(2)}) collective-permute-start(bf16[784,512]{1,0:T(8,128)(2,1)S(1)} %prep.2.refs_0_.refs_1_), channel_id=1, source_target_pairs={{0,1},{1,0},{2,3},{3,2},{4,5},{5,4},{6,7},{7,6},{8,9},{9,8},{10,11... | collective-permute-start | bytes 2408456 | tf_op jit(solution)/shard_map/ppermute | solution.py:405
  6.3 31.9 %collective-permute-start.4 = (bf16[2,384,1536]{2,1,0:T(8,128)(2,1)S(1)}, bf16[2,384,1536]{2,1,0:T(8,128)(2,1)}, u32[]{:S(2)}, u32[]{:S(2)}) collective-permute-start(bf16[2,384,1536]{2,1,0:T(8,128)(2,1)S(1)} %pack.1.refs_1_.refs_3_.refs_2_), channel_id=1, source_target_pairs={{0,0},{24,24},{8,16},{16,8},{1,1},{25,25},{9,17},{17,9},{2,2},{26,... | collective-permute-start | bytes 7077896 | tf_op jit(solution)/shard_map/ppermute | solution.py:406
  12.4 34.7 %collective-permute-start.6 = (bf16[784,640]{1,0:T(8,128)(2,1)}, bf16[784,640]{1,0:T(8,128)(2,1)}, u32[]{:S(2)}, u32[]{:S(2)}) collective-permute-start(bf16[784,640]{1,0:T(8,128)(2,1)} %get-tuple-element.80.refs_0_), channel_id=1, source_target_pairs={{0,1},{1,0},{2,3},{3,2},{4,5},{5,4},{6,7},{7,6},{8,9},{9,8},{10,11... | collective-permute-start | bytes 3010568 | tf_op jit(solution)/shard_map/ppermute | solution.py:478
  12.9 49.4 %collective-permute-start = (bf16[784,384]{1,0:T(8,128)(2,1)}, bf16[784,384]{1,0:T(8,128)(2,1)}, u32[]{:S(2)}, u32[]{:S(2)}) collective-permute-start(bf16[784,384]{1,0:T(8,128)(2,1)} %get-tuple-element.78.refs_0_.refs_1_), channel_id=1, source_target_pairs={{0,1},{1,0},{2,3},{3,2},{4,5},{5,4},{6,7},{7,6},{8,9},{9,8},{10,11... | collective-permute-start | bytes 1806344 | tf_op jit(solution)/shard_map/ppermute | solution.py:478
  26.6 22.2 %collective-permute-start.3 = (bf16[784,512]{1,0:T(8,128)(2,1)}, bf16[784,512]{1,0:T(8,128)(2,1)S(1)}, u32[]{:S(2)}, u32[]{:S(2)}) collective-permute-start(bf16[784,512]{1,0:T(8,128)(2,1)} %collective-permute-done.1.refs_0_.refs_2_), channel_id=1, source_target_pairs={{0,2},{2,4},{4,6},{6,0},{1,7},{3,1},{5,3},{7,5},{8,10},{10,12},{12... | collective-permute-start | bytes 2408456 | tf_op jit(solution)/shard_map/ppermute | solution.py:460
  47.1 25.6 %collective-permute-start.7 = (bf16[784,640]{1,0:T(8,128)(2,1)}, bf16[784,640]{1,0:T(8,128)(2,1)S(1)}, u32[]{:S(2)}, u32[]{:S(2)}) collective-permute-start(bf16[784,640]{1,0:T(8,128)(2,1)} %collective-permute-done.6.refs_0_.refs_1_), channel_id=1, source_target_pairs={{0,2},{2,4},{4,6},{6,0},{1,7},{3,1},{5,3},{7,5},{8,10},{10,12},{12... | collective-permute-start | bytes 3010568 | tf_op jit(solution)/shard_map/ppermute | solution.py:460
  55.6 28.2 %collective-permute-start.8 = (bf16[384,512]{1,0:T(8,128)(2,1)S(1)}, bf16[384,512]{1,0:T(8,128)(2,1)S(1)}, u32[]{:S(2)}, u32[]{:S(2)}) collective-permute-start(bf16[384,512]{1,0:T(8,128)(2,1)S(1)} %get-tuple-element.103), channel_id=1, source_target_pairs={{2,0},{4,2},{6,4},{1,3},{3,5},{5,7},{10,8},{12,10},{14,12},{9,11},... | collective-permute-start | bytes 1179656 | tf_op jit(solution)/shard_map/ppermute | solution.py:447
  58.0 44.3 %collective-permute-start.10 = (bf16[2,384,512]{2,1,0:T(8,128)(2,1)S(1)}, bf16[2,384,512]{2,1,0:T(8,128)(2,1)S(1)}, u32[]{:S(2)}, u32[]{:S(2)}) collective-permute-start(bf16[2,384,512]{2,1,0:T(8,128)(2,1)S(1)} %get-tuple-element.105), channel_id=1, source_target_pairs={{0,8},{8,0},{16,24},{24,16},{1,9},{9,1},{17,25},{25,17},{2,10},{10... | collective-permute-start | bytes 2359304 | tf_op jit(solution)/shard_map/ppermute | solution.py:447
  62.3 39.6 %collective-permute-start.5 = (bf16[784,384]{1,0:T(8,128)(2,1)}, bf16[784,384]{1,0:T(8,128)(2,1)S(1)}, u32[]{:S(2)}, u32[]{:S(2)}) collective-permute-start(bf16[784,384]{1,0:T(8,128)(2,1)} %collective-permute-done.refs_0_), channel_id=1, source_target_pairs={{0,2},{2,4},{4,6},{3,1},{5,3},{7,5},{8,10},{10,12},{12,14},{11,9},... | collective-permute-start | bytes 1806344 | tf_op jit(solution)/shard_map/ppermute | solution.py:460
  80.5 12.4 %collective-permute-start.15 = (bf16[384,640]{1,0:T(8,128)(2,1)S(1)}, bf16[384,640]{1,0:T(8,128)(2,1)S(1)}, u32[]{:S(2)}, u32[]{:S(2)}) collective-permute-start(bf16[384,640]{1,0:T(8,128)(2,1)S(1)} %get-tuple-element.122), channel_id=1, source_target_pairs={{2,0},{4,2},{6,4},{1,3},{3,5},{5,7},{10,8},{12,10},{14,12},{9,11},... | collective-permute-start | bytes 1474568 | tf_op jit(solution)/shard_map/ppermute | solution.py:447
  83.1 32.4 %collective-permute-start.14 = (bf16[2,384,1152]{2,1,0:T(8,128)(2,1)S(1)}, bf16[2,384,1152]{2,1,0:T(8,128)(2,1)S(1)}, u32[]{:S(2)}, u32[]{:S(2)}) collective-permute-start(bf16[2,384,1152]{2,1,0:T(8,128)(2,1)S(1)} %get-tuple-element.115), channel_id=1, source_target_pairs={{0,0},{24,24},{8,16},{16,8},{1,1},{25,25},{9,17},{17,9},{2,2},{26,... | collective-permute-start | bytes 5308424 | tf_op jit(solution)/shard_map/ppermute | solution.py:447
  84.0 18.3 %collective-permute-start.9 = (bf16[384,512]{1,0:T(8,128)(2,1)S(1)}, bf16[384,512]{1,0:T(8,128)(2,1)S(1)}, u32[]{:S(2)}, u32[]{:S(2)}) collective-permute-start(bf16[384,512]{1,0:T(8,128)(2,1)S(1)} %add_convert_fusion.1), channel_id=1, source_target_pairs={{0,1},{1,0},{2,3},{3,2},{4,5},{5,4},{6,7},{7,6},{8,9},{9,8},{10,11... | collective-permute-start | bytes 1179656 | tf_op jit(solution)/shard_map/ppermute | solution.py:464
  92.9 26.0 %collective-permute-start.13 = (bf16[2,384,640]{2,1,0:T(8,128)(2,1)S(1)}, bf16[2,384,640]{2,1,0:T(8,128)(2,1)S(1)}, u32[]{:S(2)}, u32[]{:S(2)}) collective-permute-start(bf16[2,384,640]{2,1,0:T(8,128)(2,1)S(1)} %get-tuple-element.114), channel_id=1, source_target_pairs={{0,8},{8,0},{16,24},{24,16},{1,9},{9,1},{17,25},{25,17},{2,10},{10... | collective-permute-start | bytes 2949128 | tf_op jit(solution)/shard_map/ppermute | solution.py:447
  101.9 13.2 %collective-permute-start.16 = (bf16[384,640]{1,0:T(8,128)(2,1)S(1)}, bf16[384,640]{1,0:T(8,128)(2,1)S(1)}, u32[]{:S(2)}, u32[]{:S(2)}) collective-permute-start(bf16[384,640]{1,0:T(8,128)(2,1)S(1)} %add_convert_fusion), channel_id=1, source_target_pairs={{0,1},{1,0},{2,3},{3,2},{4,5},{5,4},{6,7},{7,6},{8,9},{9,8},{10,11... | collective-permute-start | bytes 1474568 | tf_op jit(solution)/shard_map/ppermute | solution.py:464
  107.3 22.2 %collective-permute-start.11 = (bf16[2,384,384]{2,1,0:T(8,128)(2,1)S(1)}, bf16[2,384,384]{2,1,0:T(8,128)(2,1)S(1)}, u32[]{:S(2)}, u32[]{:S(2)}) collective-permute-start(bf16[2,384,384]{2,1,0:T(8,128)(2,1)S(1)} %get-tuple-element.111), channel_id=1, source_target_pairs={{0,8},{8,0},{16,24},{24,16},{1,9},{9,1},{17,25},{25,17},{2,10},{10... | collective-permute-start | bytes 1769480 | tf_op jit(solution)/shard_map/ppermute | solution.py:447
  109.9 19.6 %collective-permute-start.12 = (bf16[2,384,384]{2,1,0:T(8,128)(2,1)S(1)}, bf16[2,384,384]{2,1,0:T(8,128)(2,1)S(1)}, u32[]{:S(2)}, u32[]{:S(2)}) collective-permute-start(bf16[2,384,384]{2,1,0:T(8,128)(2,1)S(1)} %get-tuple-element.112), channel_id=1, source_target_pairs={{0,0},{24,24},{8,16},{16,8},{1,1},{25,25},{9,17},{17,9},{2,2},{26,... | collective-permute-start | bytes 1769480 | tf_op jit(solution)/shard_map/ppermute | solution.py:447
  115.1 14.4 %collective-permute-start.17 = (bf16[384,384]{1,0:T(8,128)(2,1)S(1)}, bf16[384,384]{1,0:T(8,128)(2,1)S(1)}, u32[]{:S(2)}, u32[]{:S(2)}) collective-permute-start(bf16[384,384]{1,0:T(8,128)(2,1)S(1)} %get-tuple-element.128), channel_id=1, source_target_pairs={{0,1},{1,0},{2,3},{3,2},{4,5},{5,4},{6,7},{7,6},{8,9},{9,8},{10,11... | collective-permute-start | bytes 884744 | tf_op jit(solution)/shard_map/ppermute | solution.py:447
  115.5 14.1 %collective-permute-start.18 = (bf16[384,384]{1,0:T(8,128)(2,1)S(1)}, bf16[384,384]{1,0:T(8,128)(2,1)S(1)}, u32[]{:S(2)}, u32[]{:S(2)}) collective-permute-start(bf16[384,384]{1,0:T(8,128)(2,1)S(1)} %get-tuple-element.129), channel_id=1, source_target_pairs={{0,0},{7,7},{1,2},{2,1},{3,4},{4,3},{5,6},{6,5},{8,8},{15,15},{9,1... | collective-permute-start | bytes 884744 | tf_op jit(solution)/shard_map/ppermute | solution.py:447

commit v7 on v6

--- a/solution.py
+++ b/solution.py
@@ -456,7 +456,7 @@
             backs[earlier][name] = joined
 
     def hand_on(c):
-        chain = onward_open if c == last else onward
+        chain = onward_open if c else onward
         outers[c] = lax.ppermute(after(theirs[c], *done[-1:]), "space", chain)
 
     def send_back(c):

time: 131 us -> 132 us (level)
  the two profiles are of different devices: /device:TPU:16 before, /device:TPU:9 now
where the time goes in v7:
time: 132 us; the launch traced here: 130 us
  Pallas kernels  85.3 us (65%)
  starting transfers between devices  32 us (24%)
  waiting for transfers between devices  11.1 us (8%)
    pallas_call x10, Pallas kernels, run_stage(): pl.pallas_call(functools.partial(stage_kernel, work, names, head_width **...  73.2 us
    ppermute x9, starting transfers between devices, stage(): backs[c][name] = lax.ppermute(sums[c][name], axis, pairs)  15.7 us
    ppermute x3, starting transfers between devices, hand_on(): outers[c] = lax.ppermute(after(theirs[c], *done[-1:]), 'space', chain)  7.87 us
    ppermute x9, waiting for transfers between devices, stage(): backs[c][name] = lax.ppermute(sums[c][name], axis, pairs)  7.2 us
    pallas_call x2, Pallas kernels, prep(): pl.pallas_call(functools.partial(prep_kernel, counts, *sizes), grid_spec=...  6.22 us
    pallas_call x3, Pallas kernels, finish(): pl.pallas_call(functools.partial(finish_kernel, head_width ** (-0.5), len...  4.05 us
    ppermute x1, starting transfers between devices, per_device(): far_kv = lax.ppermute(after(own_kv, mine[0]), 'tm', far_pairs)  3.34 us
  transfers between devices with their start and end apart: 19, of which 3 were waited for; matrix products, arithmetic and copies ran while one was open for 0% of the time, Pallas kernels for 64%

profile of v7, /device:TPU:9, one launch (start us, length us, event | category | flops | bytes accessed | tf_op | source)
XLA Modules:
  0.0 129.6 jit_solution(4241096125933639736)
XLA Ops:
  0.7 1.8 %pack.1.refs_1_.refs_3_.refs_2_ = bf16[2,384,1536]{2,1,0:T(8,128)(2,1)S(1)} custom-call(bf16[384,1536]{1,0:T(8,128)(2,1)} %bitcast.26, bf16[384,1536]{1,0:T(8,128)(2,1)} %bitcast.27), custom_call_target="tpu_custom_call" | custom-call | bytes 4718592 | tf_op jit(solution)/shard_map/pack/pallas_call | solution.py:157
  2.4 0.7 collective-permute-start.2
  3.2 2.2 %prep.2.refs_0_.refs_1_ = bf16[784,512]{1,0:T(8,128)(2,1)S(1)} custom-call(s32[1]{0:T(128)} %bitcast.1.frame_ref, s32[1]{0:T(128)} %bitcast.2.row_ref, s32[9]{0:T(128)S(1)} %bitcast.15, bf16[384,1536]{1,0:T(8,128)(2,1)} %bitcast.20, bf16[384,1536]{1,0:T(8,128)(2,1)} %bitcast.22, bf16[384,1536]{1,0:T(8,128)(2,1)} %bitcast.24, f32[12,1,384]{2,1,0:T(1,128)S(1)} %bitcast.13), custom_call_target="tpu_custom_call" | custom-call | flops 393216 | bytes 1966080 | tf_op jit(solution)/shard_map/prep/pallas_call | solution.py:122
  5.4 1.3 collective-permute-start.1
  6.7 3.3 %collective-permute-start.4 = (bf16[2,384,1536]{2,1,0:T(8,128)(2,1)S(1)}, bf16[2,384,1536]{2,1,0:T(8,128)(2,1)}, u32[]{:S(2)}, u32[]{:S(2)}) collective-permute-start(bf16[2,384,1536]{2,1,0:T(8,128)(2,1)S(1)} %pack.1.refs_1_.refs_3_.refs_2_), channel_id=1, source_target_pairs={{0,0},{24,24},{8,16},{16,8},{1,1},{25,25},{9,17},{17,9},{2,2},{26,... | collective-permute-start | bytes 7077896 | tf_op jit(solution)/shard_map/ppermute | solution.py:406
  10.0 4.0 %prep.3 = (bf16[784,640]{1,0:T(8,128)(2,1)}, bf16[784,384]{1,0:T(8,128)(2,1)}) custom-call(s32[1]{0:T(128)} %bitcast.1.frame_ref, s32[1]{0:T(128)} %bitcast.2.row_ref, s32[9]{0:T(128)S(1)} %bitcast.16, bf16[384,1536]{1,0:T(8,128)(2,1)} %bitcast.21, bf16[384,1536]{1,0:T(8,128)(2,1)} %bitcast.23, bf16[384,1536]{1,0:T(8,128)(2,1)} %bitcast.25, ...), custom_call_target="tpu_custom_call" | custom-call | flops 786432 | bytes 3932160 | tf_op jit(solution)/shard_map/prep/pallas_call | solution.py:122
  14.0 0.3 collective-permute-start.6
  14.3 1.2 collective-permute-start
  15.5 0.0 collective-permute-done.2.refs_2_.refs_4_.refs_3_
  15.5 5.6 %pairs.10 = (f32[384,512]{1,0:T(8,128)S(1)}, f32[2,384,512]{2,1,0:T(8,128)S(1)}, f32[2,384,512]{2,1,0:T(8,128)S(1)}) custom-call(s32[1]{0:T(128)} %bitcast.far_ref, bf16[784,512]{1,0:T(8,128)(2,1)S(1)} %prep.2.refs_0_.refs_1_, bf16[2,384,1536]{2,1,0:T(8,128)(2,1)S(1)} %pack.1.refs_1_.refs_3_.refs_2_, ...), custom_call_target="tpu_custom_call" | custom-call | flops 9059696640 | bytes 3932160 | tf_op jit(solution)/shard_map/pairs/pallas_call | solution.py:300
  21.1 6.5 %pairs.11 = (f32[384,640]{1,0:T(8,128)S(1)}, f32[2,384,640]{2,1,0:T(8,128)S(1)}, f32[2,384,640]{2,1,0:T(8,128)S(1)}) custom-call(s32[1]{0:T(128)} %bitcast.far_ref, bf16[784,640]{1,0:T(8,128)(2,1)} %get-tuple-element.80.refs_0_, bf16[2,384,1536]{2,1,0:T(8,128)(2,1)S(1)} %pack.1.refs_1_.refs_3_.refs_2_, ...), custom_call_target="tpu_custom_call" | custom-call | flops 11324620800 | bytes 4915200 | tf_op jit(solution)/shard_map/pairs/pallas_call | solution.py:300
  27.6 0.0 collective-permute-done.1.refs_0_.refs_2_
  27.6 1.4 %collective-permute-start.3 = (bf16[784,512]{1,0:T(8,128)(2,1)}, bf16[784,512]{1,0:T(8,128)(2,1)S(1)}, u32[]{:S(2)}, u32[]{:S(2)}) collective-permute-start(bf16[784,512]{1,0:T(8,128)(2,1)} %collective-permute-done.1.refs_0_.refs_2_), channel_id=1, source_target_pairs={{0,2},{2,4},{4,6},{6,0},{1,7},{3,1},{5,3},{7,5},{8,10},{10,12},{12... | collective-permute-start | bytes 2408456 | tf_op jit(solution)/shard_map/ppermute | solution.py:460
  29.0 5.8 %pairs.12 = (f32[384,512]{1,0:T(8,128)S(1)}, f32[2,384,512]{2,1,0:T(8,128)S(1)}, f32[2,384,512]{2,1,0:T(8,128)S(1)}) custom-call(s32[1]{0:T(128)} %bitcast.far_ref, bf16[784,512]{1,0:T(8,128)(2,1)} %collective-permute-done.1.refs_0_.refs_2_, bf16[2,384,1536]{2,1,0:T(8,128)(2,1)S(1)} %pack.1.refs_1_.refs_3_.refs_2_, ...), custom_call_target="tpu_custom_call" | custom-call | flops 9059696640 | bytes 3932160 | tf_op jit(solution)/shard_map/pairs/pallas_call | solution.py:300
  34.8 4.3 %pairs.13 = (f32[384,384]{1,0:T(8,128)S(1)}, f32[2,384,384]{2,1,0:T(8,128)S(1)}, f32[2,384,384]{2,1,0:T(8,128)S(1)}) custom-call(s32[1]{0:T(128)} %bitcast.far_ref, bf16[784,384]{1,0:T(8,128)(2,1)} %get-tuple-element.78.refs_0_.refs_1_, bf16[2,384,1536]{2,1,0:T(8,128)(2,1)S(1)} %pack.1.refs_1_.refs_3_.refs_2_, ...), custom_call_target="tpu_custom_call" | custom-call | flops 27179089920 | bytes 2949120 | tf_op jit(solution)/shard_map/pairs/pallas_call | solution.py:300
  39.1 0.0 collective-permute-done.4.refs_1_.refs_5_.refs_4_.refs_3_
  39.1 5.2 %pairs.14 = (f32[384,640]{1,0:T(8,128)S(1)}, f32[2,384,640]{2,1,0:T(8,128)S(1)}) custom-call(s32[1]{0:T(128)} %bitcast.far_ref, bf16[784,640]{1,0:T(8,128)(2,1)} %get-tuple-element.80.refs_0_, bf16[2,384,1536]{2,1,0:T(8,128)(2,1)} %collective-permute-done.4.refs_1_.refs_5_.refs_4_.refs_3_, f32[384,640]{1,0:T(8,128)S(1)} %get-tuple-element.82.refs_2_), custom_call_target="tpu_custom_call" | custom-call | flops 5662310400 | bytes 4915200 | tf_op jit(solution)/shard_map/pairs/pallas_call | solution.py:300
  44.3 2.3 %collective-permute-done.6.refs_0_.refs_1_ = bf16[784,640]{1,0:T(8,128)(2,1)} collective-permute-done((bf16[784,640]{1,0:T(8,128)(2,1)}, bf16[784,640]{1,0:T(8,128)(2,1)}, u32[]{:S(2)}, u32[]{:S(2)}) %collective-permute-start.6) | collective-permute-done | bytes 1003552 | tf_op jit(solution)/shard_map/ppermute | solution.py:478
  46.6 3.2 %collective-permute-start.7 = (bf16[784,640]{1,0:T(8,128)(2,1)}, bf16[784,640]{1,0:T(8,128)(2,1)S(1)}, u32[]{:S(2)}, u32[]{:S(2)}) collective-permute-start(bf16[784,640]{1,0:T(8,128)(2,1)} %collective-permute-done.6.refs_0_.refs_1_), channel_id=1, source_target_pairs={{0,2},{2,4},{4,6},{3,1},{5,3},{7,5},{8,10},{10,12},{12,14},{11,9},... | collective-permute-start | bytes 3010568 | tf_op jit(solution)/shard_map/ppermute | solution.py:460
  49.8 12.5 %pairs.15 = (bf16[384,512]{1,0:T(8,128)(2,1)S(1)}, f32[384,512]{1,0:T(8,128)S(1)}, f32[384,512]{1,0:T(8,128)S(1)}, f32[2,384,512]{2,1,0:T(8,128)S(1)}, bf16[2,38...) custom-call(s32[1]{0:T(128)} %bitcast.far_ref, bf16[784,512]{1,0:T(8,128)(2,1)S(1)} %collective-permute-done.3.refs_0_, ...), custom_call_target="tpu_custom_call" | custom-call | flops 22649241600 | bytes 3932160 | tf_op jit(solution)/shard_map/pairs/pallas_call | solution.py:300
  62.3 2.1 %collective-permute-start.8 = (bf16[384,512]{1,0:T(8,128)(2,1)S(1)}, bf16[384,512]{1,0:T(8,128)(2,1)S(1)}, u32[]{:S(2)}, u32[]{:S(2)}) collective-permute-start(bf16[384,512]{1,0:T(8,128)(2,1)S(1)} %get-tuple-element.103), channel_id=1, source_target_pairs={{2,0},{4,2},{6,4},{1,3},{3,5},{5,7},{10,8},{12,10},{14,12},{9,11},... | collective-permute-start | bytes 1179656 | tf_op jit(solution)/shard_map/ppermute | solution.py:447
  64.4 0.1 collective-permute-start.10
  64.5 0.0 collective-permute-done.refs_0_
  64.5 3.3 %collective-permute-start.5 = (bf16[784,384]{1,0:T(8,128)(2,1)}, bf16[784,384]{1,0:T(8,128)(2,1)S(1)}, u32[]{:S(2)}, u32[]{:S(2)}) collective-permute-start(bf16[784,384]{1,0:T(8,128)(2,1)} %collective-permute-done.refs_0_), channel_id=1, source_target_pairs={{0,2},{2,4},{4,6},{3,1},{5,3},{7,5},{8,10},{10,12},{12,14},{11,9},... | collective-permute-start | bytes 1806344 | tf_op jit(solution)/shard_map/ppermute | solution.py:460
  67.8 6.7 %pairs.16 = (f32[384,640]{1,0:T(8,128)S(1)}, f32[2,384,640]{2,1,0:T(8,128)S(1)}, f32[2,384,640]{2,1,0:T(8,128)S(1)}) custom-call(s32[1]{0:T(128)} %bitcast.far_ref, bf16[784,640]{1,0:T(8,128)(2,1)} %collective-permute-done.6.refs_0_.refs_1_, bf16[2,384,1536]{2,1,0:T(8,128)(2,1)S(1)} %pack.1.refs_1_.refs_3_.refs_2_, ...), custom_call_target="tpu_custom_call" | custom-call | flops 5662310400 | bytes 4915200 | tf_op jit(solution)/shard_map/pairs/pallas_call | solution.py:300
  74.6 12.5 %pairs.17 = (bf16[384,640]{1,0:T(8,128)(2,1)S(1)}, f32[384,640]{1,0:T(8,128)S(1)}, f32[2,384,640]{2,1,0:T(8,128)S(1)}, bf16[2,384,640]{2,1,0:T(8,128)(2,1)S(1)}, bf16[2,384,1152]{2,1,0:T(8,128)(2,1)S(1)}) custom-call(s32[1]{0:T(128)} %bitcast.far_ref, bf16[784,640]{1,0:T(8,128)(2,1)S(1)} %collective-permute-done.7.refs_0_, ...), custom_call_target="tpu_custom_call", output_to_operand_aliasing={{4}: (10, {})} | custom-call | flops 22649241600 | bytes 4915200 | tf_op jit(solution)/shard_map/pairs/pallas_call | solution.py:300
  87.1 2.2 %collective-permute-start.15 = (bf16[384,640]{1,0:T(8,128)(2,1)S(1)}, bf16[384,640]{1,0:T(8,128)(2,1)S(1)}, u32[]{:S(2)}, u32[]{:S(2)}) collective-permute-start(bf16[384,640]{1,0:T(8,128)(2,1)S(1)} %get-tuple-element.122), channel_id=1, source_target_pairs={{2,0},{4,2},{6,4},{1,3},{3,5},{5,7},{10,8},{12,10},{14,12},{9,11},... | collective-permute-start | bytes 1474568 | tf_op jit(solution)/shard_map/ppermute | solution.py:447
  89.2 5.4 %collective-permute-start.14 = (bf16[2,384,1152]{2,1,0:T(8,128)(2,1)S(1)}, bf16[2,384,1152]{2,1,0:T(8,128)(2,1)S(1)}, u32[]{:S(2)}, u32[]{:S(2)}) collective-permute-start(bf16[2,384,1152]{2,1,0:T(8,128)(2,1)S(1)} %get-tuple-element.115), channel_id=1, source_target_pairs={{0,0},{24,24},{8,16},{16,8},{1,1},{25,25},{9,17},{17,9},{2,2},{26,... | collective-permute-start | bytes 5308424 | tf_op jit(solution)/shard_map/ppermute | solution.py:447
  94.7 0.0 collective-permute-done.8
  94.7 0.1 add_convert_fusion.1
  94.8 1.2 collective-permute-start.9
  96.0 6.4 %pairs.18 = (bf16[384,384]{1,0:T(8,128)(2,1)S(1)}, f32[2,384,384]{2,1,0:T(8,128)S(1)}, f32[2,384,384]{2,1,0:T(8,128)S(1)}, f32[2,384,384]{2,1,0:T(8,128)S(1)}) custom-call(s32[1]{0:T(128)} %bitcast.far_ref, bf16[784,384]{1,0:T(8,128)(2,1)} %collective-permute-done.refs_0_, bf16[2,384,1536]{2,1,0:T(8,128)(2,1)S(1)} %pack.1.refs_1_.refs_3_.refs_2_, ...), custom_call_target="tpu_custom_call" | custom-call | flops 20384317440 | bytes 2949120 | tf_op jit(solution)/shard_map/pairs/pallas_call | solution.py:300
  102.4 0.0 collective-permute-done.15
  102.4 0.1 collective-permute-start.13
  102.5 0.1 add_convert_fusion
  102.7 0.0 collective-permute-done.5.refs_0_
  102.7 0.4 collective-permute-start.16
  103.1 0.0 collective-permute-done.10.near
  103.1 7.8 %pairs.19 = (bf16[384,384]{1,0:T(8,128)(2,1)S(1)}, f32[384,384]{1,0:T(8,128)S(1)}, f32[2,384,384]{2,1,0:T(8,128)S(1)}, bf16[2,384,384]{2,1,0:T(8,128)(2,1)S(1)}, bf16[2,384,384]{2,1,0:T(8,128)(2,1)S(1)}) custom-call(s32[1]{0:T(128)} %bitcast.far_ref, bf16[784,384]{1,0:T(8,128)(2,1)S(1)} %collective-permute-done.5.refs_0_, ...), custom_call_target="tpu_custom_call" | custom-call | flops 13589544960 | bytes 2949120 | tf_op jit(solution)/shard_map/pairs/pallas_call | solution.py:300
  110.9 0.1 collective-permute-start.11
  111.0 2.5 %collective-permute-start.12 = (bf16[2,384,384]{2,1,0:T(8,128)(2,1)S(1)}, bf16[2,384,384]{2,1,0:T(8,128)(2,1)S(1)}, u32[]{:S(2)}, u32[]{:S(2)}) collective-permute-start(bf16[2,384,384]{2,1,0:T(8,128)(2,1)S(1)} %get-tuple-element.112), channel_id=1, source_target_pairs={{0,0},{24,24},{8,16},{16,8},{1,1},{25,25},{9,17},{17,9},{2,2},{26,... | collective-permute-start | bytes 1769480 | tf_op jit(solution)/shard_map/ppermute | solution.py:447
  113.5 1.6 %collective-permute-done.16.rest_0_ = bf16[384,640]{1,0:T(8,128)(2,1)S(1)} collective-permute-done((bf16[384,640]{1,0:T(8,128)(2,1)S(1)}, bf16[384,640]{1,0:T(8,128)(2,1)S(1)}, u32[]{:S(2)}, u32[]{:S(2)}) %collective-permute-start.16) | collective-permute-done | bytes 491552 | tf_op jit(solution)/shard_map/ppermute | solution.py:464
  115.0 0.3 collective-permute-start.17
  115.4 2.9 %collective-permute-start.18 = (bf16[384,384]{1,0:T(8,128)(2,1)S(1)}, bf16[384,384]{1,0:T(8,128)(2,1)S(1)}, u32[]{:S(2)}, u32[]{:S(2)}) collective-permute-start(bf16[384,384]{1,0:T(8,128)(2,1)S(1)} %get-tuple-element.129), channel_id=1, source_target_pairs={{0,0},{7,7},{1,2},{2,1},{3,4},{4,3},{5,6},{6,5},{8,8},{15,15},{9,1... | collective-permute-start | bytes 884744 | tf_op jit(solution)/shard_map/ppermute | solution.py:447
  118.3 1.3 finish.3
  119.6 1.7 %finish.4 = (bf16[384,1536]{1,0:T(8,128)(2,1)}, bf16[384,1536]{1,0:T(8,128)(2,1)}, bf16[384,1536]{1,0:T(8,128)(2,1)}) custom-call(f32[2,384,640]{2,1,0:T(8,128)S(1)} %get-tuple-element.98.own_kv, bf16[2,384,640]{2,1,0:T(8,128)(2,1)S(1)} %collective-permute-done.13.near, ...), custom_call_target="tpu_custom_call", output_to_operand_aliasing={{0}: (5, {}), {1}: (6, {}), {2}: (7, {})} | custom-call | flops 1966080 | bytes 7372800 | tf_op jit(solution)/shard_map/finish/pallas_call | solution.py:349
  121.3 7.2 %collective-permute-done.17.rest_0_ = bf16[384,384]{1,0:T(8,128)(2,1)S(1)} collective-permute-done((bf16[384,384]{1,0:T(8,128)(2,1)S(1)}, bf16[384,384]{1,0:T(8,128)(2,1)S(1)}, u32[]{:S(2)}, u32[]{:S(2)}) %collective-permute-start.17) | collective-permute-done | bytes 294944 | tf_op jit(solution)/shard_map/ppermute | solution.py:447
  128.5 1.0 finish.5
  (12 shorter events, 0.0 us)
Async XLA Ops:
  0.6 2.6 %copy-start = (f32[1,1,12,384]{3,1,2,0:T(1,128)S(1)}, f32[1,1,12,384]{3,1,2,0:T(1,128)}, u32[]{:S(2)}) copy-start(f32[1,1,12,384]{3,1,2,0:T(1,128)} %param.12) | copy-start | bytes 55300
  0.6 2.5 %copy-start.1 = (s32[1,1,9]{2,1,0:T(1,128)S(1)}, s32[1,1,9]{2,1,0:T(1,128)}, u32[]{:S(2)}) copy-start(s32[1,1,9]{2,1,0:T(1,128)} %param.13) | copy-start | bytes 112
  2.4 13.1 %collective-permute-start.2 = (bf16[2,384,1536]{2,1,0:T(8,128)(2,1)S(1)}, bf16[2,384,1536]{2,1,0:T(8,128)(2,1)}, u32[]{:S(2)}, u32[]{:S(2)}) collective-permute-start(bf16[2,384,1536]{2,1,0:T(8,128)(2,1)S(1)} %pack.1.refs_1_.refs_3_.refs_2_), channel_id=1, source_target_pairs={{0,8},{8,0},{16,24},{24,16},{1,9},{9,1},{17,25},{25,17},{2,10},{10... | collective-permute-start | bytes 7077896 | tf_op jit(solution)/shard_map/ppermute | solution.py:400
  5.4 22.2 %collective-permute-start.1 = (bf16[784,512]{1,0:T(8,128)(2,1)S(1)}, bf16[784,512]{1,0:T(8,128)(2,1)}, u32[]{:S(2)}, u32[]{:S(2)}) collective-permute-start(bf16[784,512]{1,0:T(8,128)(2,1)S(1)} %prep.2.refs_0_.refs_1_), channel_id=1, source_target_pairs={{0,1},{1,0},{2,3},{3,2},{4,5},{5,4},{6,7},{7,6},{8,9},{9,8},{10,11... | collective-permute-start | bytes 2408456 | tf_op jit(solution)/shard_map/ppermute | solution.py:405
  6.7 32.4 %collective-permute-start.4 = (bf16[2,384,1536]{2,1,0:T(8,128)(2,1)S(1)}, bf16[2,384,1536]{2,1,0:T(8,128)(2,1)}, u32[]{:S(2)}, u32[]{:S(2)}) collective-permute-start(bf16[2,384,1536]{2,1,0:T(8,128)(2,1)S(1)} %pack.1.refs_1_.refs_3_.refs_2_), channel_id=1, source_target_pairs={{0,0},{24,24},{8,16},{16,8},{1,1},{25,25},{9,17},{17,9},{2,2},{26,... | collective-permute-start | bytes 7077896 | tf_op jit(solution)/shard_map/ppermute | solution.py:406
  14.0 32.5 %collective-permute-start.6 = (bf16[784,640]{1,0:T(8,128)(2,1)}, bf16[784,640]{1,0:T(8,128)(2,1)}, u32[]{:S(2)}, u32[]{:S(2)}) collective-permute-start(bf16[784,640]{1,0:T(8,128)(2,1)} %get-tuple-element.80.refs_0_), channel_id=1, source_target_pairs={{0,1},{1,0},{2,3},{3,2},{4,5},{5,4},{6,7},{7,6},{8,9},{9,8},{10,11... | collective-permute-start | bytes 3010568 | tf_op jit(solution)/shard_map/ppermute | solution.py:478
  14.3 50.2 %collective-permute-start = (bf16[784,384]{1,0:T(8,128)(2,1)}, bf16[784,384]{1,0:T(8,128)(2,1)}, u32[]{:S(2)}, u32[]{:S(2)}) collective-permute-start(bf16[784,384]{1,0:T(8,128)(2,1)} %get-tuple-element.78.refs_0_.refs_1_), channel_id=1, source_target_pairs={{0,1},{1,0},{2,3},{3,2},{4,5},{5,4},{6,7},{7,6},{8,9},{9,8},{10,11... | collective-permute-start | bytes 1806344 | tf_op jit(solution)/shard_map/ppermute | solution.py:478
  27.6 22.1 %collective-permute-start.3 = (bf16[784,512]{1,0:T(8,128)(2,1)}, bf16[784,512]{1,0:T(8,128)(2,1)S(1)}, u32[]{:S(2)}, u32[]{:S(2)}) collective-permute-start(bf16[784,512]{1,0:T(8,128)(2,1)} %collective-permute-done.1.refs_0_.refs_2_), channel_id=1, source_target_pairs={{0,2},{2,4},{4,6},{6,0},{1,7},{3,1},{5,3},{7,5},{8,10},{10,12},{12... | collective-permute-start | bytes 2408456 | tf_op jit(solution)/shard_map/ppermute | solution.py:460
  46.6 28.0 %collective-permute-start.7 = (bf16[784,640]{1,0:T(8,128)(2,1)}, bf16[784,640]{1,0:T(8,128)(2,1)S(1)}, u32[]{:S(2)}, u32[]{:S(2)}) collective-permute-start(bf16[784,640]{1,0:T(8,128)(2,1)} %collective-permute-done.6.refs_0_.refs_1_), channel_id=1, source_target_pairs={{0,2},{2,4},{4,6},{3,1},{5,3},{7,5},{8,10},{10,12},{12,14},{11,9},... | collective-permute-start | bytes 3010568 | tf_op jit(solution)/shard_map/ppermute | solution.py:460
  62.3 32.4 %collective-permute-start.8 = (bf16[384,512]{1,0:T(8,128)(2,1)S(1)}, bf16[384,512]{1,0:T(8,128)(2,1)S(1)}, u32[]{:S(2)}, u32[]{:S(2)}) collective-permute-start(bf16[384,512]{1,0:T(8,128)(2,1)S(1)} %get-tuple-element.103), channel_id=1, source_target_pairs={{2,0},{4,2},{6,4},{1,3},{3,5},{5,7},{10,8},{12,10},{14,12},{9,11},... | collective-permute-start | bytes 1179656 | tf_op jit(solution)/shard_map/ppermute | solution.py:447
  64.4 38.7 %collective-permute-start.10 = (bf16[2,384,512]{2,1,0:T(8,128)(2,1)S(1)}, bf16[2,384,512]{2,1,0:T(8,128)(2,1)S(1)}, u32[]{:S(2)}, u32[]{:S(2)}) collective-permute-start(bf16[2,384,512]{2,1,0:T(8,128)(2,1)S(1)} %get-tuple-element.105), channel_id=1, source_target_pairs={{0,8},{8,0},{16,24},{24,16},{1,9},{9,1},{17,25},{25,17},{2,10},{10... | collective-permute-start | bytes 2359304 | tf_op jit(solution)/shard_map/ppermute | solution.py:447
  64.5 38.1 %collective-permute-start.5 = (bf16[784,384]{1,0:T(8,128)(2,1)}, bf16[784,384]{1,0:T(8,128)(2,1)S(1)}, u32[]{:S(2)}, u32[]{:S(2)}) collective-permute-start(bf16[784,384]{1,0:T(8,128)(2,1)} %collective-permute-done.refs_0_), channel_id=1, source_target_pairs={{0,2},{2,4},{4,6},{3,1},{5,3},{7,5},{8,10},{10,12},{12,14},{11,9},... | collective-permute-start | bytes 1806344 | tf_op jit(solution)/shard_map/ppermute | solution.py:460
  87.1 15.4 %collective-permute-start.15 = (bf16[384,640]{1,0:T(8,128)(2,1)S(1)}, bf16[384,640]{1,0:T(8,128)(2,1)S(1)}, u32[]{:S(2)}, u32[]{:S(2)}) collective-permute-start(bf16[384,640]{1,0:T(8,128)(2,1)S(1)} %get-tuple-element.122), channel_id=1, source_target_pairs={{2,0},{4,2},{6,4},{1,3},{3,5},{5,7},{10,8},{12,10},{14,12},{9,11},... | collective-permute-start | bytes 1474568 | tf_op jit(solution)/shard_map/ppermute | solution.py:447
  89.2 26.1 %collective-permute-start.14 = (bf16[2,384,1152]{2,1,0:T(8,128)(2,1)S(1)}, bf16[2,384,1152]{2,1,0:T(8,128)(2,1)S(1)}, u32[]{:S(2)}, u32[]{:S(2)}) collective-permute-start(bf16[2,384,1152]{2,1,0:T(8,128)(2,1)S(1)} %get-tuple-element.115), channel_id=1, source_target_pairs={{0,0},{24,24},{8,16},{16,8},{1,1},{25,25},{9,17},{17,9},{2,2},{26,... | collective-permute-start | bytes 5308424 | tf_op jit(solution)/shard_map/ppermute | solution.py:447
  94.8 8.3 %collective-permute-start.9 = (bf16[384,512]{1,0:T(8,128)(2,1)S(1)}, bf16[384,512]{1,0:T(8,128)(2,1)S(1)}, u32[]{:S(2)}, u32[]{:S(2)}) collective-permute-start(bf16[384,512]{1,0:T(8,128)(2,1)S(1)} %add_convert_fusion.1), channel_id=1, source_target_pairs={{0,1},{1,0},{2,3},{3,2},{4,5},{5,4},{6,7},{7,6},{8,9},{9,8},{10,11... | collective-permute-start | bytes 1179656 | tf_op jit(solution)/shard_map/ppermute | solution.py:464
  102.4 17.2 %collective-permute-start.13 = (bf16[2,384,640]{2,1,0:T(8,128)(2,1)S(1)}, bf16[2,384,640]{2,1,0:T(8,128)(2,1)S(1)}, u32[]{:S(2)}, u32[]{:S(2)}) collective-permute-start(bf16[2,384,640]{2,1,0:T(8,128)(2,1)S(1)} %get-tuple-element.114), channel_id=1, source_target_pairs={{0,8},{8,0},{16,24},{24,16},{1,9},{9,1},{17,25},{25,17},{2,10},{10... | collective-permute-start | bytes 2949128 | tf_op jit(solution)/shard_map/ppermute | solution.py:447
  102.7 12.4 %collective-permute-start.16 = (bf16[384,640]{1,0:T(8,128)(2,1)S(1)}, bf16[384,640]{1,0:T(8,128)(2,1)S(1)}, u32[]{:S(2)}, u32[]{:S(2)}) collective-permute-start(bf16[384,640]{1,0:T(8,128)(2,1)S(1)} %add_convert_fusion), channel_id=1, source_target_pairs={{0,1},{1,0},{2,3},{3,2},{4,5},{5,4},{6,7},{7,6},{8,9},{9,8},{10,11... | collective-permute-start | bytes 1474568 | tf_op jit(solution)/shard_map/ppermute | solution.py:464
  110.9 17.6 %collective-permute-start.11 = (bf16[2,384,384]{2,1,0:T(8,128)(2,1)S(1)}, bf16[2,384,384]{2,1,0:T(8,128)(2,1)S(1)}, u32[]{:S(2)}, u32[]{:S(2)}) collective-permute-start(bf16[2,384,384]{2,1,0:T(8,128)(2,1)S(1)} %get-tuple-element.111), channel_id=1, source_target_pairs={{0,8},{8,0},{16,24},{24,16},{1,9},{9,1},{17,25},{25,17},{2,10},{10... | collective-permute-start | bytes 1769480 | tf_op jit(solution)/shard_map/ppermute | solution.py:447
  111.0 17.5 %collective-permute-start.12 = (bf16[2,384,384]{2,1,0:T(8,128)(2,1)S(1)}, bf16[2,384,384]{2,1,0:T(8,128)(2,1)S(1)}, u32[]{:S(2)}, u32[]{:S(2)}) collective-permute-start(bf16[2,384,384]{2,1,0:T(8,128)(2,1)S(1)} %get-tuple-element.112), channel_id=1, source_target_pairs={{0,0},{24,24},{8,16},{16,8},{1,1},{25,25},{9,17},{17,9},{2,2},{26,... | collective-permute-start | bytes 1769480 | tf_op jit(solution)/shard_map/ppermute | solution.py:447
  115.0 13.5 %collective-permute-start.17 = (bf16[384,384]{1,0:T(8,128)(2,1)S(1)}, bf16[384,384]{1,0:T(8,128)(2,1)S(1)}, u32[]{:S(2)}, u32[]{:S(2)}) collective-permute-start(bf16[384,384]{1,0:T(8,128)(2,1)S(1)} %get-tuple-element.128), channel_id=1, source_target_pairs={{0,1},{1,0},{2,3},{3,2},{4,5},{5,4},{6,7},{7,6},{8,9},{9,8},{10,11... | collective-permute-start | bytes 884744 | tf_op jit(solution)/shard_map/ppermute | solution.py:447
  115.4 13.1 %collective-permute-start.18 = (bf16[384,384]{1,0:T(8,128)(2,1)S(1)}, bf16[384,384]{1,0:T(8,128)(2,1)S(1)}, u32[]{:S(2)}, u32[]{:S(2)}) collective-permute-start(bf16[384,384]{1,0:T(8,128)(2,1)S(1)} %get-tuple-element.129), channel_id=1, source_target_pairs={{0,0},{7,7},{1,2},{2,1},{3,4},{4,3},{5,6},{6,5},{8,8},{15,15},{9,1... | collective-permute-start | bytes 884744 | tf_op jit(solution)/shard_map/ppermute | solution.py:447
